TPU v7x, 32 devices: a whole 2x2x4 slice. The times are simulated.
32 devices in a mesh: rows: 8 (over y, x, core), ffn: 4 (over z).
Axes of the slice: x: 2, y: 2, z: 4, core: 2. Of those that a mesh axis runs over, the one named last changes fastest.
Arguments:
- source: bfloat16 [16, 1024, 512], P('rows', 'ffn'), may hold values from -6 to 6
- target: bfloat16 [16, 1024, 512], P('rows', 'ffn'), may hold values from -6 to 6
- cotangent: bfloat16 [16, 1024, 512], P('rows', 'ffn'), may hold values from -6 to 6
- source_lengths: int32 [16], P('rows'), may hold values from 128 to 1024, as said below
- target_lengths: int32 [16], P('rows'), may hold values from 128 to 1024, as said below
- routes: int32 [3, 16, 1024, 2], P(None, 'rows', 'ffn'), may hold values from 0 to 7, all different within a row
- norm_gain: float32 [5, 512], replicated, may hold values from 0.5 to 1.5
- norm_shift: float32 [5, 512], replicated, may hold values from -0.9 to 0.9
- moa_router: bfloat16 [3, 512, 8], replicated, may hold values from -0.1875 to 0.1875
- moa_query: bfloat16 [3, 512, 512], replicated, may hold values from -0.5 to 0.5
- moa_keyval: bfloat16 [3, 512, 128], replicated, may hold values from -0.25 to 0.25
- moa_out: bfloat16 [3, 512, 512], replicated, may hold values from -4 to 4
- ffn_in: bfloat16 [2, 512, 2048], P(None, None, 'ffn'), may hold values from -0.25 to 0.25
- ffn_in_bias: bfloat16 [2, 2048], P(None, 'ffn'), may hold values from -0.8984375 to 0.8984375
- ffn_out: bfloat16 [2, 2048, 512], P(None, 'ffn'), may hold values from -0.125 to 0.125
- ffn_out_bias: bfloat16 [2, 512], replicated, may hold values from -0.8984375 to 0.8984375
Outputs:
- memory: float32 [16, 1024, 512], P('rows', 'ffn')
- decoded: float32 [16, 1024, 512], P('rows', 'ffn')
- source_grad: float32 [16, 1024, 512], P('rows', 'ffn')
- target_grad: float32 [16, 1024, 512], P('rows', 'ffn')
- memory_grad: float32 [16, 1024, 512], P('rows', 'ffn')
- gain_grad: float32 [4, 512], replicated
- shift_grad: float32 [4, 512], replicated
- final_norm_grad: float32 [2, 512], replicated
- router_grad: float32 [3, 512, 8], replicated
- query_grad: float32 [3, 512, 512], replicated
- keyval_grad: float32 [3, 512, 128], replicated
- out_grad: float32 [3, 512, 512], replicated
- ffn_in_grad: float32 [2, 512, 2048], P(None, None, 'ffn')
- ffn_in_bias_grad: float32 [2, 2048], P(None, 'ffn')
- ffn_out_grad: float32 [2, 2048, 512], P(None, 'ffn')
- ffn_out_bias_grad: float32 [2, 512], replicated
- routed_counts: int32 [3, 8], replicated
Inputs may be any that keep to these rules, and one draw needn't show every extreme that they name: `source_lengths`: in each aligned pair of sequences, one has length 1024; some sequence has length 128. `target_lengths`: in each aligned pair of sequences, one has length 1024; some sequence has length 128.
All inputs are finite; a program needn't handle non-finite values.
Results may differ from a plain program's by a relative error of at most 0.039.
The roundings to bfloat16 on the way count: a program that leaves them out, or rounds other values in their place, can miss the bound.
Values may be sent and summed in bfloat16 or wider, within the bound.
No kernel may reach another device: no remote copies, remote signals or barrier semaphores. Data moves between devices by JAX's collectives and lax.ppermute only.
A program may use at most 128 MiB of HBM per device.

v0:
```python
import jax
import jax.numpy as jnp
from jax import lax
from jax.sharding import PartitionSpec as P

EPS = 1e-05
PRECISE = lax.Precision.HIGHEST


def softmax_last(values):
    maximum = jnp.max(values, -1, keepdims=True)
    raised = jnp.exp(values - maximum)
    return raised / jnp.sum(raised, -1, keepdims=True)


def norm_forward(values, gain_row, shift_row):
    center = values - jnp.mean(values, -1, keepdims=True)
    inverse = lax.rsqrt(jnp.mean(center * center, -1, keepdims=True) + EPS)
    normal = center * inverse
    return ((normal * gain_row + shift_row).astype(jnp.bfloat16), (normal, inverse))


def norm_backward(upstream, kept_items, gain_row):
    normal, inverse = kept_items
    scaled = upstream * gain_row
    result = inverse * (
        scaled
        - jnp.mean(scaled, -1, keepdims=True)
        - normal * jnp.mean(scaled * normal, -1, keepdims=True)
    )
    return (result, jnp.sum(upstream * normal, (0, 1)), jnp.sum(upstream, (0, 1)))


def attend_forward(query_in, key_in, route_ids, allowed, weights):
    router, query_proj, keyval, output = weights
    groups, row_count, model_width = query_in.shape
    tokens_here = groups * row_count
    experts = router.shape[1]
    head_dim = keyval.shape[1] // 2
    flat_query = query_in.reshape(tokens_here, model_width)
    flat_key = key_in.reshape(tokens_here, model_width)
    logits = jnp.dot(flat_query, router, preferred_element_type=jnp.float32)
    picked = (
        route_ids.reshape(tokens_here, 2)[:, :, None]
        == jnp.arange(experts, dtype=jnp.int32)[None, None, :]
    )
    gate_vals = softmax_last(jnp.sum(jnp.where(picked, logits[:, None, :], 0.0), -1))
    queries = (
        jnp.dot(flat_query, query_proj, preferred_element_type=jnp.float32)
        .astype(jnp.bfloat16)
        .reshape(tokens_here, experts, head_dim)
    )
    slot_query = jnp.sum(
        jnp.where(picked[:, :, :, None], queries[:, None, :, :], jnp.zeros((), jnp.bfloat16)), 2
    )
    key_value = (
        jnp.dot(flat_key, keyval, preferred_element_type=jnp.float32)
        .astype(jnp.bfloat16)
        .reshape(groups, row_count, 2 * head_dim)
    )
    gathered = lax.all_gather(key_value, "ffn", axis=1, tiled=True)
    query_rows = slot_query.reshape(groups, row_count * 2, head_dim)
    score_scale = float(head_dim) ** (-0.5)
    scores = (
        jnp.einsum(
            "gqd,gmd->gqm",
            query_rows,
            gathered[:, :, :head_dim],
            preferred_element_type=jnp.float32,
        )
        * score_scale
    )
    masked = jnp.where(allowed, scores, -1e30)
    maximum = jnp.max(masked, -1, keepdims=True)
    raised = jnp.exp(masked - maximum)
    totals = jnp.sum(raised, -1, keepdims=True)
    log_total = maximum + jnp.log(totals)
    weights_low = (raised / totals).astype(jnp.bfloat16)
    attended = jnp.einsum(
        "gqm,gmd->gqd", weights_low, gathered[:, :, head_dim:], preferred_element_type=jnp.float32
    ).reshape(tokens_here, 2, head_dim)
    mixed_rows = jnp.sum(
        jnp.where(picked[:, :, :, None], (gate_vals[:, :, None] * attended)[:, :, None, :], 0.0), 1
    )
    mixed_rows = mixed_rows.astype(jnp.bfloat16).reshape(tokens_here, experts * head_dim)
    result = jnp.dot(mixed_rows, output, preferred_element_type=jnp.float32).reshape(
        groups, row_count, model_width
    )
    return (
        result,
        (
            flat_query,
            flat_key,
            picked,
            gate_vals,
            query_rows,
            gathered,
            log_total,
            attended,
            mixed_rows,
        ),
    )


def attend_backward(upstream, kept_items, allowed, weights):
    router, query_proj, keyval, output = weights
    (
        flat_query,
        flat_key,
        picked,
        gate_vals,
        query_rows,
        gathered,
        log_total,
        attended,
        mixed_rows,
    ) = kept_items
    groups, row_count, model_width = upstream.shape
    tokens_here = groups * row_count
    experts = router.shape[1]
    head_dim = keyval.shape[1] // 2
    branch_grad = upstream.reshape(tokens_here, model_width).astype(jnp.bfloat16)
    output_grad = jnp.einsum(
        "ne,nd->ed", mixed_rows, branch_grad, preferred_element_type=jnp.float32
    )
    mixed_grad = jnp.einsum(
        "nd,ed->ne", branch_grad, output, preferred_element_type=jnp.float32
    ).reshape(tokens_here, experts, head_dim)
    slot_grad = jnp.sum(jnp.where(picked[:, :, :, None], mixed_grad[:, None, :, :], 0.0), 2)
    attended_grad = (
        (gate_vals[:, :, None] * slot_grad)
        .astype(jnp.bfloat16)
        .reshape(groups, row_count * 2, head_dim)
    )
    gate_grad = jnp.sum(attended * slot_grad, -1)
    chosen_grad = gate_vals * (gate_grad - jnp.sum(gate_vals * gate_grad, -1, keepdims=True))
    logit_grad = jnp.sum(jnp.where(picked, chosen_grad[:, :, None], 0.0), 1)
    router_grad = jnp.dot(flat_query.astype(jnp.float32).T, logit_grad, precision=PRECISE)
    input_grad = jnp.dot(logit_grad, router.astype(jnp.float32).T, precision=PRECISE)
    key_rows = gathered[:, :, :head_dim]
    value_rows = gathered[:, :, head_dim:]
    score_scale = float(head_dim) ** (-0.5)
    scores = (
        jnp.einsum("gqd,gmd->gqm", query_rows, key_rows, preferred_element_type=jnp.float32)
        * score_scale
    )
    weights_now = jnp.exp(jnp.where(allowed, scores, -1e30) - log_total)
    value_grad = jnp.einsum(
        "gqm,gqd->gmd",
        weights_now.astype(jnp.bfloat16),
        attended_grad,
        preferred_element_type=jnp.float32,
    )
    weight_grad = jnp.einsum(
        "gqd,gmd->gqm", attended_grad, value_rows, preferred_element_type=jnp.float32
    )
    score_grad = (
        weights_now * (weight_grad - jnp.sum(weights_now * weight_grad, -1, keepdims=True))
    ).astype(jnp.bfloat16)
    query_rows_grad = (
        jnp.einsum("gqm,gmd->gqd", score_grad, key_rows, preferred_element_type=jnp.float32)
        * score_scale
    )
    key_grad = (
        jnp.einsum("gqm,gqd->gmd", score_grad, query_rows, preferred_element_type=jnp.float32)
        * score_scale
    )
    joined = jnp.concatenate([key_grad, value_grad], -1)
    keyval_rows = lax.psum_scatter(
        joined.astype(jnp.bfloat16), "ffn", scatter_dimension=1, tiled=True
    ).reshape(tokens_here, 2 * head_dim)
    placed = jnp.where(
        picked[:, :, :, None], query_rows_grad.reshape(tokens_here, 2, 1, head_dim), 0.0
    )
    query_grad_rows = (
        jnp.sum(placed, 1).astype(jnp.bfloat16).reshape(tokens_here, experts * head_dim)
    )
    query_grad = jnp.einsum(
        "nd,ne->de", flat_query, query_grad_rows, preferred_element_type=jnp.float32
    )
    input_grad = input_grad + jnp.einsum(
        "ne,de->nd", query_grad_rows, query_proj, preferred_element_type=jnp.float32
    )
    keyval_grad = jnp.einsum("nd,ne->de", flat_key, keyval_rows, preferred_element_type=jnp.float32)
    source_part = jnp.einsum("ne,de->nd", keyval_rows, keyval, preferred_element_type=jnp.float32)
    shape_out = (groups, row_count, model_width)
    return (
        input_grad.reshape(shape_out),
        source_part.reshape(shape_out),
        (router_grad, query_grad, keyval_grad, output_grad),
    )


def feed_forward(normed, weight_in, bias_in, weight_out):
    groups, row_count, model_width = normed.shape
    gathered = lax.all_gather(normed, "ffn", axis=1, tiled=True)
    flat_rows = gathered.reshape(-1, model_width)
    pre_act = jnp.dot(flat_rows, weight_in, preferred_element_type=jnp.float32) + bias_in.astype(
        jnp.float32
    )
    act_rows = jax.nn.gelu(pre_act).astype(jnp.bfloat16)
    partial_rows = jnp.dot(act_rows, weight_out, preferred_element_type=jnp.float32).reshape(
        gathered.shape
    )
    result = lax.psum_scatter(partial_rows, "ffn", scatter_dimension=1, tiled=True)
    return (result, (flat_rows, pre_act, act_rows, weight_in, weight_out))


def feed_backward(upstream, kept_items):
    flat_rows, pre_act, act_rows, used_in, used_out = kept_items
    groups, row_count, model_width = upstream.shape
    upstream_low = upstream.astype(jnp.bfloat16)
    rows_grad = lax.all_gather(upstream_low, "ffn", axis=1, tiled=True).reshape(-1, model_width)
    act_grad = jnp.einsum("nd,fd->nf", rows_grad, used_out, preferred_element_type=jnp.float32)
    unused, pull_back = jax.vjp(jax.nn.gelu, pre_act)
    pre_grad = pull_back(act_grad)[0].astype(jnp.bfloat16)
    out_weight_grad = jnp.einsum(
        "nf,nd->fd", act_rows, rows_grad, preferred_element_type=jnp.float32
    )
    in_weight_grad = jnp.einsum(
        "nd,nf->df", flat_rows, pre_grad, preferred_element_type=jnp.float32
    )
    in_bias_grad = jnp.sum(pre_grad.astype(jnp.float32), 0)
    flat_grad = jnp.einsum("nf,df->nd", pre_grad, used_in, preferred_element_type=jnp.float32)
    normed_grad = lax.psum_scatter(
        flat_grad.reshape(groups, -1, model_width), "ffn", scatter_dimension=1, tiled=True
    )
    return (normed_grad, (in_weight_grad, in_bias_grad, out_weight_grad))


def body(
    source,
    target,
    cotangent,
    source_lengths,
    target_lengths,
    routes,
    norm_gain,
    norm_shift,
    moa_router,
    moa_query,
    moa_keyval,
    moa_out,
    ffn_in,
    ffn_in_bias,
    ffn_out,
    ffn_out_bias,
):
    groups, row_count, model_width = source.shape
    length = row_count * lax.axis_size("ffn")
    query_pos = lax.axis_index("ffn") * row_count + jnp.arange(row_count, dtype=jnp.int32)
    key_pos = jnp.arange(length, dtype=jnp.int32)
    source_keys = (key_pos[None, :] < source_lengths[:, None])[:, None, :]
    target_keys = (key_pos[None, :] < target_lengths[:, None])[:, None, :] & (
        key_pos[None, None, :] <= jnp.repeat(query_pos, 2)[None, :, None]
    )
    source_rows = query_pos[None, :] < source_lengths[:, None]
    target_rows = query_pos[None, :] < target_lengths[:, None]
    moa_weights = [
        (moa_router[layer_idx], moa_query[layer_idx], moa_keyval[layer_idx], moa_out[layer_idx])
        for layer_idx in range(3)
    ]
    source_f = source.astype(jnp.float32)
    normed, norm_zero = norm_forward(source_f, norm_gain[0], norm_shift[0])
    branch, attend_zero = attend_forward(normed, normed, routes[0], source_keys, moa_weights[0])
    middle = source_f + branch
    normed, norm_one = norm_forward(middle, norm_gain[1], norm_shift[1])
    branch, feed_zero = feed_forward(normed, ffn_in[0], ffn_in_bias[0], ffn_out[0])
    memory = middle + branch + ffn_out_bias[0].astype(jnp.float32)
    memory_low = memory.astype(jnp.bfloat16)
    target_f = target.astype(jnp.float32)
    normed, norm_two = norm_forward(target_f, norm_gain[2], norm_shift[2])
    branch, attend_one = attend_forward(normed, normed, routes[1], target_keys, moa_weights[1])
    first_state = target_f + branch
    normed, norm_three = norm_forward(first_state, norm_gain[3], norm_shift[3])
    branch, attend_two = attend_forward(normed, memory_low, routes[2], source_keys, moa_weights[2])
    second = first_state + branch
    normed, norm_four = norm_forward(second, norm_gain[4], norm_shift[4])
    branch, feed_one = feed_forward(normed, ffn_in[1], ffn_in_bias[1], ffn_out[1])
    decoded = second + branch + ffn_out_bias[1].astype(jnp.float32)
    upstream = cotangent.astype(jnp.float32) * target_rows[:, :, None].astype(jnp.float32)
    out_bias_one = jnp.sum(upstream, (0, 1))
    hidden_grad, feed_grads_one = feed_backward(upstream, feed_one)
    carried, gain_four, shift_four = norm_backward(hidden_grad, norm_four, norm_gain[4])
    second_grad = upstream + carried
    hidden_grad, memory_grad, cross_grads = attend_backward(
        second_grad, attend_two, source_keys, moa_weights[2]
    )
    carried, gain_three, shift_three = norm_backward(hidden_grad, norm_three, norm_gain[3])
    first_grad = second_grad + carried
    hidden_grad, self_part, self_grads = attend_backward(
        first_grad, attend_one, target_keys, moa_weights[1]
    )
    carried, gain_two, shift_two = norm_backward(hidden_grad + self_part, norm_two, norm_gain[2])
    target_grad = first_grad + carried
    out_bias_zero = jnp.sum(memory_grad, (0, 1))
    hidden_grad, feed_grads_zero = feed_backward(memory_grad, feed_zero)
    carried, gain_one, shift_one = norm_backward(hidden_grad, norm_one, norm_gain[1])
    middle_grad = memory_grad + carried
    hidden_grad, encoder_part, encoder_grads = attend_backward(
        middle_grad, attend_zero, source_keys, moa_weights[0]
    )
    carried, gain_zero, shift_zero = norm_backward(
        hidden_grad + encoder_part, norm_zero, norm_gain[0]
    )
    source_grad = middle_grad + carried
    experts = moa_router.shape[2]
    valid_rows = jnp.stack([source_rows, target_rows, target_rows])
    routed_hits = (routes[..., None] == jnp.arange(experts, dtype=jnp.int32)) & valid_rows[
        :, :, :, None, None
    ]
    counted = jnp.sum(jnp.where(routed_hits, 1.0, 0.0), (1, 2, 3))
    layer_grads = (encoder_grads, self_grads, cross_grads)
    shared = lax.psum(
        (
            jnp.stack([gain_zero, gain_one, gain_two, gain_three, gain_four]),
            jnp.stack([shift_zero, shift_one, shift_two, shift_three, shift_four]),
            jnp.stack([grads_of[0] for grads_of in layer_grads]),
            jnp.stack([grads_of[1] for grads_of in layer_grads]),
            jnp.stack([grads_of[2] for grads_of in layer_grads]),
            jnp.stack([grads_of[3] for grads_of in layer_grads]),
            jnp.stack([out_bias_zero, out_bias_one]),
            counted,
        ),
        ("rows", "ffn"),
    )
    sliced = lax.psum(
        (
            jnp.stack([feed_grads_zero[0], feed_grads_one[0]]),
            jnp.stack([feed_grads_zero[1], feed_grads_one[1]]),
            jnp.stack([feed_grads_zero[2], feed_grads_one[2]]),
        ),
        "rows",
    )
    final_norm = jnp.stack([shared[0][4], shared[1][4]])
    return (
        memory,
        decoded,
        source_grad,
        target_grad,
        memory_grad,
        shared[0][:4],
        shared[1][:4],
        final_norm,
        shared[2],
        shared[3],
        shared[4],
        shared[5],
        sliced[0],
        sliced[1],
        sliced[2],
        shared[6],
        shared[7].astype(jnp.int32),
    )


def solution(mesh):
    in_specs = (
        P("rows", "ffn", None),
        P("rows", "ffn", None),
        P("rows", "ffn", None),
        P("rows"),
        P("rows"),
        P(None, "rows", "ffn", None),
        P(),
        P(),
        P(),
        P(),
        P(),
        P(),
        P(None, None, "ffn"),
        P(None, "ffn"),
        P(None, "ffn", None),
        P(),
    )
    out_specs = (
        P("rows", "ffn", None),
        P("rows", "ffn", None),
        P("rows", "ffn", None),
        P("rows", "ffn", None),
        P("rows", "ffn", None),
        P(),
        P(),
        P(),
        P(),
        P(),
        P(),
        P(),
        P(None, None, "ffn"),
        P(None, "ffn"),
        P(None, "ffn", None),
        P(),
        P(),
    )
    return jax.shard_map(body, mesh=mesh, in_specs=in_specs, out_specs=out_specs, check_vma=False)
```

profile of v0, /device:TPU:1, one launch (start us, length us, event | category | flops | bytes accessed | tf_op | source)
XLA Modules:
  0.0 1110.7 jit_solution(862009613183422209)
XLA Ops:
  19.2 15.3 %all_gather.21 = bf16[2,1024,128]{1,2,0:T(8,128)(2,1)S(1)} all-gather(bf16[2,256,128]{1,2,0:T(8,128)(2,1)S(1)} %copy.106), channel_id=1, replica_groups=mesh['rows'=8,'ffn'=4] {'ffn'}, dimensions={1}, use_global_device_ids=true | all-gather | bytes 655360 | tf_op jit(solution)/shard_map/all_gather | solution.py:61
  34.5 1.7 convolution_convert_fusion.2
  46.8 48.6 %all-gather.5.cloned.1.call-done = bf16[2,1024,512]{2,1,0:T(8,128)(2,1)} async-done(((bf16[2,256,512]{2,1,0:T(8,128)(2,1)}), bf16[2,1024,512]{2,1,0:T(8,128)(2,1)}) %all-gather.5.cloned.1.call-update) | async-done | bytes 2097168 | tf_op jit(solution)/shard_map/all_gather | solution.py:196
  95.5 5.8 multiply_convert_fusion.4
  102.6 3.2 fusion.92
  112.0 21.0 %all_gather.23 = bf16[2,1024,128]{1,2,0:T(8,128)(2,1)S(1)} all-gather(bf16[2,256,128]{1,2,0:T(8,128)(2,1)S(1)} %copy.113), channel_id=1, replica_groups=mesh['rows'=8,'ffn'=4] {'ffn'}, dimensions={1}, use_global_device_ids=true | all-gather | bytes 655360 | tf_op jit(solution)/shard_map/all_gather | solution.py:61
  148.5 41.5 %reduce-scatter.8.cloned.1.call-done = f32[2,256,512]{2,1,0:T(8,128)} async-done(((f32[2,1024,512]{2,1,0:T(8,128)}), f32[2,256,512]{2,1,0:T(8,128)}) %reduce-scatter.8.cloned.1.call-update) | async-done | bytes 1048592 | tf_op jit(solution)/shard_map/reduce_scatter | solution.py:205
  190.0 2.5 fusion.180
  194.6 13.5 %all_gather.24 = bf16[2,1024,128]{1,2,0:T(8,128)(2,1)S(1)} all-gather(bf16[2,256,128]{1,2,0:T(8,128)(2,1)S(1)} %copy.120), channel_id=1, replica_groups=mesh['rows'=8,'ffn'=4] {'ffn'}, dimensions={1}, use_global_device_ids=true | all-gather | bytes 655360 | tf_op jit(solution)/shard_map/all_gather | solution.py:61
  217.1 1.8 fusion.190
  220.4 2.0 fusion.73
  222.7 46.1 %all-gather.7.cloned.1.call-done = bf16[2,1024,512]{2,1,0:T(8,128)(2,1)} async-done(((bf16[2,256,512]{2,1,0:T(8,128)(2,1)}), bf16[2,1024,512]{2,1,0:T(8,128)(2,1)}) %all-gather.7.cloned.1.call-update) | async-done | bytes 2097168 | tf_op jit(solution)/shard_map/all_gather | solution.py:196
  268.8 6.5 multiply_convert_fusion.3
  275.3 40.3 %all-gather.9.cloned.1.call-done = bf16[2,1024,512]{2,1,0:T(8,128)(2,1)} async-done(((bf16[2,256,512]{2,1,0:T(8,128)(2,1)}), bf16[2,1024,512]{2,1,0:T(8,128)(2,1)}) %all-gather.9.cloned.1.call-update) | async-done | bytes 2097168 | tf_op jit(solution)/shard_map/all_gather | solution.py:213
  315.6 7.5 convert_reduce_fusion
  324.4 3.3 fusion.76
  334.2 2.5 fusion.181
  336.8 66.7 %reduce-scatter.12.cloned.1.call-done = f32[2,256,512]{2,1,0:T(8,128)} async-done(((f32[2,1024,512]{2,1,0:T(8,128)}), f32[2,256,512]{2,1,0:T(8,128)}) %reduce-scatter.12.cloned.1.call-update) | async-done | bytes 1048592 | tf_op jit(solution)/shard_map/reduce_scatter | solution.py:225
  403.5 1.8 multiply_reduce_fusion.3
  405.3 1.8 fusion.176
  409.2 1.9 copy.126
  411.2 3.4 fusion.44
  414.9 2.1 multiply_reduce_fusion.2
  420.6 4.9 fusion.78
  431.6 1.9 copy.142
  436.6 3.1 convolution_multiply_fusion.4
  439.7 1.9 copy.145
  441.6 1.9 copy.146
  445.6 3.1 fusion.177
  448.7 2.5 fusion.191
  451.4 2.7 multiply_reduce_fusion.4
  454.1 66.1 %reduce-scatter.10.cloned.1.call-done = f32[2,256,512]{2,1,0:T(8,128)} async-done(((f32[2,1024,512]{2,1,0:T(8,128)}), f32[2,256,512]{2,1,0:T(8,128)}) %reduce-scatter.10.cloned.1.call-update) | async-done | bytes 1048592 | tf_op jit(solution)/shard_map/reduce_scatter | solution.py:205
  520.2 4.1 fusion.178
  525.5 3.6 multiply_reduce_fusion
  532.5 36.3 %all-gather.11.cloned.1.call-done = bf16[2,1024,512]{2,1,0:T(8,128)(2,1)} async-done(((bf16[2,256,512]{2,1,0:T(8,128)(2,1)}), bf16[2,1024,512]{2,1,0:T(8,128)(2,1)}) %all-gather.11.cloned.1.call-update) | async-done | bytes 2097168 | tf_op jit(solution)/shard_map/all_gather | solution.py:213
  568.8 7.5 convert_reduce_fusion.1
  577.6 3.3 fusion.74
  588.1 5.0 convolution_bitcast_fusion
  593.1 2.2 convolution_bitcast_fusion.2
  595.4 1.9 copy.148
  600.4 2.4 convolution_multiply_fusion.3
  607.3 2.9 convolution_bitcast_fusion.7
  612.4 3.1 fusion.62
  615.5 3.6 convolution_bitcast_fusion.3
  620.7 2.2 convolution_bitcast_fusion.1
  622.9 46.6 %reduce-scatter.16.cloned.1.call-done = f32[2,256,512]{2,1,0:T(8,128)} async-done(((f32[2,1024,512]{2,1,0:T(8,128)}), f32[2,256,512]{2,1,0:T(8,128)}) %reduce-scatter.16.cloned.1.call-update) | async-done | bytes 1048592 | tf_op jit(solution)/shard_map/reduce_scatter | solution.py:225
  669.6 1.7 multiply_reduce_fusion.5
  671.3 2.6 fusion.179
  675.4 3.2 fusion.47
  688.3 16.1 %reduce-scatter.18.cloned.1.call-done = bf16[2,256,128]{1,2,0:T(8,128)(2,1)} async-done(((bf16[2,1024,128]{1,2,0:T(8,128)(2,1)}), bf16[2,256,128]{1,2,0:T(8,128)(2,1)}) %reduce-scatter.18.cloned.1.call-update) | async-done | bytes 131088 | tf_op jit(solution)/shard_map/reduce_scatter | solution.py:169
  704.4 2.5 fusion.70
  708.3 3.1 pad_maximum_fusion.3
  711.5 1.7 convolution_bitcast_fusion.8
  713.2 1.7 convolution_bitcast_fusion.4
  717.0 2.0 pad_maximum_fusion.1
  719.0 2.0 pad_maximum_fusion
  722.9 2.6 fusion.61
  725.5 14.2 %psum.84 = f32[2,512]{1,0:T(2,128)} all-reduce(f32[2,512]{1,0:T(2,128)S(1)} %pad_maximum_fusion.10), channel_id=1, replica_groups=mesh['rows'=8,'ffn'=4] {'rows'}, use_global_device_ids=true, to_apply=%region_85.86 | all-reduce | flops 1024 | bytes 8192 | tf_op jit(solution)/shard_map/psum | solution.py:327
  739.7 2.6 fusion.69
  742.2 91.1 %all-reduce.7.cloned.1.call-done = (f32[5,512]{1,0:T(8,128)}, f32[5,512]{1,0:T(8,128)}, f32[3,512,8]{1,2,0:T(8,128)}, f32[2,512]{1,0:T(2,128)}, f32[3,8]{1,0:T(4,128)}) async-done(((f32[5,512]{1,0:T(8,128)}, f32[5,512]{1,0:T(8,128)}, f32[3,512,8]{1,2,0:T(8,128)}, f32[2,512]{1,0:T(2,128)}, f32[3,8]{1,0:T(4,128)}), (f32[5,512]{1,0:T(8,128)}, f32[5,512]{1,0:T(8,128)}, f32[3,512,8]{1,2,0:T(8,128)}, ...) | async-done | bytes 73840 | tf_op jit(solution)/shard_map/psum | solution.py:314
  839.2 80.7 %all-reduce.11.cloned.1.call-done = (f32[2,512,512]{2,1,0:T(8,128)}, f32[2,512,512]{2,1,0:T(8,128)}) async-done(((f32[2,512,512]{2,1,0:T(8,128)}, f32[2,512,512]{2,1,0:T(8,128)}), (f32[2,512,512]{2,1,0:T(8,128)}, f32[2,512,512]{2,1,0:T(8,128)})) %all-reduce.11.cloned.1.call-update) | async-done | bytes 4194320 | tf_op jit(solution)/shard_map/psum | solution.py:327
  919.9 172.4 %all-reduce.9.cloned.1.call-done = (f32[3,512,512]{2,1,0:T(8,128)}, f32[3,512,128]{2,1,0:T(8,128)}, f32[3,512,512]{2,1,0:T(8,128)}) async-done(((f32[3,512,512]{2,1,0:T(8,128)}, f32[3,512,128]{2,1,0:T(8,128)}, f32[3,512,512]{2,1,0:T(8,128)}), (f32[3,512,512]{2,1,0:T(8,128)}, f32[3,512,128]{2,1,0:T(8,128)}, f32[3,512,512]{2,1,0:T(8,128)})) %all-reduce.9.cloned.1.call-update) | async-done | bytes 7077904 | tf_op jit(solution)/shard_map/psum | solution.py:314
  1093.9 3.9 copy.208
  1098.6 1.7 copy.210
  (560 shorter events, 135.1 us)
Async XLA Ops:
  7.2 88.3 %all-gather.5.cloned.1.call-start = ((), (), s32[]{:S(2)}) async-start(), calls=%async_computation.7 | async-start | bytes 2621440 | tf_op jit(solution)/shard_map/all_gather | solution.py:196
  8.4 28.2 %copy-start.113 = (f32[2,256]{1,0:T(2,128)}, f32[2,256]{1,0:T(2,128)S(1)}, u32[]{:S(2)}) copy-start(f32[2,256]{1,0:T(2,128)S(1)} %broadcast_multiply_fusion.17) | copy-start | bytes 6148
  9.8 27.6 %copy-start.125 = (f32[2,256]{1,0:T(2,128)}, f32[2,256]{1,0:T(2,128)S(1)}, u32[]{:S(2)}) copy-start(f32[2,256]{1,0:T(2,128)S(1)} %add_rsqrt_fusion.4) | copy-start | bytes 6148
  10.5 26.9 %copy-start.108 = (pred[2,1024]{1,0:T(4,128)(4,1)}, pred[2,1024]{1,0:T(4,128)(4,1)S(1)}, u32[]{:S(2)}) copy-start(pred[2,1024]{1,0:T(4,128)(4,1)S(1)} %iota_compare_fusion.6) | copy-start | bytes 6148
  12.0 33.1 %copy-start.111 = (f32[1,512]{1,0:T(1,128)}, f32[1,512]{1,0:T(1,128)S(1)}, u32[]{:S(2)}) copy-start(f32[1,512]{1,0:T(1,128)S(1)} %get-tuple-element.61) | copy-start | bytes 6148
  12.0 95.0 %copy-start.123 = (f32[1,512]{1,0:T(1,128)}, f32[1,512]{1,0:T(1,128)S(1)}, u32[]{:S(2)}) copy-start(f32[1,512]{1,0:T(1,128)S(1)} %get-tuple-element.60) | copy-start | bytes 6148
  12.0 131.4 %copy-start.105 = (f32[1,512]{1,0:T(1,128)}, f32[1,512]{1,0:T(1,128)S(1)}, u32[]{:S(2)}) copy-start(f32[1,512]{1,0:T(1,128)S(1)} %get-tuple-element.63) | copy-start | bytes 6148
  14.2 95.8 %copy-start.90 = (s32[1,2,256,2]{2,3,1,0:T(2,128)}, s32[1,2,256,2]{2,3,1,0:T(2,128)S(1)}, u32[]{:S(2)}) copy-start(s32[1,2,256,2]{2,3,1,0:T(2,128)S(1)} %get-tuple-element.70) | copy-start | bytes 12292
  14.2 131.0 %copy-start.92 = (s32[1,2,256,2]{2,3,1,0:T(2,128)}, s32[1,2,256,2]{2,3,1,0:T(2,128)S(1)}, u32[]{:S(2)}) copy-start(s32[1,2,256,2]{2,3,1,0:T(2,128)S(1)} %get-tuple-element.69) | copy-start | bytes 12292
  15.6 21.8 %copy-start.7 = (bf16[2,256,512]{2,1,0:T(8,128)(2,1)}, bf16[2,256,512]{2,1,0:T(8,128)(2,1)S(1)}, u32[]{:S(2)}) copy-start(bf16[2,256,512]{2,1,0:T(8,128)(2,1)S(1)} %fusion.65) | copy-start | bytes 1572868
  41.9 53.6 %copy-start.65 = (bf16[2,512,512]{2,1,0:T(8,128)(2,1)S(1)}, bf16[2,512,512]{2,1,0:T(8,128)(2,1)}, u32[]{:S(2)}) copy-start(bf16[2,512,512]{2,1,0:T(8,128)(2,1)} %param.28) | copy-start | bytes 3145732
  44.8 56.4 %copy-start.94 = (f32[2,256]{1,0:T(2,128)}, f32[2,256]{1,0:T(2,128)S(1)}, u32[]{:S(2)}) copy-start(f32[2,256]{1,0:T(2,128)S(1)} %broadcast_multiply_fusion.16) | copy-start | bytes 6148
  45.1 56.1 %copy-start.117 = (f32[2,256]{1,0:T(2,128)}, f32[2,256]{1,0:T(2,128)S(1)}, u32[]{:S(2)}) copy-start(f32[2,256]{1,0:T(2,128)S(1)} %add_rsqrt_fusion.3) | copy-start | bytes 6148
  46.2 143.8 %reduce-scatter.8.cloned.1.call-start = ((), (), s32[]{:S(2)}) async-start(), calls=%async_computation.8 | async-start | bytes 5242880 | tf_op jit(solution)/shard_map/reduce_scatter | solution.py:205
  46.8 54.4 %copy-start.148 = (f32[1,512]{1,0:T(1,128)}, f32[1,512]{1,0:T(1,128)S(1)}, u32[]{:S(2)}) copy-start(f32[1,512]{1,0:T(1,128)S(1)} %get-tuple-element.75) | copy-start | bytes 6148
  105.8 27.2 %copy-start.143 = (s32[2]{0:T(128)S(1)}, s32[2]{0:T(128)}, u32[]{:S(2)}) copy-start(s32[2]{0:T(128)} %param.20) | copy-start | bytes 28
  105.8 163.0 %all-gather.7.cloned.1.call-start = ((), (), s32[]{:S(2)}) async-start(), calls=%async_computation.9 | async-start | bytes 2621440 | tf_op jit(solution)/shard_map/all_gather | solution.py:196
  107.5 27.1 %copy-start.9 = (bf16[2,256,512]{2,1,0:T(8,128)(2,1)}, bf16[2,256,512]{2,1,0:T(8,128)(2,1)S(1)}, u32[]{:S(2)}) copy-start(bf16[2,256,512]{2,1,0:T(8,128)(2,1)S(1)} %fusion.57) | copy-start | bytes 1572868
  107.8 26.8 %copy-start.74 = (f32[512,2]{0,1:T(2,128)}, f32[512,2]{0,1:T(2,128)S(1)}, u32[]{:S(2)}) copy-start(f32[512,2]{0,1:T(2,128)S(1)} %select_reduce_fusion.17) | copy-start | bytes 12292
  107.8 26.8 %copy-start.84 = (f32[512]{0:T(512)}, f32[512]{0:T(512)S(1)}, u32[]{:S(2)}) copy-start(f32[512]{0:T(512)S(1)} %reduce_max.56) | copy-start | bytes 6148
  109.2 25.5 %copy-start.98 = (f32[512]{0:T(512)}, f32[512]{0:T(512)S(1)}, u32[]{:S(2)}) copy-start(f32[512]{0:T(512)S(1)} %fusion.170) | copy-start | bytes 6148
  112.0 22.7 %copy-start.60 = (bf16[512,2,64]{2,1,0:T(2,128)(2,1)}, bf16[512,2,64]{2,1,0:T(2,128)(2,1)S(1)}, u32[]{:S(2)}) copy-start(bf16[512,2,64]{2,1,0:T(2,128)(2,1)S(1)} %copy.112) | copy-start | bytes 393220
  144.0 64.0 %copy-start.18 = (bf16[2,256,512]{2,1,0:T(8,128)(2,1)}, bf16[2,256,512]{2,1,0:T(8,128)(2,1)S(1)}, u32[]{:S(2)}) copy-start(bf16[2,256,512]{2,1,0:T(8,128)(2,1)S(1)} %add_convert_fusion.1) | copy-start | bytes 1572868
  147.2 62.3 %copy-start.46 = (bf16[512,2,64]{2,1,0:T(2,128)(2,1)}, bf16[512,2,64]{2,1,0:T(2,128)(2,1)S(1)}, u32[]{:S(2)}) copy-start(bf16[512,2,64]{2,1,0:T(2,128)(2,1)S(1)} %copy.119) | copy-start | bytes 393220
  217.1 51.7 %copy-start.151 = (f32[1,512]{1,0:T(1,128)S(1)}, f32[1,512]{1,0:T(1,128)}, u32[]{:S(2)}) copy-start(f32[1,512]{1,0:T(1,128)} %get-tuple-element.74) | copy-start | bytes 6148
  220.3 95.3 %all-gather.9.cloned.1.call-start = ((), (), s32[]{:S(2)}) async-start(), calls=%async_computation.11 | async-start | bytes 2621440 | tf_op jit(solution)/shard_map/all_gather | solution.py:213
  222.4 181.0 %reduce-scatter.12.cloned.1.call-start = ((), (), s32[]{:S(2)}) async-start(), calls=%async_computation.12 | async-start | bytes 5242880 | tf_op jit(solution)/shard_map/reduce_scatter | solution.py:225
  315.6 8.9 copy-start.66
  327.7 120.9 %reduce-scatter.14.cloned.1.call-start = ((), (), s32[]{:S(2)}) async-start(), calls=%async_computation.13 | async-start | bytes 655360 | tf_op jit(solution)/shard_map/reduce_scatter | solution.py:169
  420.5 99.6 %reduce-scatter.10.cloned.1.call-start = ((), (), s32[]{:S(2)}) async-start(), calls=%async_computation.10 | async-start | bytes 5242880 | tf_op jit(solution)/shard_map/reduce_scatter | solution.py:205
  425.5 18.1 %copy-start.93 = (s32[1,2,256,2]{2,3,1,0:T(2,128)S(1)}, s32[1,2,256,2]{2,3,1,0:T(2,128)}, u32[]{:S(2)}) copy-start(s32[1,2,256,2]{2,3,1,0:T(2,128)} %copy-done.92) | copy-start | bytes 12292
  425.5 143.3 %all-gather.11.cloned.1.call-start = ((), (), s32[]{:S(2)}) async-start(), calls=%async_computation.14 | async-start | bytes 2621440 | tf_op jit(solution)/shard_map/all_gather | solution.py:213
  425.6 19.1 %copy-start.81 = (bf16[3,512,8]{1,2,0:T(8,128)(2,1)S(1)}, bf16[3,512,8]{1,2,0:T(8,128)(2,1)}, u32[]{:S(2)}) copy-start(bf16[3,512,8]{1,2,0:T(8,128)(2,1)} %param.24) | copy-start | bytes 73732
  430.4 15.2 %copy-start.106 = (f32[1,512]{1,0:T(1,128)S(1)}, f32[1,512]{1,0:T(1,128)}, u32[]{:S(2)}) copy-start(f32[1,512]{1,0:T(1,128)} %copy-done.105) | copy-start | bytes 6148
  441.6 9.8 copy-start.104
  441.6 9.8 copy-start.120
  445.6 74.6 %copy-start.141 = (f32[1,512]{1,0:T(1,128)S(1)}, f32[1,512]{1,0:T(1,128)}, u32[]{:S(2)}) copy-start(f32[1,512]{1,0:T(1,128)} %get-tuple-element.72) | copy-start | bytes 6148
  451.2 161.2 %reduce-scatter.20.cloned.1.call-start = ((), (), s32[]{:S(2)}) async-start(), calls=%async_computation.17 | async-start | bytes 655360 | tf_op jit(solution)/shard_map/reduce_scatter | solution.py:169
  530.1 38.7 %copy-start.149 = (f32[1,512]{1,0:T(1,128)S(1)}, f32[1,512]{1,0:T(1,128)}, u32[]{:S(2)}) copy-start(f32[1,512]{1,0:T(1,128)} %copy-done.148) | copy-start | bytes 6148
  532.4 137.2 %reduce-scatter.16.cloned.1.call-start = ((), (), s32[]{:S(2)}) async-start(), calls=%async_computation.15 | async-start | bytes 5242880 | tf_op jit(solution)/shard_map/reduce_scatter | solution.py:225
  568.8 8.8 copy-start.67
  581.0 123.4 %reduce-scatter.18.cloned.1.call-start = ((), (), s32[]{:S(2)}) async-start(), calls=%async_computation.16 | async-start | bytes 655360 | tf_op jit(solution)/shard_map/reduce_scatter | solution.py:169
  595.4 8.9 copy-start.91
  604.2 8.2 copy-start.15
  604.2 8.2 copy-start.116
  604.2 8.2 copy-start.124
  620.7 48.9 %copy-start.95 = (f32[2,256]{1,0:T(2,128)S(1)}, f32[2,256]{1,0:T(2,128)}, u32[]{:S(2)}) copy-start(f32[2,256]{1,0:T(2,128)} %copy-done.94) | copy-start | bytes 6148
  620.7 48.9 %copy-start.112 = (f32[1,512]{1,0:T(1,128)S(1)}, f32[1,512]{1,0:T(1,128)}, u32[]{:S(2)}) copy-start(f32[1,512]{1,0:T(1,128)} %copy-done.111) | copy-start | bytes 6148
  620.7 48.9 %copy-start.118 = (f32[2,256]{1,0:T(2,128)S(1)}, f32[2,256]{1,0:T(2,128)}, u32[]{:S(2)}) copy-start(f32[2,256]{1,0:T(2,128)} %copy-done.117) | copy-start | bytes 6148
  620.7 50.7 %copy-start.36 = (f32[2,256,512]{2,1,0:T(8,128)S(1)}, f32[2,256,512]{2,1,0:T(8,128)}, u32[]{:S(2)}) copy-start(f32[2,256,512]{2,1,0:T(8,128)} %get-tuple-element.115) | copy-start | bytes 3145732
  622.9 51.0 %copy-start.39 = (bf16[1,512,512]{2,1,0:T(8,128)(2,1)S(1)}, bf16[1,512,512]{2,1,0:T(8,128)(2,1)}, u32[]{:S(2)}) copy-start(bf16[1,512,512]{2,1,0:T(8,128)(2,1)} %get-tuple-element.54) | copy-start | bytes 1572868
  683.1 21.4 %copy-start.17 = (bf16[2,256,512]{2,1,0:T(8,128)(2,1)S(1)}, bf16[2,256,512]{2,1,0:T(8,128)(2,1)}, u32[]{:S(2)}) copy-start(bf16[2,256,512]{2,1,0:T(8,128)(2,1)} %param.16) | copy-start | bytes 1572868
  683.1 21.4 %copy-start.114 = (f32[2,256]{1,0:T(2,128)S(1)}, f32[2,256]{1,0:T(2,128)}, u32[]{:S(2)}) copy-start(f32[2,256]{1,0:T(2,128)} %copy-done.113) | copy-start | bytes 6148
  683.1 21.4 %copy-start.122 = (f32[1,512]{1,0:T(1,128)S(1)}, f32[1,512]{1,0:T(1,128)}, u32[]{:S(2)}) copy-start(f32[1,512]{1,0:T(1,128)} %copy-done.121) | copy-start | bytes 6148
  683.1 21.4 %copy-start.126 = (f32[2,256]{1,0:T(2,128)S(1)}, f32[2,256]{1,0:T(2,128)}, u32[]{:S(2)}) copy-start(f32[2,256]{1,0:T(2,128)} %copy-done.125) | copy-start | bytes 6148
  683.9 149.4 %all-reduce.7.cloned.1.call-start = ((), (), s32[]{:S(2)}) async-start(), calls=%async_computation.18 | async-start | bytes 176128 | tf_op jit(solution)/shard_map/psum | solution.py:314
  685.3 21.6 %copy-start.140 = (f32[512]{0:T(512)S(1)}, f32[512]{0:T(512)}, u32[]{:S(2)}) copy-start(f32[512]{0:T(512)} %get-tuple-element.25) | copy-start | bytes 6148
  685.3 21.6 %copy-start.154 = (f32[512]{0:T(512)S(1)}, f32[512]{0:T(512)}, u32[]{:S(2)}) copy-start(f32[512]{0:T(512)} %get-tuple-element.21) | copy-start | bytes 6148
  685.3 22.2 %copy-start.139 = (f32[512]{0:T(512)S(1)}, f32[512]{0:T(512)}, u32[]{:S(2)}) copy-start(f32[512]{0:T(512)} %get-tuple-element.32) | copy-start | bytes 6148
  685.3 22.2 %copy-start.153 = (f32[512]{0:T(512)S(1)}, f32[512]{0:T(512)}, u32[]{:S(2)}) copy-start(f32[512]{0:T(512)} %get-tuple-element.34) | copy-start | bytes 6148
  686.2 22.0 %copy-start.29 = (bf16[512,8,64]{0,2,1:T(8,128)(2,1)}, bf16[512,8,64]{0,2,1:T(8,128)(2,1)S(1)}, u32[]{:S(2)}) copy-start(bf16[512,8,64]{0,2,1:T(8,128)(2,1)S(1)} %select_reduce_fusion.3) | copy-start | bytes 1572868
  708.2 211.7 %all-reduce.11.cloned.1.call-start = ((), (), s32[]{:S(2)}) async-start(), calls=%async_computation.20 | async-start | bytes 8388608 | tf_op jit(solution)/shard_map/psum | solution.py:327
  711.4 380.9 %all-reduce.9.cloned.1.call-start = ((), (), s32[]{:S(2)}) async-start(), calls=%async_computation.19 | async-start | bytes 14155776 | tf_op jit(solution)/shard_map/psum | solution.py:314
  722.3 17.4 %copy-start.35 = (f32[2,256,512]{2,1,0:T(8,128)S(1)}, f32[2,256,512]{2,1,0:T(8,128)}, u32[]{:S(2)}) copy-start(f32[2,256,512]{2,1,0:T(8,128)} %get-tuple-element.50) | copy-start | bytes 3145732
  (107 other events, 336.9 us)
Sparse Core Ops, SparseCore 0:
  46.3 49.1 all-gather.4
  106.0 83.9 reduce-scatter.7
  220.4 48.3 all-gather.6
  270.9 44.6 all-gather.8
  327.9 75.5 reduce-scatter.11
  420.6 20.1 reduce-scatter.13
  443.2 76.9 reduce-scatter.9
  522.4 46.3 all-gather.10
  571.7 18.7 reduce-scatter.19
  592.7 76.7 reduce-scatter.15
  684.1 20.3 reduce-scatter.17
  711.3 122.0 all-reduce.6
  837.2 82.6 all-reduce.10
  927.6 164.6 all-reduce.8
where the time goes:
time: 1120 us; the launch traced here: 1110 us
  waiting for transfers between devices  753 us (67%)
  matrix products  129 us (12%)
  local copies, waits for them, and re-layouts  80.2 us (7%)
  other arithmetic  67.2 us (6%)
  blocking collectives  64 us (6%)
  between operations  16.5 us (1%)
    psum x2, waiting for transfers between devices, body(): lax.psum((jnp.stack([gain_zero, gain_one, gain_two, gain_three, gain_four...  263 us
    reduce_scatter x2, waiting for transfers between devices, feed_backward(): lax.psum_scatter(flat_grad.reshape(groups, -1, model_width), 'ffn', scatt...  113 us
    reduce_scatter x2, waiting for transfers between devices, feed_forward(): lax.psum_scatter(partial_rows, 'ffn', scatter_dimension=1, tiled=True)  108 us
    all_gather x2, waiting for transfers between devices, feed_forward(): gathered = lax.all_gather(normed, 'ffn', axis=1, tiled=True)  94.8 us
    psum x1, waiting for transfers between devices, body(): lax.psum((jnp.stack([feed_grads_zero[0], feed_grads_one[0]]), jnp.stack([...  80.7 us
    all_gather x2, waiting for transfers between devices, feed_backward(): lax.all_gather(upstream_low, 'ffn', axis=1, tiled=True)  76.6 us
    all_gather x3, blocking collectives, attend_forward(): gathered = lax.all_gather(key_value, 'ffn', axis=1, tiled=True)  49.8 us
    unnamed x321, local copies, waits for them, and re-layouts  29.1 us
  transfers between devices with their start and end apart: 14, of which 12 were waited for; matrix products, arithmetic and copies ran while one was open for 15% of the time, Pallas kernels for 0%

commit v1 on v0

--- a/solution.py
+++ b/solution.py
@@ -58,7 +58,7 @@
         .astype(jnp.bfloat16)
         .reshape(groups, row_count, 2 * head_dim)
     )
-    gathered = lax.all_gather(key_value, "ffn", axis=1, tiled=True)
+    gathered = gather_positions(key_value)
     query_rows = slot_query.reshape(groups, row_count * 2, head_dim)
     score_scale = float(head_dim) ** (-0.5)
     scores = (
@@ -166,9 +166,9 @@
         * score_scale
     )
     joined = jnp.concatenate([key_grad, value_grad], -1)
-    keyval_rows = lax.psum_scatter(
-        joined.astype(jnp.bfloat16), "ffn", scatter_dimension=1, tiled=True
-    ).reshape(tokens_here, 2 * head_dim)
+    keyval_rows = scatter_positions(joined.astype(jnp.bfloat16)).reshape(
+        tokens_here, 2 * head_dim
+    )
     placed = jnp.where(
         picked[:, :, :, None], query_rows_grad.reshape(tokens_here, 2, 1, head_dim), 0.0
     )
@@ -191,41 +191,196 @@
     )
 
 
-def feed_forward(normed, weight_in, bias_in, weight_out):
+def swap(values, axis_name, bit):
+    size = lax.axis_size(axis_name)
+    return lax.ppermute(values, axis_name, [(i, i ^ bit) for i in range(size)])
+
+
+def bits_of(axis_name):
+    size = lax.axis_size(axis_name)
+    return [1 << k for k in range(size.bit_length() - 1)]
+
+
+def relative(values, axis_name):
+    me = lax.axis_index(axis_name)
+    size = values.shape[0]
+    rest = values.shape[1:]
+    for bit in bits_of(axis_name):
+        split = values.reshape((size // (2 * bit), 2, bit) + rest)
+        values = jnp.where((me & bit) != 0, split[:, ::-1], split).reshape((size,) + rest)
+    return values
+
+
+def gather_relative(values, axis_name):
+    size = lax.axis_size(axis_name)
+    return jnp.stack([values] + [swap(values, axis_name, k) for k in range(1, size)])
+
+
+def gather_positions(key_value):
+    groups, row_count, width = key_value.shape
+    blocks = relative(gather_relative(key_value, "ffn"), "ffn")
+    return jnp.swapaxes(blocks, 0, 1).reshape(groups, -1, width)
+
+
+def scatter_positions(partial_rows):
+    groups, length, width = partial_rows.shape
+    size = lax.axis_size("ffn")
+    blocks = jnp.swapaxes(partial_rows.reshape(groups, size, length // size, width), 0, 1)
+    blocks = relative(blocks, "ffn")
+    return scatter_relative(blocks, "ffn").astype(jnp.bfloat16)
+
+
+def scatter_relative(blocks, axis_name):
+    total = blocks[0].astype(jnp.float32)
+    for k in range(1, blocks.shape[0]):
+        total = total + swap(blocks[k].astype(jnp.bfloat16), axis_name, k).astype(jnp.float32)
+    return total
+
+
+def orders():
+    bits = bits_of("rows")
+    return bits[1:], bits[1:][::-1]
+
+
+def rows_gather(values):
+    half = values.shape[0] // 2
+    size = lax.axis_size("rows")
+    parts = []
+    for order, part in zip(orders(), (values[:half], values[half:])):
+        buffer, index = part[None], [0]
+        for bit in order:
+            buffer = jnp.concatenate([buffer, swap(buffer, "rows", bit)])
+            index = index + [i ^ bit for i in index]
+        parts.append((buffer, index))
+    joined = jnp.concatenate(
+        [buffer[jnp.array([index.index(2 * k) for k in range(size // 2)])] if index != [2 * k for k in range(size // 2)] else buffer for buffer, index in parts], 1
+    )
+    both = jnp.stack([joined, swap(joined, "rows", 1)], 1)
+    return both.reshape((size,) + values.shape)
+
+
+def rows_scatter(blocks):
+    size, count = blocks.shape[:2]
+    split = blocks.reshape((size // 2, 2) + blocks.shape[1:])
+    kept = split[:, 0].astype(jnp.float32) + swap(
+        split[:, 1].astype(jnp.bfloat16), "rows", 1
+    ).astype(jnp.float32)
+    half = count // 2
+    results = []
+    for order, part in zip(orders(), (kept[:, :half], kept[:, half:])):
+        index = [2 * k for k in range(size // 2)]
+        for bit in order[::-1]:
+            keep = [n for n, i in enumerate(index) if not i & bit]
+            send = [index.index(index[n] ^ bit) for n in keep]
+            sent = jnp.stack([part[n] for n in send]).astype(jnp.bfloat16)
+            received = swap(sent, "rows", bit)
+            part = jnp.stack([part[n] for n in keep]) + received.astype(jnp.float32)
+            index = [index[n] for n in keep]
+        results.append(part[0])
+    return jnp.concatenate(results)
+
+
+def add_everywhere(values):
+    for axis_name in ("rows", "ffn"):
+        for bit in bits_of(axis_name):
+            values = values + swap(values, axis_name, bit)
+    return values
+
+
+def gather_weights(weight_in, bias_in, weight_out):
+    size = lax.axis_size("rows")
+    hidden, width = weight_out.shape
+    piece = hidden // size
+    me = lax.axis_index("rows")
+    bias_rows = jnp.zeros((size, 16, width), weight_out.dtype)
+    bias_rows = bias_rows.at[:, 0, :piece].set(bias_in.reshape(size, piece))
+    pieces = jnp.concatenate(
+        [
+            weight_in.T.reshape(size, piece, width),
+            weight_out.reshape(size, piece, width),
+            bias_rows,
+        ],
+        1,
+    )
+    mine = lax.dynamic_index_in_dim(pieces, me, 0, keepdims=False)
+    crossed = gather_relative(mine, "ffn")
+    planes = lax.axis_size("ffn")
+    rows_here = mine.shape[0]
+    full = rows_gather(crossed.reshape(planes * rows_here, width))
+    full = full.reshape(size, planes, rows_here, width)
+    first = full[:, :, :piece].reshape(-1, width)
+    second = full[:, :, piece : 2 * piece].reshape(-1, width)
+    bias = full[:, :, 2 * piece, :piece].reshape(-1)
+    return first, second, bias
+
+
+def reduce_feed(first_grad, second_grad, bias_grad):
+    size, planes = lax.axis_size("rows"), lax.axis_size("ffn")
+    width = first_grad.shape[1]
+    piece = first_grad.shape[0] // (size * planes)
+    bias_rows = jnp.zeros((size, planes, 16, width), jnp.float32)
+    bias_rows = bias_rows.at[:, :, 0, :piece].set(bias_grad.reshape(size, planes, piece))
+    pieces = jnp.concatenate(
+        [
+            first_grad.reshape(size, planes, piece, width),
+            second_grad.reshape(size, planes, piece, width),
+            bias_rows,
+        ],
+        2,
+    )
+    rows_here = pieces.shape[2]
+    summed = rows_scatter(pieces.reshape(size, planes * rows_here, width))
+    summed = scatter_relative(summed.reshape(planes, rows_here, width), "ffn")
+    full = relative(rows_gather(summed.astype(jnp.bfloat16)), "rows").astype(jnp.float32)
+    hidden = size * piece
+    return (
+        full[:, :piece].reshape(hidden, width).T,
+        full[:, 2 * piece, :piece].reshape(hidden),
+        full[:, piece : 2 * piece].reshape(hidden, width),
+    )
+
+
+def reduce_attention(query_grad, keyval_grad, output_grad):
+    size, planes = lax.axis_size("rows"), lax.axis_size("ffn")
+    width = query_grad.shape[1]
+    stacked = jnp.concatenate([query_grad, output_grad, keyval_grad.T]).astype(jnp.bfloat16)
+    count = stacked.shape[0] // size
+    lanes = width // planes
+    blocks = relative(stacked.reshape(size, count, width), "rows")
+    summed = rows_scatter(blocks)
+    by_plane = jnp.swapaxes(summed.reshape(count, planes, lanes), 0, 1)
+    own = scatter_relative(relative(by_plane, "ffn"), "ffn").astype(jnp.bfloat16)
+    planes_full = relative(gather_relative(own, "ffn"), "ffn")
+    rows_here = jnp.swapaxes(planes_full, 0, 1).reshape(count, width)
+    full = relative(rows_gather(rows_here), "rows").reshape(-1, width).astype(jnp.float32)
+    model = query_grad.shape[0]
+    return full[:model], full[2 * model :].T, full[model : 2 * model]
+
+
+def feed_forward(normed, weights):
+    first, second, bias = weights
     groups, row_count, model_width = normed.shape
-    gathered = lax.all_gather(normed, "ffn", axis=1, tiled=True)
-    flat_rows = gathered.reshape(-1, model_width)
-    pre_act = jnp.dot(flat_rows, weight_in, preferred_element_type=jnp.float32) + bias_in.astype(
-        jnp.float32
-    )
+    flat_rows = normed.reshape(-1, model_width)
+    pre_act = jnp.einsum("nd,fd->nf", flat_rows, first, preferred_element_type=jnp.float32)
+    pre_act = pre_act + bias.astype(jnp.float32)
     act_rows = jax.nn.gelu(pre_act).astype(jnp.bfloat16)
-    partial_rows = jnp.dot(act_rows, weight_out, preferred_element_type=jnp.float32).reshape(
-        gathered.shape
-    )
-    result = lax.psum_scatter(partial_rows, "ffn", scatter_dimension=1, tiled=True)
-    return (result, (flat_rows, pre_act, act_rows, weight_in, weight_out))
+    result = jnp.dot(act_rows, second, preferred_element_type=jnp.float32).reshape(normed.shape)
+    return (result, (flat_rows, pre_act, act_rows, first, second))
 
 
 def feed_backward(upstream, kept_items):
-    flat_rows, pre_act, act_rows, used_in, used_out = kept_items
+    flat_rows, pre_act, act_rows, first, second = kept_items
     groups, row_count, model_width = upstream.shape
-    upstream_low = upstream.astype(jnp.bfloat16)
-    rows_grad = lax.all_gather(upstream_low, "ffn", axis=1, tiled=True).reshape(-1, model_width)
-    act_grad = jnp.einsum("nd,fd->nf", rows_grad, used_out, preferred_element_type=jnp.float32)
+    rows_grad = upstream.astype(jnp.bfloat16).reshape(-1, model_width)
+    act_grad = jnp.einsum("nd,fd->nf", rows_grad, second, preferred_element_type=jnp.float32)
     unused, pull_back = jax.vjp(jax.nn.gelu, pre_act)
     pre_grad = pull_back(act_grad)[0].astype(jnp.bfloat16)
-    out_weight_grad = jnp.einsum(
-        "nf,nd->fd", act_rows, rows_grad, preferred_element_type=jnp.float32
-    )
-    in_weight_grad = jnp.einsum(
-        "nd,nf->df", flat_rows, pre_grad, preferred_element_type=jnp.float32
-    )
-    in_bias_grad = jnp.sum(pre_grad.astype(jnp.float32), 0)
-    flat_grad = jnp.einsum("nf,df->nd", pre_grad, used_in, preferred_element_type=jnp.float32)
-    normed_grad = lax.psum_scatter(
-        flat_grad.reshape(groups, -1, model_width), "ffn", scatter_dimension=1, tiled=True
-    )
-    return (normed_grad, (in_weight_grad, in_bias_grad, out_weight_grad))
+    second_grad = jnp.einsum("nf,nd->fd", act_rows, rows_grad, preferred_element_type=jnp.float32)
+    first_grad = jnp.einsum("nf,nd->fd", pre_grad, flat_rows, preferred_element_type=jnp.float32)
+    bias_grad = jnp.sum(pre_grad.astype(jnp.float32), 0)
+    normed_grad = jnp.dot(pre_grad, first, preferred_element_type=jnp.float32)
+    reduced = reduce_feed(first_grad, second_grad, bias_grad)
+    return (normed_grad.reshape(upstream.shape), reduced)
 
 
 def body(
@@ -256,6 +411,9 @@
     )
     source_rows = query_pos[None, :] < source_lengths[:, None]
     target_rows = query_pos[None, :] < target_lengths[:, None]
+    feed_weights = [
+        gather_weights(ffn_in[layer], ffn_in_bias[layer], ffn_out[layer]) for layer in range(2)
+    ]
     moa_weights = [
         (moa_router[layer_idx], moa_query[layer_idx], moa_keyval[layer_idx], moa_out[layer_idx])
         for layer_idx in range(3)
@@ -265,7 +423,7 @@
     branch, attend_zero = attend_forward(normed, normed, routes[0], source_keys, moa_weights[0])
     middle = source_f + branch
     normed, norm_one = norm_forward(middle, norm_gain[1], norm_shift[1])
-    branch, feed_zero = feed_forward(normed, ffn_in[0], ffn_in_bias[0], ffn_out[0])
+    branch, feed_zero = feed_forward(normed, feed_weights[0])
     memory = middle + branch + ffn_out_bias[0].astype(jnp.float32)
     memory_low = memory.astype(jnp.bfloat16)
     target_f = target.astype(jnp.float32)
@@ -276,7 +434,7 @@
     branch, attend_two = attend_forward(normed, memory_low, routes[2], source_keys, moa_weights[2])
     second = first_state + branch
     normed, norm_four = norm_forward(second, norm_gain[4], norm_shift[4])
-    branch, feed_one = feed_forward(normed, ffn_in[1], ffn_in_bias[1], ffn_out[1])
+    branch, feed_one = feed_forward(normed, feed_weights[1])
     decoded = second + branch + ffn_out_bias[1].astype(jnp.float32)
     upstream = cotangent.astype(jnp.float32) * target_rows[:, :, None].astype(jnp.float32)
     out_bias_one = jnp.sum(upstream, (0, 1))
@@ -311,46 +469,39 @@
     ]
     counted = jnp.sum(jnp.where(routed_hits, 1.0, 0.0), (1, 2, 3))
     layer_grads = (encoder_grads, self_grads, cross_grads)
-    shared = lax.psum(
-        (
+    small = jnp.concatenate(
+        [
             jnp.stack([gain_zero, gain_one, gain_two, gain_three, gain_four]),
             jnp.stack([shift_zero, shift_one, shift_two, shift_three, shift_four]),
-            jnp.stack([grads_of[0] for grads_of in layer_grads]),
-            jnp.stack([grads_of[1] for grads_of in layer_grads]),
-            jnp.stack([grads_of[2] for grads_of in layer_grads]),
-            jnp.stack([grads_of[3] for grads_of in layer_grads]),
             jnp.stack([out_bias_zero, out_bias_one]),
-            counted,
-        ),
-        ("rows", "ffn"),
-    )
-    sliced = lax.psum(
-        (
-            jnp.stack([feed_grads_zero[0], feed_grads_one[0]]),
-            jnp.stack([feed_grads_zero[1], feed_grads_one[1]]),
-            jnp.stack([feed_grads_zero[2], feed_grads_one[2]]),
-        ),
-        "rows",
-    )
-    final_norm = jnp.stack([shared[0][4], shared[1][4]])
+            jnp.concatenate([grads_of[0].T for grads_of in layer_grads]),
+            jnp.zeros((1, model_width)).at[0, : 3 * experts].set(counted.reshape(-1)),
+        ]
+    )
+    small = add_everywhere(small)
+    reduced = [reduce_attention(*grads_of[1:]) for grads_of in layer_grads]
+    gains, shifts, out_biases = small[:5], small[5:10], small[10:12]
+    routers = jnp.swapaxes(small[12 : 12 + 3 * experts].reshape(3, experts, model_width), 1, 2)
+    counts = small[-1, : 3 * experts].reshape(3, experts)
+    feeds = (feed_grads_zero, feed_grads_one)
     return (
         memory,
         decoded,
         source_grad,
         target_grad,
         memory_grad,
-        shared[0][:4],
-        shared[1][:4],
-        final_norm,
-        shared[2],
-        shared[3],
-        shared[4],
-        shared[5],
-        sliced[0],
-        sliced[1],
-        sliced[2],
-        shared[6],
-        shared[7].astype(jnp.int32),
+        gains[:4],
+        shifts[:4],
+        jnp.stack([gains[4], shifts[4]]),
+        routers,
+        jnp.stack([grads_of[0] for grads_of in reduced]),
+        jnp.stack([grads_of[1] for grads_of in reduced]),
+        jnp.stack([grads_of[2] for grads_of in reduced]),
+        jnp.stack([grads_of[0] for grads_of in feeds]),
+        jnp.stack([grads_of[1] for grads_of in feeds]),
+        jnp.stack([grads_of[2] for grads_of in feeds]),
+        out_biases,
+        counts.astype(jnp.int32),
     )
 
 

time: 1120 us -> 635 us (0.57)
  waiting for transfers between devices: 753 us -> 87.5 us
  starting transfers between devices: 1.58 us -> 136 us
  other arithmetic: 67.2 us -> 146 us
  blocking collectives: 64 us -> 0 us
  local copies, waits for them, and re-layouts: 80.2 us -> 136 us
    psum x3 -> x0, waiting for transfers between devices: 344 us -> none  [the longest x2 263 us: body(): lax.psum((jnp.stack([gain_zero, gain_one, gain_two, gain_three, gain_four...]
    reduce_scatter x7 -> x0, waiting for transfers between devices: 237 us -> none  [the longest x2 113 us: feed_backward(): lax.psum_scatter(flat_grad.reshape(groups, -1, model_width), 'ffn', scatt...]
    all_gather x4 -> x0, waiting for transfers between devices: 171 us -> none  [the longest x2 94.8 us: feed_forward(): gathered = lax.all_gather(normed, 'ffn', axis=1, tiled=True)]
    ppermute x0 -> x113, starting transfers between devices: none -> 136 us  [swap(): return lax.ppermute(values, axis_name, [(i, i ^ bit) for i in range(size)])]
    ppermute x0 -> x113, waiting for transfers between devices: none -> 87.5 us  [swap(): return lax.ppermute(values, axis_name, [(i, i ^ bit) for i in range(size)])]
    all_gather x3 -> x0, blocking collectives: 49.8 us -> none  [attend_forward(): gathered = lax.all_gather(key_value, 'ffn', axis=1, tiled=True)]
    another operation x9 -> x59, other arithmetic: 11.3 us -> 48.1 us  [the longest x14 17.9 us: rows_gather(): both = jnp.stack([joined, swap(joined, 'rows', 1)], 1)]
    convert_element_type x0 -> x16, local copies, waits for them, and re-layouts: none -> 19.2 us  [the longest x2 7.91 us: feed_backward(): pre_grad = pull_back(act_grad)[0].astype(jnp.bfloat16)]
  transfers between devices with their start and end apart: 14 -> 113, of which waited for: 12 -> 32; matrix products, arithmetic and copies ran while one was open for 15% -> 44% of each run, Pallas kernels for 0% -> 0%
where the time goes in v1:
time: 635 us; the launch traced here: 628 us
  other arithmetic  146 us (23%)
  local copies, waits for them, and re-layouts  136 us (21%)
  starting transfers between devices  136 us (21%)
  matrix products  118 us (19%)
  waiting for transfers between devices  87.5 us (14%)
    ppermute x113, starting transfers between devices, swap(): return lax.ppermute(values, axis_name, [(i, i ^ bit) for i in range(size)])  136 us
    ppermute x113, waiting for transfers between devices, swap(): return lax.ppermute(values, axis_name, [(i, i ^ bit) for i in range(size)])  87.5 us
    unnamed x444, local copies, waits for them, and re-layouts  26.4 us
    another operation x14, other arithmetic, rows_gather(): both = jnp.stack([joined, swap(joined, 'rows', 1)], 1)  17.9 us
    concatenate x21, other arithmetic, rows_gather(): buffer = jnp.concatenate([buffer, swap(buffer, 'rows', bit)])  16.8 us
    dot_general x2, matrix products, feed_forward(): jnp.einsum('nd,fd->nf', flat_rows, first, preferred_element_type=jnp.floa...  13.6 us
    convert_element_type x2, other arithmetic, feed_backward(): pre_grad = pull_back(act_grad)[0].astype(jnp.bfloat16)  13.5 us
  transfers between devices with their start and end apart: 113, of which 32 were waited for; matrix products, arithmetic and copies ran while one was open for 44% of the time, Pallas kernels for 0%

profile of v1, /device:TPU:1, one launch (start us, length us, event | category | flops | bytes accessed | tf_op | source)
XLA Modules:
  0.0 628.3 jit_solution(7869447503221854855)
XLA Ops:
  8.6 4.2 collective-permute-start.2
  15.3 3.3 collective-permute-start.13
  34.0 2.5 fusion.260
  59.2 3.3 collective-permute-start.21
  64.3 3.2 collective-permute-start.7
  81.2 2.3 convolution_convert_fusion.6
  117.0 8.5 %collective-permute-done.23 = bf16[2,288,512]{2,1,0:T(8,128)(2,1)} collective-permute-done((bf16[2,288,512]{2,1,0:T(8,128)(2,1)}, bf16[2,288,512]{2,1,0:T(8,128)(2,1)}, u32[]{:S(2)}, u32[]{:S(2)}) %collective-permute-start.23) | collective-permute-done | bytes 589856 | tf_op jit(solution)/shard_map/ppermute | solution.py:196
  125.6 2.3 pad_maximum_fusion.9
  127.8 3.0 gather_fusion.1
  130.8 3.5 fusion.241
  134.4 6.8 %collective-permute-start.24 = (bf16[4,576,512]{2,1,0:T(8,128)(2,1)}, bf16[4,576,512]{2,1,0:T(8,128)(2,1)}, u32[]{:S(2)}, u32[]{:S(2)}) collective-permute-start(bf16[4,576,512]{2,1,0:T(8,128)(2,1)} %get-tuple-element.224), channel_id=1, source_target_pairs={{0,4},{4,0},{8,12},{12,8},{16,20},{20,16},{24,28},{28,24},{1,5},{5... | collective-permute-start | bytes 7077896 | tf_op jit(solution)/shard_map/ppermute | solution.py:196
  141.2 2.4 pad_maximum_fusion.8
  143.6 3.0 gather_fusion
  146.6 4.0 fusion.242
  159.0 2.2 copy-done.16
  163.7 2.3 fusion.255
  166.2 5.9 multiply_convert_fusion.4
  172.1 2.2 fusion.281
  175.7 2.8 collective-permute-start.16
  180.9 3.4 fusion.285
  184.4 5.8 collective-permute-done.15
  203.5 7.7 %convert_reduce_fusion = (f32[2048]{0:T(1024)S(1)}, bf16[512,2048]{1,0:T(8,128)(2,1)S(1)}, bf16[512,2048]{1,0:T(8,128)(2,1)}, f32[512,2048]{1,0:T(8,128)}) fusion(f32[512,2048]{1,0:T(8,128)S(1)} %copy-done.8, f32[2048]{0:T(1024)S(1)} %reshape.1484, bf16[512,512]{1,0:T(8,128)(2,1)S(1)} %bitcast.871, bf16[2048,512]{1,0:T(8,128)(2,1)} %bitcast.908), kind=kOutput, calls=%fused_computation.69 | convolution fusion | flops 1099954176 | bytes 15220736 | tf_op jit(solution)/shard_map/nd,fd->nf/dot_general | solution.py:364
  218.0 4.1 fusion.74
  222.0 4.0 multiply_reduce_fusion.2
  227.9 4.3 multiply_convert_fusion.2
  241.3 2.5 fusion.243
  245.7 4.0 fusion.250
  251.8 3.5 multiply_reduce_fusion
  275.8 2.5 convolution_add_fusion.3
  283.5 6.5 %fusion.31 = (bf16[2048,512]{0,1:T(8,128)(2,1)}, bf16[2048,512]{0,1:T(8,128)(2,1)}) fusion(f32[512,2048]{1,0:T(8,128)} %get-tuple-element.333, f32[512,2048]{1,0:T(8,128)} %fusion.285), kind=kLoop, calls=%fused_computation.54 | loop fusion | flops 23068672 | bytes 12582912 | tf_op jit(solution)/shard_map/convert_element_type | solution.py:377
  290.0 3.9 copy.473
  294.0 4.0 copy.472
  298.0 3.0 fusion.295
  311.0 2.2 fusion.60
  316.2 2.7 collective-permute-start.100
  321.3 5.8 convert_reduce_fusion.1
  333.0 3.5 multiply_reduce_fusion.1
  344.3 2.6 convolution_add_fusion.6
  354.0 3.0 fusion.95
  363.7 7.0 %fusion.24 = (bf16[2048,512]{0,1:T(8,128)(2,1)}, bf16[2048,512]{0,1:T(8,128)(2,1)}) fusion(f32[512,2048]{1,0:T(8,128)} %get-tuple-element.326, f32[512,2048]{1,0:T(8,128)} %get-tuple-element.339), kind=kLoop, calls=%fused_computation.47 | loop fusion | flops 23068672 | bytes 12582912 | tf_op jit(solution)/shard_map/convert_element_type | solution.py:377
  370.7 2.9 copy.468
  373.5 3.9 copy.467
  377.5 2.5 fusion.293
  390.4 2.5 fusion.103
  393.6 2.6 fusion.102
  400.5 2.5 collective-permute-done.36
  403.3 3.0 collective-permute-done.37
  407.7 3.6 collective-permute-done.38
  411.2 5.0 collective-permute-start.39
  440.5 2.2 collective-permute-start.76
  487.1 2.7 collective-permute-done.52
  493.3 2.9 collective-permute-done.50
  496.1 14.2 %collective-permute-start.86 = (bf16[4,144,512]{2,1,0:T(8,128)(2,1)S(1)}, bf16[4,144,512]{2,1,0:T(8,128)(2,1)}, u32[]{:S(2)}, u32[]{:S(2)}) collective-permute-start(bf16[4,144,512]{2,1,0:T(8,128)(2,1)S(1)} %get-tuple-element.260), channel_id=1, source_target_pairs={{0,4},{4,0},{8,12},{12,8},{16,20},{20,16},{24,28},{28,24},{1,5},{5... | collective-permute-start | bytes 1769480 | tf_op jit(solution)/shard_map/ppermute | solution.py:196
  513.3 3.5 collective-permute-done.53
  531.7 3.5 fusion.247
  537.1 2.8 fusion.244
  541.7 8.0 %collective-permute-done.101 = bf16[2,288,512]{2,1,0:T(8,128)(2,1)S(1)} collective-permute-done((bf16[2,288,512]{2,1,0:T(8,128)(2,1)S(1)}, bf16[2,288,512]{2,1,0:T(8,128)(2,1)S(1)}, u32[]{:S(2)}, u32[]{:S(2)}) %collective-permute-start.101) | collective-permute-done | bytes 589856 | tf_op jit(solution)/shard_map/ppermute | solution.py:196
  551.8 10.5 %collective-permute-done.88 = bf16[2,288,512]{2,1,0:T(8,128)(2,1)S(1)} collective-permute-done((bf16[2,288,512]{2,1,0:T(8,128)(2,1)S(1)}, bf16[2,288,512]{2,1,0:T(8,128)(2,1)S(1)}, u32[]{:S(2)}, u32[]{:S(2)}) %collective-permute-start.88) | collective-permute-done | bytes 589856 | tf_op jit(solution)/shard_map/ppermute | solution.py:196
  564.4 4.2 collective-permute-done.105
  572.6 2.4 collective-permute-done.92
  576.9 8.3 %collective-permute-done.106 = bf16[144,512]{1,0:T(8,128)(2,1)S(1)} collective-permute-done((bf16[144,512]{1,0:T(8,128)(2,1)S(1)}, bf16[144,512]{1,0:T(8,128)(2,1)S(1)}, u32[]{:S(2)}, u32[]{:S(2)}) %collective-permute-start.106) | collective-permute-done | bytes 147488 | tf_op jit(solution)/shard_map/ppermute | solution.py:196
  590.6 4.6 collective-permute-done.93
  597.6 6.5 %collective-permute-start.112 = (bf16[4,144,512]{2,1,0:T(8,128)(2,1)S(1)}, bf16[4,144,512]{2,1,0:T(8,128)(2,1)S(1)}, u32[]{:S(2)}, u32[]{:S(2)}) collective-permute-start(bf16[4,144,512]{2,1,0:T(8,128)(2,1)S(1)} %get-tuple-element.250), channel_id=1, source_target_pairs={{0,4},{4,0},{8,12},{12,8},{16,20},{20,16},{24,28},{28,24},{1,5},{5... | collective-permute-start | bytes 1769480 | tf_op jit(solution)/shard_map/ppermute | solution.py:196
  625.4 2.7 pad_maximum_fusion.7
  (1147 shorter events, 361.9 us)
Async XLA Ops:
  8.6 45.2 %collective-permute-start.2 = (bf16[2,256,128]{2,1,0:T(8,128)(2,1)}, bf16[2,256,128]{2,1,0:T(8,128)(2,1)}, u32[]{:S(2)}, u32[]{:S(2)}) collective-permute-start(bf16[2,256,128]{2,1,0:T(8,128)(2,1)} %bitcast.10), channel_id=1, source_target_pairs={{0,3},{1,2},{2,1},{3,0},{4,7},{5,6},{6,5},{7,4},{8,11},{9,10},{10,... | collective-permute-start | bytes 393224 | tf_op jit(solution)/shard_map/ppermute | solution.py:196
  12.7 46.5 %collective-permute-start.1 = (bf16[2,256,128]{2,1,0:T(8,128)(2,1)}, bf16[2,256,128]{2,1,0:T(8,128)(2,1)}, u32[]{:S(2)}, u32[]{:S(2)}) collective-permute-start(bf16[2,256,128]{2,1,0:T(8,128)(2,1)} %bitcast.10), channel_id=1, source_target_pairs={{0,2},{1,3},{2,0},{3,1},{4,6},{5,7},{6,4},{7,5},{8,10},{9,11},{10,... | collective-permute-start | bytes 393224 | tf_op jit(solution)/shard_map/ppermute | solution.py:196
  12.7 49.7 %collective-permute-start = (bf16[2,256,128]{2,1,0:T(8,128)(2,1)}, bf16[2,256,128]{2,1,0:T(8,128)(2,1)}, u32[]{:S(2)}, u32[]{:S(2)}) collective-permute-start(bf16[2,256,128]{2,1,0:T(8,128)(2,1)} %bitcast.10), channel_id=1, source_target_pairs={{0,1},{1,0},{2,3},{3,2},{4,5},{5,4},{6,7},{7,6},{8,9},{9,8},{10,11... | collective-permute-start | bytes 393224 | tf_op jit(solution)/shard_map/ppermute | solution.py:196
  15.3 48.5 %collective-permute-start.13 = (bf16[2,256,128]{2,1,0:T(8,128)(2,1)}, bf16[2,256,128]{2,1,0:T(8,128)(2,1)}, u32[]{:S(2)}, u32[]{:S(2)}) collective-permute-start(bf16[2,256,128]{2,1,0:T(8,128)(2,1)} %bitcast.52), channel_id=1, source_target_pairs={{0,3},{1,2},{2,1},{3,0},{4,7},{5,6},{6,5},{7,4},{8,11},{9,10},{10,... | collective-permute-start | bytes 393224 | tf_op jit(solution)/shard_map/ppermute | solution.py:196
  18.6 45.7 %collective-permute-start.12 = (bf16[2,256,128]{2,1,0:T(8,128)(2,1)}, bf16[2,256,128]{2,1,0:T(8,128)(2,1)}, u32[]{:S(2)}, u32[]{:S(2)}) collective-permute-start(bf16[2,256,128]{2,1,0:T(8,128)(2,1)} %bitcast.52), channel_id=1, source_target_pairs={{0,2},{1,3},{2,0},{3,1},{4,6},{5,7},{6,4},{7,5},{8,10},{9,11},{10,... | collective-permute-start | bytes 393224 | tf_op jit(solution)/shard_map/ppermute | solution.py:196
  53.8 13.7 %collective-permute-start.11 = (bf16[2,256,128]{2,1,0:T(8,128)(2,1)}, bf16[2,256,128]{2,1,0:T(8,128)(2,1)S(1)}, u32[]{:S(2)}, u32[]{:S(2)}) collective-permute-start(bf16[2,256,128]{2,1,0:T(8,128)(2,1)} %bitcast.52), channel_id=1, source_target_pairs={{0,1},{1,0},{2,3},{3,2},{4,5},{5,4},{6,7},{7,6},{8,9},{9,8},{10,11... | collective-permute-start | bytes 393224 | tf_op jit(solution)/shard_map/ppermute | solution.py:196
  59.2 36.8 %collective-permute-start.21 = (bf16[144,512]{1,0:T(8,128)(2,1)S(1)}, bf16[144,512]{1,0:T(8,128)(2,1)}, u32[]{:S(2)}, u32[]{:S(2)}) collective-permute-start(bf16[144,512]{1,0:T(8,128)(2,1)S(1)} %bitcast.923), channel_id=1, source_target_pairs={{0,3},{1,2},{2,1},{3,0},{4,7},{5,6},{6,5},{7,4},{8,11},{9,10},{10,... | collective-permute-start | bytes 442376 | tf_op jit(solution)/shard_map/ppermute | solution.py:196
  62.5 33.6 %collective-permute-start.20 = (bf16[144,512]{1,0:T(8,128)(2,1)S(1)}, bf16[144,512]{1,0:T(8,128)(2,1)}, u32[]{:S(2)}, u32[]{:S(2)}) collective-permute-start(bf16[144,512]{1,0:T(8,128)(2,1)S(1)} %bitcast.924), channel_id=1, source_target_pairs={{0,2},{1,3},{2,0},{3,1},{4,6},{5,7},{6,4},{7,5},{8,10},{9,11},{10,... | collective-permute-start | bytes 442376 | tf_op jit(solution)/shard_map/ppermute | solution.py:196
  63.9 34.7 %collective-permute-start.17 = (bf16[144,512]{1,0:T(8,128)(2,1)S(1)}, bf16[144,512]{1,0:T(8,128)(2,1)}, u32[]{:S(2)}, u32[]{:S(2)}) collective-permute-start(bf16[144,512]{1,0:T(8,128)(2,1)S(1)} %bitcast.925), channel_id=1, source_target_pairs={{0,1},{1,0},{2,3},{3,2},{4,5},{5,4},{6,7},{7,6},{8,9},{9,8},{10,11... | collective-permute-start | bytes 442376 | tf_op jit(solution)/shard_map/ppermute | solution.py:196
  64.3 36.6 %collective-permute-start.7 = (bf16[144,512]{1,0:T(8,128)(2,1)}, bf16[144,512]{1,0:T(8,128)(2,1)}, u32[]{:S(2)}, u32[]{:S(2)}) collective-permute-start(bf16[144,512]{1,0:T(8,128)(2,1)} %bitcast.28), channel_id=1, source_target_pairs={{0,3},{1,2},{2,1},{3,0},{4,7},{5,6},{6,5},{7,4},{8,11},{9,10},{10,... | collective-permute-start | bytes 442376 | tf_op jit(solution)/shard_map/ppermute | solution.py:196
  67.5 33.4 %collective-permute-start.6 = (bf16[144,512]{1,0:T(8,128)(2,1)}, bf16[144,512]{1,0:T(8,128)(2,1)}, u32[]{:S(2)}, u32[]{:S(2)}) collective-permute-start(bf16[144,512]{1,0:T(8,128)(2,1)} %bitcast.28), channel_id=1, source_target_pairs={{0,2},{1,3},{2,0},{3,1},{4,6},{5,7},{6,4},{7,5},{8,10},{9,11},{10,... | collective-permute-start | bytes 442376 | tf_op jit(solution)/shard_map/ppermute | solution.py:196
  96.0 6.8 %collective-permute-start.3 = (bf16[144,512]{1,0:T(8,128)(2,1)}, bf16[144,512]{1,0:T(8,128)(2,1)S(1)}, u32[]{:S(2)}, u32[]{:S(2)}) collective-permute-start(bf16[144,512]{1,0:T(8,128)(2,1)} %bitcast.28), channel_id=1, source_target_pairs={{0,1},{1,0},{2,3},{3,2},{4,5},{5,4},{6,7},{7,6},{8,9},{9,8},{10,11... | collective-permute-start | bytes 442376 | tf_op jit(solution)/shard_map/ppermute | solution.py:196
  97.3 6.8 %collective-permute-start.22 = (bf16[1,288,512]{2,1,0:T(8,128)(2,1)S(1)}, bf16[1,288,512]{2,1,0:T(8,128)(2,1)S(1)}, u32[]{:S(2)}, u32[]{:S(2)}) collective-permute-start(bf16[1,288,512]{2,1,0:T(8,128)(2,1)S(1)} %bitcast.856), channel_id=1, source_target_pairs={{0,16},{4,20},{8,24},{12,28},{16,0},{20,4},{24,8},{28,12},{1,17},{... | collective-permute-start | bytes 884744 | tf_op jit(solution)/shard_map/ppermute | solution.py:196
  102.6 8.0 %collective-permute-start.8 = (bf16[1,288,512]{2,1,0:T(8,128)(2,1)}, bf16[1,288,512]{2,1,0:T(8,128)(2,1)}, u32[]{:S(2)}, u32[]{:S(2)}) collective-permute-start(bf16[1,288,512]{2,1,0:T(8,128)(2,1)} %bitcast.33), channel_id=1, source_target_pairs={{0,16},{4,20},{8,24},{12,28},{16,0},{20,4},{24,8},{28,12},{1,17},{... | collective-permute-start | bytes 884744 | tf_op jit(solution)/shard_map/ppermute | solution.py:196
  103.8 10.3 %collective-permute-start.4 = (bf16[1,288,512]{2,1,0:T(8,128)(2,1)S(1)}, bf16[1,288,512]{2,1,0:T(8,128)(2,1)}, u32[]{:S(2)}, u32[]{:S(2)}) collective-permute-start(bf16[1,288,512]{2,1,0:T(8,128)(2,1)S(1)} %bitcast.850), channel_id=1, source_target_pairs={{0,8},{4,12},{8,0},{12,4},{16,24},{20,28},{24,16},{28,20},{1,9},{5... | collective-permute-start | bytes 884744 | tf_op jit(solution)/shard_map/ppermute | solution.py:196
  105.0 20.5 %collective-permute-start.23 = (bf16[2,288,512]{2,1,0:T(8,128)(2,1)}, bf16[2,288,512]{2,1,0:T(8,128)(2,1)}, u32[]{:S(2)}, u32[]{:S(2)}) collective-permute-start(bf16[2,288,512]{2,1,0:T(8,128)(2,1)} %pad_maximum_fusion.22), channel_id=1, source_target_pairs={{0,8},{4,12},{8,0},{12,4},{16,24},{20,28},{24,16},{28,20},{1,9},{5... | collective-permute-start | bytes 1769480 | tf_op jit(solution)/shard_map/ppermute | solution.py:196
  107.1 23.7 %collective-permute-start.19 = (bf16[2,288,512]{2,1,0:T(8,128)(2,1)}, bf16[2,288,512]{2,1,0:T(8,128)(2,1)}, u32[]{:S(2)}, u32[]{:S(2)}) collective-permute-start(bf16[2,288,512]{2,1,0:T(8,128)(2,1)} %pad_maximum_fusion.21), channel_id=1, source_target_pairs={{0,16},{4,20},{8,24},{12,28},{16,0},{20,4},{24,8},{28,12},{1,17},{... | collective-permute-start | bytes 1769480 | tf_op jit(solution)/shard_map/ppermute | solution.py:196
  112.5 28.7 %collective-permute-start.9 = (bf16[2,288,512]{2,1,0:T(8,128)(2,1)}, bf16[2,288,512]{2,1,0:T(8,128)(2,1)}, u32[]{:S(2)}, u32[]{:S(2)}) collective-permute-start(bf16[2,288,512]{2,1,0:T(8,128)(2,1)} %pad_maximum_fusion.20), channel_id=1, source_target_pairs={{0,8},{4,12},{8,0},{12,4},{16,24},{20,28},{24,16},{28,20},{1,9},{5... | collective-permute-start | bytes 1769480 | tf_op jit(solution)/shard_map/ppermute | solution.py:196
  115.9 30.7 %collective-permute-start.5 = (bf16[2,288,512]{2,1,0:T(8,128)(2,1)}, bf16[2,288,512]{2,1,0:T(8,128)(2,1)}, u32[]{:S(2)}, u32[]{:S(2)}) collective-permute-start(bf16[2,288,512]{2,1,0:T(8,128)(2,1)} %pad_maximum_fusion.19), channel_id=1, source_target_pairs={{0,16},{4,20},{8,24},{12,28},{16,0},{20,4},{24,8},{28,12},{1,17},{... | collective-permute-start | bytes 1769480 | tf_op jit(solution)/shard_map/ppermute | solution.py:196
  134.4 22.2 %collective-permute-start.24 = (bf16[4,576,512]{2,1,0:T(8,128)(2,1)}, bf16[4,576,512]{2,1,0:T(8,128)(2,1)}, u32[]{:S(2)}, u32[]{:S(2)}) collective-permute-start(bf16[4,576,512]{2,1,0:T(8,128)(2,1)} %get-tuple-element.224), channel_id=1, source_target_pairs={{0,4},{4,0},{8,12},{12,8},{16,20},{20,16},{24,28},{28,24},{1,5},{5... | collective-permute-start | bytes 7077896 | tf_op jit(solution)/shard_map/ppermute | solution.py:196
  150.6 8.4 %collective-permute-start.10 = (bf16[4,576,512]{2,1,0:T(8,128)(2,1)}, bf16[4,576,512]{2,1,0:T(8,128)(2,1)}, u32[]{:S(2)}, u32[]{:S(2)}) collective-permute-start(bf16[4,576,512]{2,1,0:T(8,128)(2,1)} %get-tuple-element.226), channel_id=1, source_target_pairs={{0,4},{4,0},{8,12},{12,8},{16,20},{20,16},{24,28},{28,24},{1,5},{5... | collective-permute-start | bytes 7077896 | tf_op jit(solution)/shard_map/ppermute | solution.py:196
  175.7 8.7 %collective-permute-start.16 = (bf16[2,256,128]{2,1,0:T(8,128)(2,1)S(1)}, bf16[2,256,128]{2,1,0:T(8,128)(2,1)S(1)}, u32[]{:S(2)}, u32[]{:S(2)}) collective-permute-start(bf16[2,256,128]{2,1,0:T(8,128)(2,1)S(1)} %bitcast.934), channel_id=1, source_target_pairs={{0,3},{1,2},{2,1},{3,0},{4,7},{5,6},{6,5},{7,4},{8,11},{9,10},{10,... | collective-permute-start | bytes 393224 | tf_op jit(solution)/shard_map/ppermute | solution.py:196
  178.5 11.6 %collective-permute-start.15 = (bf16[2,256,128]{2,1,0:T(8,128)(2,1)S(1)}, bf16[2,256,128]{2,1,0:T(8,128)(2,1)S(1)}, u32[]{:S(2)}, u32[]{:S(2)}) collective-permute-start(bf16[2,256,128]{2,1,0:T(8,128)(2,1)S(1)} %bitcast.935), channel_id=1, source_target_pairs={{0,2},{1,3},{2,0},{3,1},{4,6},{5,7},{6,4},{7,5},{8,10},{9,11},{10,... | collective-permute-start | bytes 393224 | tf_op jit(solution)/shard_map/ppermute | solution.py:196
  178.5 11.6 %collective-permute-start.14 = (bf16[2,256,128]{2,1,0:T(8,128)(2,1)S(1)}, bf16[2,256,128]{2,1,0:T(8,128)(2,1)S(1)}, u32[]{:S(2)}, u32[]{:S(2)}) collective-permute-start(bf16[2,256,128]{2,1,0:T(8,128)(2,1)S(1)} %bitcast.936), channel_id=1, source_target_pairs={{0,1},{1,0},{2,3},{3,2},{4,5},{5,4},{6,7},{7,6},{8,9},{9,8},{10,11... | collective-permute-start | bytes 393224 | tf_op jit(solution)/shard_map/ppermute | solution.py:196
  268.6 45.6 %collective-permute-start.27 = (bf16[2,256,128]{1,2,0:T(8,128)(2,1)}, bf16[2,256,128]{1,2,0:T(8,128)(2,1)}, u32[]{:S(2)}, u32[]{:S(2)}) collective-permute-start(bf16[2,256,128]{1,2,0:T(8,128)(2,1)} %get-tuple-element.271), channel_id=1, source_target_pairs={{0,3},{1,2},{2,1},{3,0},{4,7},{5,6},{6,5},{7,4},{8,11},{9,10},{10,... | collective-permute-start | bytes 393224 | tf_op jit(solution)/shard_map/ppermute | solution.py:196
  270.1 46.1 %collective-permute-start.26 = (bf16[2,256,128]{1,2,0:T(8,128)(2,1)}, bf16[2,256,128]{1,2,0:T(8,128)(2,1)}, u32[]{:S(2)}, u32[]{:S(2)}) collective-permute-start(bf16[2,256,128]{1,2,0:T(8,128)(2,1)} %get-tuple-element.272), channel_id=1, source_target_pairs={{0,2},{1,3},{2,0},{3,1},{4,6},{5,7},{6,4},{7,5},{8,10},{9,11},{10,... | collective-permute-start | bytes 393224 | tf_op jit(solution)/shard_map/ppermute | solution.py:196
  270.1 48.8 %collective-permute-start.25 = (bf16[2,256,128]{1,2,0:T(8,128)(2,1)}, bf16[2,256,128]{1,2,0:T(8,128)(2,1)}, u32[]{:S(2)}, u32[]{:S(2)}) collective-permute-start(bf16[2,256,128]{1,2,0:T(8,128)(2,1)} %get-tuple-element.270), channel_id=1, source_target_pairs={{0,1},{1,0},{2,3},{3,2},{4,5},{5,4},{6,7},{7,6},{8,9},{9,8},{10,11... | collective-permute-start | bytes 393224 | tf_op jit(solution)/shard_map/ppermute | solution.py:196
  281.9 68.6 %collective-permute-start.33 = (bf16[2,256,128]{1,2,0:T(8,128)(2,1)}, bf16[2,256,128]{1,2,0:T(8,128)(2,1)}, u32[]{:S(2)}, u32[]{:S(2)}) collective-permute-start(bf16[2,256,128]{1,2,0:T(8,128)(2,1)} %get-tuple-element.265), channel_id=1, source_target_pairs={{0,3},{1,2},{2,1},{3,0},{4,7},{5,6},{6,5},{7,4},{8,11},{9,10},{10,... | collective-permute-start | bytes 393224 | tf_op jit(solution)/shard_map/ppermute | solution.py:196
  283.4 67.1 %collective-permute-start.32 = (bf16[2,256,128]{1,2,0:T(8,128)(2,1)}, bf16[2,256,128]{1,2,0:T(8,128)(2,1)}, u32[]{:S(2)}, u32[]{:S(2)}) collective-permute-start(bf16[2,256,128]{1,2,0:T(8,128)(2,1)} %get-tuple-element.266), channel_id=1, source_target_pairs={{0,2},{1,3},{2,0},{3,1},{4,6},{5,7},{6,4},{7,5},{8,10},{9,11},{10,... | collective-permute-start | bytes 393224 | tf_op jit(solution)/shard_map/ppermute | solution.py:196
  314.2 38.4 %collective-permute-start.31 = (bf16[2,256,128]{1,2,0:T(8,128)(2,1)}, bf16[2,256,128]{1,2,0:T(8,128)(2,1)}, u32[]{:S(2)}, u32[]{:S(2)}) collective-permute-start(bf16[2,256,128]{1,2,0:T(8,128)(2,1)} %get-tuple-element.264), channel_id=1, source_target_pairs={{0,1},{1,0},{2,3},{3,2},{4,5},{5,4},{6,7},{7,6},{8,9},{9,8},{10,11... | collective-permute-start | bytes 393224 | tf_op jit(solution)/shard_map/ppermute | solution.py:196
  316.2 214.0 %collective-permute-start.100 = (bf16[4,576,512]{2,1,0:T(8,128)(2,1)}, bf16[4,576,512]{2,1,0:T(8,128)(2,1)}, u32[]{:S(2)}, u32[]{:S(2)}) collective-permute-start(bf16[4,576,512]{2,1,0:T(8,128)(2,1)} %fusion.47), channel_id=1, source_target_pairs={{0,4},{4,0},{8,12},{12,8},{16,20},{20,16},{24,28},{28,24},{1,5},{5... | collective-permute-start | bytes 7077896 | tf_op jit(solution)/shard_map/ppermute | solution.py:196
  348.7 39.9 %collective-permute-start.30 = (bf16[2,256,128]{1,2,0:T(8,128)(2,1)}, bf16[2,256,128]{1,2,0:T(8,128)(2,1)S(1)}, u32[]{:S(2)}, u32[]{:S(2)}) collective-permute-start(bf16[2,256,128]{1,2,0:T(8,128)(2,1)} %get-tuple-element.268), channel_id=1, source_target_pairs={{0,3},{1,2},{2,1},{3,0},{4,7},{5,6},{6,5},{7,4},{8,11},{9,10},{10,... | collective-permute-start | bytes 393224 | tf_op jit(solution)/shard_map/ppermute | solution.py:196
  350.5 38.2 %collective-permute-start.29 = (bf16[2,256,128]{1,2,0:T(8,128)(2,1)}, bf16[2,256,128]{1,2,0:T(8,128)(2,1)S(1)}, u32[]{:S(2)}, u32[]{:S(2)}) collective-permute-start(bf16[2,256,128]{1,2,0:T(8,128)(2,1)} %get-tuple-element.269), channel_id=1, source_target_pairs={{0,2},{1,3},{2,0},{3,1},{4,6},{5,7},{6,4},{7,5},{8,10},{9,11},{10,... | collective-permute-start | bytes 393224 | tf_op jit(solution)/shard_map/ppermute | solution.py:196
  350.6 38.6 %collective-permute-start.28 = (bf16[2,256,128]{1,2,0:T(8,128)(2,1)}, bf16[2,256,128]{1,2,0:T(8,128)(2,1)S(1)}, u32[]{:S(2)}, u32[]{:S(2)}) collective-permute-start(bf16[2,256,128]{1,2,0:T(8,128)(2,1)} %get-tuple-element.267), channel_id=1, source_target_pairs={{0,1},{1,0},{2,3},{3,2},{4,5},{5,4},{6,7},{7,6},{8,9},{9,8},{10,11... | collective-permute-start | bytes 393224 | tf_op jit(solution)/shard_map/ppermute | solution.py:196
  360.1 61.5 %collective-permute-start.71 = (bf16[4,144,512]{2,1,0:T(8,128)(2,1)}, bf16[4,144,512]{2,1,0:T(8,128)(2,1)}, u32[]{:S(2)}, u32[]{:S(2)}) collective-permute-start(bf16[4,144,512]{2,1,0:T(8,128)(2,1)} %slice_bitcast_fusion.7), channel_id=1, source_target_pairs={{0,4},{4,0},{8,12},{12,8},{16,20},{20,16},{24,28},{28,24},{1,5},{5... | collective-permute-start | bytes 1769480 | tf_op jit(solution)/shard_map/ppermute | solution.py:196
  388.5 34.4 %collective-permute-start.55 = (bf16[4,144,512]{2,1,0:T(8,128)(2,1)}, bf16[4,144,512]{2,1,0:T(8,128)(2,1)}, u32[]{:S(2)}, u32[]{:S(2)}) collective-permute-start(bf16[4,144,512]{2,1,0:T(8,128)(2,1)} %slice_bitcast_fusion.9), channel_id=1, source_target_pairs={{0,4},{4,0},{8,12},{12,8},{16,20},{20,16},{24,28},{28,24},{1,5},{5... | collective-permute-start | bytes 1769480 | tf_op jit(solution)/shard_map/ppermute | solution.py:196
  388.6 148.4 %collective-permute-start.87 = (bf16[4,576,512]{2,1,0:T(8,128)(2,1)}, bf16[4,576,512]{2,1,0:T(8,128)(2,1)}, u32[]{:S(2)}, u32[]{:S(2)}) collective-permute-start(bf16[4,576,512]{2,1,0:T(8,128)(2,1)} %fusion.46), channel_id=1, source_target_pairs={{0,4},{4,0},{8,12},{12,8},{16,20},{20,16},{24,28},{28,24},{1,5},{5... | collective-permute-start | bytes 7077896 | tf_op jit(solution)/shard_map/ppermute | solution.py:196
  411.2 14.7 %collective-permute-start.39 = (bf16[4,144,512]{2,1,0:T(8,128)(2,1)}, bf16[4,144,512]{2,1,0:T(8,128)(2,1)}, u32[]{:S(2)}, u32[]{:S(2)}) collective-permute-start(bf16[4,144,512]{2,1,0:T(8,128)(2,1)} %slice_bitcast_fusion.11), channel_id=1, source_target_pairs={{0,4},{4,0},{8,12},{12,8},{16,20},{20,16},{24,28},{28,24},{1,5},{5... | collective-permute-start | bytes 1769480 | tf_op jit(solution)/shard_map/ppermute | solution.py:196
  426.0 7.1 %collective-permute-start.58 = (bf16[2,72,512]{2,1,0:T(8,128)(2,1)S(1)}, bf16[2,72,512]{2,1,0:T(8,128)(2,1)S(1)}, u32[]{:S(2)}, u32[]{:S(2)}) collective-permute-start(bf16[2,72,512]{2,1,0:T(8,128)(2,1)S(1)} %pad_maximum_fusion.49), channel_id=1, source_target_pairs={{0,8},{4,12},{8,0},{12,4},{16,24},{20,28},{24,16},{28,20},{1,9},{5... | collective-permute-start | bytes 442376 | tf_op jit(solution)/shard_map/ppermute | solution.py:196
  464.3 8.2 %collective-permute-start.84 = (bf16[1,72,512]{2,1,0:T(8,128)(2,1)S(1)}, bf16[1,72,512]{2,1,0:T(8,128)(2,1)S(1)}, u32[]{:S(2)}, u32[]{:S(2)}) collective-permute-start(bf16[1,72,512]{2,1,0:T(8,128)(2,1)S(1)} %broadcast_in_dim.434), channel_id=1, source_target_pairs={{0,16},{4,20},{8,24},{12,28},{16,0},{20,4},{24,8},{28,12},{1,17},{... | collective-permute-start | bytes 221192 | tf_op jit(solution)/shard_map/ppermute | solution.py:196
  482.1 9.0 %collective-permute-start.85 = (bf16[2,72,512]{2,1,0:T(8,128)(2,1)S(1)}, bf16[2,72,512]{2,1,0:T(8,128)(2,1)S(1)}, u32[]{:S(2)}, u32[]{:S(2)}) collective-permute-start(bf16[2,72,512]{2,1,0:T(8,128)(2,1)S(1)} %pad_maximum_fusion.56), channel_id=1, source_target_pairs={{0,8},{4,12},{8,0},{12,4},{16,24},{20,28},{24,16},{28,20},{1,9},{5... | collective-permute-start | bytes 442376 | tf_op jit(solution)/shard_map/ppermute | solution.py:196
  483.1 9.1 %collective-permute-start.83 = (bf16[2,72,512]{2,1,0:T(8,128)(2,1)S(1)}, bf16[2,72,512]{2,1,0:T(8,128)(2,1)S(1)}, u32[]{:S(2)}, u32[]{:S(2)}) collective-permute-start(bf16[2,72,512]{2,1,0:T(8,128)(2,1)S(1)} %pad_maximum_fusion.55), channel_id=1, source_target_pairs={{0,16},{4,20},{8,24},{12,28},{16,0},{20,4},{24,8},{28,12},{1,17},{... | collective-permute-start | bytes 442376 | tf_op jit(solution)/shard_map/ppermute | solution.py:196
  489.8 21.2 %collective-permute-start.69 = (bf16[2,72,512]{2,1,0:T(8,128)(2,1)S(1)}, bf16[2,72,512]{2,1,0:T(8,128)(2,1)S(1)}, u32[]{:S(2)}, u32[]{:S(2)}) collective-permute-start(bf16[2,72,512]{2,1,0:T(8,128)(2,1)S(1)} %pad_maximum_fusion.52), channel_id=1, source_target_pairs={{0,8},{4,12},{8,0},{12,4},{16,24},{20,28},{24,16},{28,20},{1,9},{5... | collective-permute-start | bytes 442376 | tf_op jit(solution)/shard_map/ppermute | solution.py:196
  491.1 21.3 %collective-permute-start.67 = (bf16[2,72,512]{2,1,0:T(8,128)(2,1)S(1)}, bf16[2,72,512]{2,1,0:T(8,128)(2,1)S(1)}, u32[]{:S(2)}, u32[]{:S(2)}) collective-permute-start(bf16[2,72,512]{2,1,0:T(8,128)(2,1)S(1)} %pad_maximum_fusion.51), channel_id=1, source_target_pairs={{0,16},{4,20},{8,24},{12,28},{16,0},{20,4},{24,8},{28,12},{1,17},{... | collective-permute-start | bytes 442376 | tf_op jit(solution)/shard_map/ppermute | solution.py:196
  496.1 23.1 %collective-permute-start.86 = (bf16[4,144,512]{2,1,0:T(8,128)(2,1)S(1)}, bf16[4,144,512]{2,1,0:T(8,128)(2,1)}, u32[]{:S(2)}, u32[]{:S(2)}) collective-permute-start(bf16[4,144,512]{2,1,0:T(8,128)(2,1)S(1)} %get-tuple-element.260), channel_id=1, source_target_pairs={{0,4},{4,0},{8,12},{12,8},{16,20},{20,16},{24,28},{28,24},{1,5},{5... | collective-permute-start | bytes 1769480 | tf_op jit(solution)/shard_map/ppermute | solution.py:196
  535.2 14.5 %collective-permute-start.101 = (bf16[2,288,512]{2,1,0:T(8,128)(2,1)S(1)}, bf16[2,288,512]{2,1,0:T(8,128)(2,1)S(1)}, u32[]{:S(2)}, u32[]{:S(2)}) collective-permute-start(bf16[2,288,512]{2,1,0:T(8,128)(2,1)S(1)} %stack.453), channel_id=1, source_target_pairs={{0,16},{4,20},{8,24},{12,28},{16,0},{20,4},{24,8},{28,12},{1,17},{... | collective-permute-start | bytes 1769480 | tf_op jit(solution)/shard_map/ppermute | solution.py:196
  536.2 14.6 %collective-permute-start.104 = (bf16[2,288,512]{2,1,0:T(8,128)(2,1)S(1)}, bf16[2,288,512]{2,1,0:T(8,128)(2,1)S(1)}, u32[]{:S(2)}, u32[]{:S(2)}) collective-permute-start(bf16[2,288,512]{2,1,0:T(8,128)(2,1)S(1)} %pad_maximum_fusion.28), channel_id=1, source_target_pairs={{0,8},{4,12},{8,0},{12,4},{16,24},{20,28},{24,16},{28,20},{1,9},{5... | collective-permute-start | bytes 1769480 | tf_op jit(solution)/shard_map/ppermute | solution.py:196
  539.9 22.4 %collective-permute-start.88 = (bf16[2,288,512]{2,1,0:T(8,128)(2,1)S(1)}, bf16[2,288,512]{2,1,0:T(8,128)(2,1)S(1)}, u32[]{:S(2)}, u32[]{:S(2)}) collective-permute-start(bf16[2,288,512]{2,1,0:T(8,128)(2,1)S(1)} %stack.451), channel_id=1, source_target_pairs={{0,16},{4,20},{8,24},{12,28},{16,0},{20,4},{24,8},{28,12},{1,17},{... | collective-permute-start | bytes 1769480 | tf_op jit(solution)/shard_map/ppermute | solution.py:196
  540.9 22.5 %collective-permute-start.91 = (bf16[2,288,512]{2,1,0:T(8,128)(2,1)S(1)}, bf16[2,288,512]{2,1,0:T(8,128)(2,1)S(1)}, u32[]{:S(2)}, u32[]{:S(2)}) collective-permute-start(bf16[2,288,512]{2,1,0:T(8,128)(2,1)S(1)} %pad_maximum_fusion.26), channel_id=1, source_target_pairs={{0,8},{4,12},{8,0},{12,4},{16,24},{20,28},{24,16},{28,20},{1,9},{5... | collective-permute-start | bytes 1769480 | tf_op jit(solution)/shard_map/ppermute | solution.py:196
  550.0 20.5 %collective-permute-start.102 = (bf16[1,288,512]{2,1,0:T(8,128)(2,1)S(1)}, bf16[1,288,512]{2,1,0:T(8,128)(2,1)S(1)}, u32[]{:S(2)}, u32[]{:S(2)}) collective-permute-start(bf16[1,288,512]{2,1,0:T(8,128)(2,1)S(1)} %slice.1349), channel_id=1, source_target_pairs={{0,8},{4,12},{8,0},{12,4},{16,24},{20,28},{24,16},{28,20},{1,9},{5... | collective-permute-start | bytes 884744 | tf_op jit(solution)/shard_map/ppermute | solution.py:196
  551.0 17.7 %collective-permute-start.105 = (bf16[1,288,512]{2,1,0:T(8,128)(2,1)S(1)}, bf16[1,288,512]{2,1,0:T(8,128)(2,1)S(1)}, u32[]{:S(2)}, u32[]{:S(2)}) collective-permute-start(bf16[1,288,512]{2,1,0:T(8,128)(2,1)S(1)} %slice.1348), channel_id=1, source_target_pairs={{0,16},{4,20},{8,24},{12,28},{16,0},{20,4},{24,8},{28,12},{1,17},{... | collective-permute-start | bytes 884744 | tf_op jit(solution)/shard_map/ppermute | solution.py:196
  562.6 14.2 %collective-permute-start.89 = (bf16[1,288,512]{2,1,0:T(8,128)(2,1)S(1)}, bf16[1,288,512]{2,1,0:T(8,128)(2,1)S(1)}, u32[]{:S(2)}, u32[]{:S(2)}) collective-permute-start(bf16[1,288,512]{2,1,0:T(8,128)(2,1)S(1)} %slice.1351), channel_id=1, source_target_pairs={{0,8},{4,12},{8,0},{12,4},{16,24},{20,28},{24,16},{28,20},{1,9},{5... | collective-permute-start | bytes 884744 | tf_op jit(solution)/shard_map/ppermute | solution.py:196
  563.6 11.4 %collective-permute-start.92 = (bf16[1,288,512]{2,1,0:T(8,128)(2,1)S(1)}, bf16[1,288,512]{2,1,0:T(8,128)(2,1)S(1)}, u32[]{:S(2)}, u32[]{:S(2)}) collective-permute-start(bf16[1,288,512]{2,1,0:T(8,128)(2,1)S(1)} %slice.1350), channel_id=1, source_target_pairs={{0,16},{4,20},{8,24},{12,28},{16,0},{20,4},{24,8},{28,12},{1,17},{... | collective-permute-start | bytes 884744 | tf_op jit(solution)/shard_map/ppermute | solution.py:196
  568.8 8.1 %collective-permute-start.107 = (bf16[144,512]{1,0:T(8,128)(2,1)S(1)}, bf16[144,512]{1,0:T(8,128)(2,1)S(1)}, u32[]{:S(2)}, u32[]{:S(2)}) collective-permute-start(bf16[144,512]{1,0:T(8,128)(2,1)S(1)} %get-tuple-element.276), channel_id=1, source_target_pairs={{0,3},{1,2},{2,1},{3,0},{4,7},{5,6},{6,5},{7,4},{8,11},{9,10},{10,... | collective-permute-start | bytes 442376 | tf_op jit(solution)/shard_map/ppermute | solution.py:196
  570.5 14.7 %collective-permute-start.106 = (bf16[144,512]{1,0:T(8,128)(2,1)S(1)}, bf16[144,512]{1,0:T(8,128)(2,1)S(1)}, u32[]{:S(2)}, u32[]{:S(2)}) collective-permute-start(bf16[144,512]{1,0:T(8,128)(2,1)S(1)} %get-tuple-element.275), channel_id=1, source_target_pairs={{0,2},{1,3},{2,0},{3,1},{4,6},{5,7},{6,4},{7,5},{8,10},{9,11},{10,... | collective-permute-start | bytes 442376 | tf_op jit(solution)/shard_map/ppermute | solution.py:196
  570.6 14.6 %collective-permute-start.103 = (bf16[144,512]{1,0:T(8,128)(2,1)S(1)}, bf16[144,512]{1,0:T(8,128)(2,1)S(1)}, u32[]{:S(2)}, u32[]{:S(2)}) collective-permute-start(bf16[144,512]{1,0:T(8,128)(2,1)S(1)} %fusion.175), channel_id=1, source_target_pairs={{0,1},{1,0},{2,3},{3,2},{4,5},{5,4},{6,7},{7,6},{8,9},{9,8},{10,11... | collective-permute-start | bytes 442376 | tf_op jit(solution)/shard_map/ppermute | solution.py:196
  575.1 15.5 %collective-permute-start.94 = (bf16[144,512]{1,0:T(8,128)(2,1)S(1)}, bf16[144,512]{1,0:T(8,128)(2,1)S(1)}, u32[]{:S(2)}, u32[]{:S(2)}) collective-permute-start(bf16[144,512]{1,0:T(8,128)(2,1)S(1)} %get-tuple-element.274), channel_id=1, source_target_pairs={{0,3},{1,2},{2,1},{3,0},{4,7},{5,6},{6,5},{7,4},{8,11},{9,10},{10,... | collective-permute-start | bytes 442376 | tf_op jit(solution)/shard_map/ppermute | solution.py:196
  576.8 18.4 %collective-permute-start.93 = (bf16[144,512]{1,0:T(8,128)(2,1)S(1)}, bf16[144,512]{1,0:T(8,128)(2,1)S(1)}, u32[]{:S(2)}, u32[]{:S(2)}) collective-permute-start(bf16[144,512]{1,0:T(8,128)(2,1)S(1)} %get-tuple-element.273), channel_id=1, source_target_pairs={{0,2},{1,3},{2,0},{3,1},{4,6},{5,7},{6,4},{7,5},{8,10},{9,11},{10,... | collective-permute-start | bytes 442376 | tf_op jit(solution)/shard_map/ppermute | solution.py:196
  586.2 9.0 %collective-permute-start.90 = (bf16[144,512]{1,0:T(8,128)(2,1)S(1)}, bf16[144,512]{1,0:T(8,128)(2,1)S(1)}, u32[]{:S(2)}, u32[]{:S(2)}) collective-permute-start(bf16[144,512]{1,0:T(8,128)(2,1)S(1)} %fusion.174), channel_id=1, source_target_pairs={{0,1},{1,0},{2,3},{3,2},{4,5},{5,4},{6,7},{7,6},{8,9},{9,8},{10,11... | collective-permute-start | bytes 442376 | tf_op jit(solution)/shard_map/ppermute | solution.py:196
  588.9 8.0 %collective-permute-start.111 = (bf16[2,72,512]{2,1,0:T(8,128)(2,1)S(1)}, bf16[2,72,512]{2,1,0:T(8,128)(2,1)S(1)}, u32[]{:S(2)}, u32[]{:S(2)}) collective-permute-start(bf16[2,72,512]{2,1,0:T(8,128)(2,1)S(1)} %pad_maximum_fusion.60), channel_id=1, source_target_pairs={{0,8},{4,12},{8,0},{12,4},{16,24},{20,28},{24,16},{28,20},{1,9},{5... | collective-permute-start | bytes 442376 | tf_op jit(solution)/shard_map/ppermute | solution.py:196
  589.9 7.6 %collective-permute-start.109 = (bf16[2,72,512]{2,1,0:T(8,128)(2,1)S(1)}, bf16[2,72,512]{2,1,0:T(8,128)(2,1)S(1)}, u32[]{:S(2)}, u32[]{:S(2)}) collective-permute-start(bf16[2,72,512]{2,1,0:T(8,128)(2,1)S(1)} %pad_maximum_fusion.59), channel_id=1, source_target_pairs={{0,16},{4,20},{8,24},{12,28},{16,0},{20,4},{24,8},{28,12},{1,17},{... | collective-permute-start | bytes 442376 | tf_op jit(solution)/shard_map/ppermute | solution.py:196
  595.3 8.8 %collective-permute-start.97 = (bf16[1,72,512]{2,1,0:T(8,128)(2,1)S(1)}, bf16[1,72,512]{2,1,0:T(8,128)(2,1)}, u32[]{:S(2)}, u32[]{:S(2)}) collective-permute-start(bf16[1,72,512]{2,1,0:T(8,128)(2,1)S(1)} %get-tuple-element.278), channel_id=1, source_target_pairs={{0,16},{4,20},{8,24},{12,28},{16,0},{20,4},{24,8},{28,12},{1,17},{... | collective-permute-start | bytes 221192 | tf_op jit(solution)/shard_map/ppermute | solution.py:196
  596.2 10.2 %collective-permute-start.95 = (bf16[1,72,512]{2,1,0:T(8,128)(2,1)S(1)}, bf16[1,72,512]{2,1,0:T(8,128)(2,1)}, u32[]{:S(2)}, u32[]{:S(2)}) collective-permute-start(bf16[1,72,512]{2,1,0:T(8,128)(2,1)S(1)} %get-tuple-element.277), channel_id=1, source_target_pairs={{0,8},{4,12},{8,0},{12,4},{16,24},{20,28},{24,16},{28,20},{1,9},{5... | collective-permute-start | bytes 221192 | tf_op jit(solution)/shard_map/ppermute | solution.py:196
  597.6 19.0 %collective-permute-start.112 = (bf16[4,144,512]{2,1,0:T(8,128)(2,1)S(1)}, bf16[4,144,512]{2,1,0:T(8,128)(2,1)S(1)}, u32[]{:S(2)}, u32[]{:S(2)}) collective-permute-start(bf16[4,144,512]{2,1,0:T(8,128)(2,1)S(1)} %get-tuple-element.250), channel_id=1, source_target_pairs={{0,4},{4,0},{8,12},{12,8},{16,20},{20,16},{24,28},{28,24},{1,5},{5... | collective-permute-start | bytes 1769480 | tf_op jit(solution)/shard_map/ppermute | solution.py:196
  (269 other events, 1295.8 us)

commit v2 on v0

v2 whole, which is shorter than its diff:
```python
import functools
import jax
import jax.numpy as jnp
from jax import lax
from jax.experimental import pallas as pl
from jax.experimental.pallas import tpu as pltpu
from jax.sharding import PartitionSpec as P

EPS = 1e-05
LOW = jnp.bfloat16
FULL = jnp.float32
VMEM_BYTES = 56 * 1024 * 1024


def mm(left, right):
    return jnp.dot(left, right, preferred_element_type=FULL)


def mm_nt(left, right):
    return lax.dot_general(left, right, (((1,), (1,)), ((), ())), preferred_element_type=FULL)


def normalise(values):
    center = values - jnp.mean(values, -1, keepdims=True)
    inverse = lax.rsqrt(jnp.mean(center * center, -1, keepdims=True) + EPS)
    return center * inverse, inverse


def norm_back(upstream, normal, inverse, gain_row):
    scaled = upstream * gain_row
    return inverse * (
        scaled
        - jnp.mean(scaled, -1, keepdims=True)
        - normal * jnp.mean(scaled * normal, -1, keepdims=True)
    )


def split_low(values):
    high = values.astype(LOW)
    return high, (values - high.astype(FULL)).astype(LOW)


def gelu_parts(pre):
    c = 0.7978845608028654
    square = pre * pre
    t = jnp.tanh(c * pre * (1.0 + 0.044715 * square))
    half = 0.5 * (1.0 + t)
    act = pre * half
    slope = half + (0.5 * c) * pre * (1.0 - t * t) * (1.0 + 0.134145 * square)
    return act, slope


def call(body, out_shape, args, scratch=(), smem=1, flops=0, name=None):
    specs = [pl.BlockSpec(memory_space=pltpu.SMEM)] * smem + [
        pl.BlockSpec(memory_space=pltpu.VMEM)
    ] * (len(args) - smem)
    return pl.pallas_call(
        body,
        out_shape=out_shape,
        in_specs=specs,
        out_specs=jax.tree.map(lambda _: pl.BlockSpec(memory_space=pltpu.VMEM), out_shape),
        scratch_shapes=list(scratch),
        compiler_params=pltpu.CompilerParams(vmem_limit_bytes=VMEM_BYTES),
        cost_estimate=pl.CostEstimate(flops=flops, bytes_accessed=4 << 20, transcendentals=0),
        name=name,
    )(*args)


def like(shape, dtype):
    return jax.ShapeDtypeStruct(shape, dtype)


def prepare_kernel(meta, source, target, gain, shift, keyval, h_source, h_target, kv_source, kv_target):
    for value, row, h_out, kv_out in ((source, 0, h_source, kv_source), (target, 2, h_target, kv_target)):
        normal, _ = normalise(value[...].astype(FULL))
        h = (normal * gain[row : row + 1] + shift[row : row + 1]).astype(LOW)
        h_out[...] = h
        kv_out[...] = mm(h, keyval[row // 2]).astype(LOW)


def to_slots(values, groups):
    part = values.shape[1] // groups
    blocks = []
    for g in range(groups):
        block = values[:, g * part : (g + 1) * part]
        blocks += [block, block]
    return jnp.concatenate(blocks, 1)


def slot_queries(h, route, query_proj, router_t, groups, slot_out, gate_out):
    experts = router_t.shape[0]
    queries = mm(h, query_proj).astype(LOW)
    spread = to_slots(queries.T, groups)
    head = spread.shape[0] // experts
    chosen = jnp.zeros((head, spread.shape[1]), LOW)
    for e in range(experts):
        chosen = jnp.where(route == e, spread[e * head : (e + 1) * head], chosen)
    slot_out[...] = chosen * jnp.asarray(float(head) ** -0.5, LOW)
    logits = to_slots(mm_nt(router_t, h), groups)
    ids = lax.broadcasted_iota(jnp.int32, logits.shape, 0)
    picked = jnp.sum(jnp.where(ids == route, logits, 0.0), 0, keepdims=True)
    part = picked.shape[1] // (2 * groups)
    gates = []
    for g in range(groups):
        a = picked[:, 2 * g * part : (2 * g + 1) * part]
        b = picked[:, (2 * g + 1) * part : (2 * g + 2) * part]
        top = jnp.maximum(a, b)
        ea, eb = jnp.exp(a - top), jnp.exp(b - top)
        total = ea + eb
        gates += [ea / total, eb / total]
    gate_out[...] = jnp.concatenate(gates, 1)


def allowed_keys(shape, z, part, planes, length, causal):
    blocks = []
    for k in range(planes):
        position = (z ^ k) * part + lax.broadcasted_iota(jnp.int32, (part, shape[1]), 0)
        ok = position < length
        if causal:
            lane = lax.broadcasted_iota(jnp.int32, (part, shape[1]), 1)
            query = z * part + jnp.where(lane >= part, lane - part, lane)
            ok = ok & (position <= query)
        blocks.append(ok)
    return jnp.concatenate(blocks, 0)


def attend(meta, side, causal, slots, gates, route, kv_refs, out_proj, groups, experts, lse_out, att_out):
    z = meta[1]
    part = kv_refs[0].shape[0] // groups
    planes = len(kv_refs)
    head = slots.shape[0]
    lanes = 2 * part
    columns = []
    for g in range(groups):
        kv = jnp.concatenate([ref[g * part : (g + 1) * part, :] for ref in kv_refs], 0)
        q = slots[:, g * lanes : (g + 1) * lanes]
        padded = jnp.concatenate([q, jnp.zeros_like(q)], 0)
        scores = mm(kv, padded)
        ok = allowed_keys(scores.shape, z, part, planes, meta[2 + 2 * side + g], causal)
        scores = jnp.where(ok, scores, -1e30)
        top = jnp.max(scores, 0, keepdims=True)
        raised = jnp.exp(scores - top)
        total = jnp.sum(raised, 0, keepdims=True)
        lse_out[:, g * lanes : (g + 1) * lanes] = top + jnp.log(total)
        low = (raised * (1.0 / total)).astype(LOW)
        attended = mm(kv.T, low)[head:]
        att_out[:, g * lanes : (g + 1) * lanes] = attended
        gated = attended * gates[:, g * lanes : (g + 1) * lanes]
        ids = route[:, g * lanes : (g + 1) * lanes]
        rows = []
        for e in range(experts):
            first = jnp.where(ids[:, :part] == e, gated[:, :part], 0.0)
            rows.append(jnp.where(ids[:, part:] == e, gated[:, part:], first).astype(LOW))
        columns.append(jnp.concatenate(rows, 0))
    mixed = jnp.concatenate(columns, 1)
    return mixed, mm(mixed.T, out_proj)


def queries_kernel(groups, meta, h, route, query_proj, router_t, slot_out, gate_out):
    slot_queries(h[...], route[...], query_proj[...], router_t[...], groups, slot_out, gate_out)


def attend_kernel(groups, side, causal, planes, next_queries, meta, resid, slots, gates, route, *rest):
    kv_refs, rest = rest[:planes], rest[planes:]
    out_proj, rest = rest[0], rest[1:]
    if next_queries:
        (gain, shift, next_route, next_proj, next_router, new_resid, lse_out, att_out, mixed_out, next_slots, next_gates) = rest
    else:
        (new_resid, lse_out, att_out, mixed_out) = rest
    experts = out_proj.shape[0] // slots.shape[0]
    mixed, branch = attend(meta, side, causal, slots, gates, route, kv_refs, out_proj[...], groups, experts, lse_out, att_out)
    mixed_out[...] = mixed
    total = resid[...].astype(FULL) + branch
    new_resid[...] = total
    if next_queries:
        normal, _ = normalise(total)
        h = (normal * gain[3:4] + shift[3:4]).astype(LOW)
        slot_queries(h, next_route[...], next_proj[...], next_router[...], groups, next_slots, next_gates)


def place_weights(meta, own_first, own_second, pieces, first, second):
    r = meta[0]
    first[0] = own_first[...]
    second[0] = own_second[...]
    ways = len(pieces)
    rows = own_first.shape[0] // ways
    for j, piece in enumerate(pieces):
        at = pl.ds(pl.multiple_of((r ^ j) * rows, rows), rows)
        for k in range(1, first.shape[0]):
            first[k, at, :] = piece[k - 1, :rows]
            second[k, at, :] = piece[k - 1, rows : 2 * rows]


def feed_forward_kernel(ways, meta, state, gain, shift, out_bias, bias, keyval, own_first, own_second, *rest):
    pieces, (memory, low_out, kv_out, first, second) = rest[:ways], rest[ways:]
    place_weights(meta, own_first, own_second, pieces, first, second)
    value = state[...]
    normal, _ = normalise(value)
    h = (normal * gain[1:2] + shift[1:2]).astype(LOW)
    memory[...] = value + out_bias[0:1].astype(FULL)

    def step(k, carry):
        pre = mm(h, first[k]) + bias[k]
        act = jax.nn.gelu(pre).astype(LOW)
        memory[...] += mm_nt(act, second[k])
        return carry

    lax.fori_loop(0, first.shape[0], step, 0)
    low = memory[...].astype(LOW)
    low_out[...] = low
    kv_out[...] = mm(low, keyval[...]).astype(LOW)


def feed_backward_core(meta, h, upstream_low, ways, bias, first, second, grad, d_h, kept, sent, bias_grad, state):
    r, z = meta[0], meta[1]
    h_t = h.T
    up_t = upstream_low.T
    d_h[...] = jnp.zeros_like(d_h)
    rows = h.shape[1] // ways

    def step(k, carry):
        w_first, w_second = first[k], second[k]
        pre = mm(h, w_first) + bias[k]
        act, slope = gelu_parts(pre)
        act = act.astype(LOW)
        if state is not None:
            state[...] += mm_nt(act, w_second)
        d_pre_full = (mm(upstream_low, w_second) * slope).astype(LOW)
        d_h[...] += mm_nt(d_pre_full, w_first)
        bias_grad[z ^ k] = jnp.sum(d_pre_full.astype(FULL), 0, keepdims=True)
        for half, product in enumerate((mm(h_t, d_pre_full), mm(up_t, act))):
            grad[...] = product
            for j in range(ways):
                block = grad[pl.ds(pl.multiple_of((r ^ j) * rows, rows), rows), :].astype(LOW)
                target = sent if j & 1 else kept
                target[j // 2, k, half * rows : (half + 1) * rows, :] = block
        return carry

    lax.fori_loop(0, first.shape[0], step, 0)


def decoder_feed_kernel(ways, groups, meta, state_in, cotangent, gain, shift, out_bias, bias, own_first, own_second, *rest):
    pieces, (decoded, state_grad, kept, sent, bias_grad, sums, first, second, grad, d_h) = rest[:ways], rest[ways:]
    place_weights(meta, own_first, own_second, pieces, first, second)
    value = state_in[...]
    normal, inverse = normalise(value)
    h = (normal * gain[4:5] + shift[4:5]).astype(LOW)
    decoded[...] = value + out_bias[1:2].astype(FULL)
    part = value.shape[0] // groups
    seeds = []
    for g in range(groups):
        row = meta[1] * part + lax.broadcasted_iota(jnp.int32, (part, value.shape[1]), 0)
        seeds.append(jnp.where(row < meta[4 + g], cotangent[g * part : (g + 1) * part, :].astype(FULL), 0.0))
    seed = jnp.concatenate(seeds, 0)
    feed_backward_core(meta, h, seed.astype(LOW), ways, bias, first, second, grad, d_h, kept, sent, bias_grad, decoded)
    normal, inverse = normalise(state_in[...])
    upstream = d_h[...]
    state_grad[...] = seed + norm_back(upstream, normal, inverse, gain[4:5])
    sums[0:1] = jnp.sum(upstream * normal, 0, keepdims=True)
    sums[1:2] = jnp.sum(upstream, 0, keepdims=True)
    sums[2:3] = jnp.sum(seed, 0, keepdims=True)
    sums[3:8] = jnp.zeros((5, sums.shape[1]), FULL)


def total_of(blocks):
    total = blocks[0][...].astype(FULL)
    for block in blocks[1:]:
        total = total + block[...].astype(FULL)
    return total.astype(LOW)


def encoder_feed_kernel(ways, planes, meta, state_in, memory_low, gain, shift, bias, keyval, *rest):
    blocks, rest = rest[:planes], rest[planes:]
    own_first, own_second = rest[:2]
    pieces, rest = rest[2 : 2 + ways], rest[2 + ways :]
    (memory_grad, state_grad, keyval_grad, kept, sent, bias_grad, sums, first, second, grad, d_h) = rest
    place_weights(meta, own_first, own_second, pieces, first, second)
    d_kv = total_of(blocks)
    upstream_in = mm_nt(d_kv, keyval[...])
    memory_grad[...] = upstream_in
    keyval_grad[...] = mm(d_kv.T, memory_low[...])
    normal, inverse = normalise(state_in[...])
    h = (normal * gain[1:2] + shift[1:2]).astype(LOW)
    feed_backward_core(meta, h, upstream_in.astype(LOW), ways, bias, first, second, grad, d_h, kept, sent, bias_grad, None)
    normal, inverse = normalise(state_in[...])
    upstream = d_h[...]
    state_grad[...] = memory_grad[...] + norm_back(upstream, normal, inverse, gain[1:2])
    sums[0:1] = jnp.sum(upstream * normal, 0, keepdims=True)
    sums[1:2] = jnp.sum(upstream, 0, keepdims=True)
    sums[2:3] = jnp.sum(memory_grad[...], 0, keepdims=True)
    sums[3:8] = jnp.zeros((5, sums.shape[1]), FULL)


def attend_back_kernel(groups, side, causal, planes, ways, norm_row, finish, meta, upstream_ref, state, gain, shift, slots, gates, route, lse, att, mixed, *rest):
    kv_refs, rest = rest[:planes], rest[planes:]
    (query_proj, out_proj, router, result, kept, sent, router_grad, sums), rest = rest[:8], rest[8:]
    d_kv_out, scratch = rest[:planes], rest[planes:]
    (grad,) = scratch
    r, z = meta[0], meta[1]
    experts = router.shape[1]
    head = slots.shape[0]
    upstream = upstream_ref[...]
    branch_grad = upstream.astype(LOW)
    normal, inverse = normalise(state[...].astype(FULL))
    h = (normal * gain[norm_row : norm_row + 1] + shift[norm_row : norm_row + 1]).astype(LOW)
    part = h.shape[0] // groups
    lanes = 2 * part
    d_mixed = mm_nt(out_proj[...], branch_grad)
    out_grad = mm(mixed[...], branch_grad)
    query_columns, logit_columns = [], []
    for g in range(groups):
        here = slice(g * lanes, (g + 1) * lanes)
        ids = route[:, here]
        gate = gates[:, here]
        attended = att[:, here]
        mine = d_mixed[:, g * part : (g + 1) * part]
        spread = jnp.concatenate([mine, mine], 1)
        slot_grad = jnp.zeros((head, lanes), FULL)
        for e in range(experts):
            slot_grad = jnp.where(ids == e, spread[e * head : (e + 1) * head], slot_grad)
        gate_grad = jnp.sum(attended * slot_grad, 0, keepdims=True)
        weighted = gate * gate_grad
        both = weighted[:, :part] + weighted[:, part:]
        chosen_grad = gate * (gate_grad - jnp.concatenate([both, both], 1))
        att_grad = (gate * slot_grad).astype(LOW)
        inner = jnp.sum(att_grad.astype(FULL) * attended, 0, keepdims=True)
        q = slots[:, here]
        zeros = jnp.zeros_like(q)
        kv = jnp.concatenate([ref[g * part : (g + 1) * part, :] for ref in kv_refs], 0)
        scores = mm(kv, jnp.concatenate([q, zeros], 0))
        ok = allowed_keys(scores.shape, z, part, planes, meta[2 + 2 * side + g], causal)
        probs = jnp.exp(jnp.where(ok, scores, -1e30) - lse[:, here])
        probs_grad = mm(kv, jnp.concatenate([zeros, att_grad], 0))
        score_grad = (probs * (probs_grad - inner)).astype(LOW)
        d_kv = mm(score_grad, jnp.concatenate([q, zeros], 0).T) + mm(
            probs.astype(LOW), jnp.concatenate([zeros, att_grad], 0).T
        )
        for k in range(planes):
            d_kv_out[k][g * part : (g + 1) * part, :] = d_kv[k * part : (k + 1) * part].astype(LOW)
        slot_query_grad = mm(kv.T, score_grad)[:head] * (float(head) ** -0.5)
        rows = []
        for e in range(experts):
            first = jnp.where(ids[:, :part] == e, slot_query_grad[:, :part], 0.0)
            rows.append(jnp.where(ids[:, part:] == e, slot_query_grad[:, part:], first).astype(LOW))
        query_columns.append(jnp.concatenate(rows, 0))
        expert = lax.broadcasted_iota(jnp.int32, (experts, part), 0)
        first = jnp.where(ids[:, :part] == expert, chosen_grad[:, :part], 0.0)
        logit_columns.append(jnp.where(ids[:, part:] == expert, chosen_grad[:, part:], first))
    query_grad_rows = jnp.concatenate(query_columns, 1)
    logit_grad = jnp.concatenate(logit_columns, 1)
    high, low = split_low(logit_grad)
    router_grad[...] = mm(high, h) + mm(low, h)
    d_h = mm_nt(query_grad_rows.T, query_proj[...])
    d_h = d_h + mm_nt(high.T, router[...]) + mm_nt(low.T, router[...])
    rows_each = out_grad.shape[0] // ways
    for half in range(2):
        grad[...] = mm(query_grad_rows, h) if half == 0 else out_grad
        for j in range(ways):
            block = grad[pl.ds(pl.multiple_of((r ^ j) * rows_each, rows_each), rows_each), :].astype(LOW)
            place = sent if j & 1 else kept
            place[j // 2, half * rows_each : (half + 1) * rows_each, :] = block
    if finish:
        result[...] = upstream_ref[...] + norm_back(d_h, normal, inverse, gain[norm_row : norm_row + 1])
        sums[0:1] = jnp.sum(d_h * normal, 0, keepdims=True)
        sums[1:2] = jnp.sum(d_h, 0, keepdims=True)
        sums[2:8] = jnp.zeros((6, sums.shape[1]), FULL)
    else:
        result[...] = d_h
        sums[...] = jnp.zeros_like(sums)


def finish_kernel(planes, norm_row, meta, partial, upstream, state, gain, shift, keyval, *rest):
    blocks, (result, keyval_grad, sums) = rest[:planes], rest[planes:]
    d_kv = total_of(blocks)
    normal, inverse = normalise(state[...].astype(FULL))
    h = (normal * gain[norm_row : norm_row + 1] + shift[norm_row : norm_row + 1]).astype(LOW)
    keyval_grad[...] = mm(d_kv.T, h)
    d_h = partial[...] + mm_nt(d_kv, keyval[...])
    result[...] = upstream[...] + norm_back(d_h, normal, inverse, gain[norm_row : norm_row + 1])
    sums[0:1] = jnp.sum(d_h * normal, 0, keepdims=True)
    sums[1:2] = jnp.sum(d_h, 0, keepdims=True)
    sums[2:8] = jnp.zeros((6, sums.shape[1]), FULL)


def swap(values, axis_name, bits):
    size = lax.axis_size(axis_name)
    return lax.ppermute(values, axis_name, [(i, i ^ bits) for i in range(size)])


def ways_of():
    return min(lax.axis_size("rows"), 8)


def other_bits():
    size, ways = lax.axis_size("rows"), ways_of()
    bits = []
    while ways < size:
        bits.append(ways)
        ways *= 2
    return bits


def add_over(values, axis_name, bits):
    for bit in bits:
        values = values.astype(FULL) + swap(values, axis_name, bit).astype(FULL)
        values = values.astype(LOW)
    return values


def plane_bits():
    size, bits = lax.axis_size("ffn"), []
    while (1 << len(bits)) < size:
        bits.append(1 << len(bits))
    return bits


def gather_planes(values):
    return [values] + [swap(values, "ffn", k) for k in range(1, lax.axis_size("ffn"))]


def gather_weights(first, second, bias, device):
    ways = ways_of()
    rows = first.shape[0] // ways
    start = (device[0] % ways) * rows
    mine = jnp.concatenate(
        [
            lax.dynamic_slice_in_dim(first, start, rows, 0),
            lax.dynamic_slice_in_dim(second, start, rows, 0),
            jnp.broadcast_to(bias[None], (16,) + bias.shape),
        ]
    )
    crossed = [swap(mine, "ffn", k) for k in range(1, lax.axis_size("ffn"))]
    all_bias = jnp.stack([bias] + [part[2 * rows] for part in crossed])[:, None].astype(FULL)
    own = jnp.stack([part[: 2 * rows] for part in crossed])
    pieces = []
    for even in range(0, ways, 2):
        piece = own if even == 0 else swap(own, "rows", even)
        pieces += [piece, swap(piece, "rows", 1)]
    return all_bias, pieces


def scatter_rows(kept, sent):
    pairs = (kept.astype(FULL) + swap(sent, "rows", 1).astype(FULL)).astype(LOW)
    total = pairs[0].astype(FULL)
    for half in range(1, pairs.shape[0]):
        total = total + swap(pairs[half], "rows", 2 * half).astype(FULL)
    return total


def gather_rows(own):
    ways = ways_of()
    even = jnp.stack([own] + [swap(own, "rows", k) for k in range(2, ways, 2)])
    return even, swap(even, "rows", 1)


def reduce_feed(kept, sent):
    own = scatter_rows(kept, sent)
    total = own[0]
    low = own.astype(LOW)
    for k in range(1, own.shape[0]):
        total = total + swap(low[k], "ffn", k).astype(FULL)
    total = add_over(total.astype(LOW), "rows", other_bits())
    return gather_rows(total)


def reduce_attention(kept, sent):
    own = scatter_rows(kept, sent).astype(LOW)
    own = add_over(own, "ffn", plane_bits())
    own = add_over(own, "rows", other_bits())
    return gather_rows(own)


def add_small(values):
    for axis_name in ("rows", "ffn"):
        bit = 1
        while bit < lax.axis_size(axis_name):
            values = values + swap(values, axis_name, bit)
            bit *= 2
    return values


def add_tail(values):
    bits, bit = [], 1
    while bit < lax.axis_size("rows"):
        bits.append(bit)
        bit *= 2
    return add_over(add_over(values, "rows", bits), "ffn", plane_bits())


def place_kernel(layers, attentions, meta, *refs):
    feeds, refs = refs[: 2 * layers], refs[2 * layers :]
    moas, refs = refs[: 2 * attentions], refs[2 * attentions :]
    first_out, second_out, query_out, out_out, scratch = refs
    r = meta[0]
    for layer in range(layers):
        ways = 2 * feeds[2 * layer].shape[0]
        rows = feeds[2 * layer].shape[1] // 2
        for j in range(ways):
            piece = feeds[2 * layer + (j & 1)]
            at = pl.ds(pl.multiple_of(((r ^ j) & (ways - 1)) * rows, rows), rows)
            first_out[layer, at, :] = piece[j // 2, :rows].astype(FULL)
            scratch[at, :] = piece[j // 2, rows:].astype(FULL)
        second_out[layer] = scratch[...].T
    for item in range(attentions):
        ways = 2 * moas[2 * item].shape[0]
        rows = moas[2 * item].shape[1] // 2
        for j in range(ways):
            piece = moas[2 * item + (j & 1)]
            at = pl.ds(pl.multiple_of(((r ^ j) & (ways - 1)) * rows, rows), rows)
            scratch[at, :] = piece[j // 2, :rows].astype(FULL)
            out_out[item, at, :] = piece[j // 2, rows:].astype(FULL)
        query_out[item] = scratch[...].T


MICRO = 1 << 30


def body(
    source,
    target,
    cotangent,
    source_lengths,
    target_lengths,
    routes,
    norm_gain,
    norm_shift,
    moa_router,
    moa_query,
    moa_keyval,
    moa_out,
    ffn_in,
    ffn_in_bias,
    ffn_out,
    ffn_out_bias,
):
    groups, row_count, width = source.shape
    tokens = groups * row_count
    planes = lax.axis_size("ffn")
    ways = ways_of()
    experts = moa_router.shape[2]
    both = moa_keyval.shape[2]
    head = both // 2
    hidden = ffn_in.shape[2]
    slots_all = 2 * tokens
    row_index, plane_index = lax.axis_index("rows"), lax.axis_index("ffn")
    device = (row_index, plane_index)
    meta = jnp.concatenate(
        [
            jnp.stack([row_index % ways, plane_index]).astype(jnp.int32),
            source_lengths,
            target_lengths,
        ]
    )
    flat = lambda values: values.reshape(tokens, width)
    source, target, cotangent = flat(source), flat(target), flat(cotangent)
    route_rows = jnp.swapaxes(routes, 2, 3).reshape(3, 1, slots_all)
    router_t = jnp.swapaxes(moa_router, 1, 2)
    second_weights = [ffn_out[layer].T for layer in range(2)]

    bias_zero, pieces_zero = gather_weights(ffn_in[0], second_weights[0], ffn_in_bias[0], device)
    rows_like = like((tokens, width), FULL)
    low_like = like((tokens, width), LOW)
    kv_like = like((tokens, both), LOW)
    h_source, h_target, kv_source, kv_target = call(
        prepare_kernel,
        [low_like, low_like, kv_like, kv_like],
        (meta, source, target, norm_gain, norm_shift, moa_keyval),
        flops=3 * MICRO,
        name="prepare",
    )
    kv_zero = gather_planes(kv_source)
    kv_one = gather_planes(kv_target)
    bias_one, pieces_one = gather_weights(ffn_in[1], second_weights[1], ffn_in_bias[1], device)
    slot_like = [like((head, slots_all), LOW), like((1, slots_all), FULL)]
    slots_zero, slots_one = (
        call(
            functools.partial(queries_kernel, groups),
            slot_like,
            (meta, h, route_rows[j], moa_query[j], router_t[j]),
            flops=2 * MICRO,
            name="queries",
        )
        for j, h in ((0, h_source), (1, h_target))
    )
    kept_like = [
        rows_like,
        like((1, slots_all), FULL),
        like((head, slots_all), FULL),
        like((experts * head, tokens), LOW),
    ]

    def attention(j, side, causal, resid, slots, kv_blocks, following):
        extra, more = (), []
        if following:
            extra = (norm_gain, norm_shift, route_rows[2], moa_query[2], router_t[2])
            more = slot_like
        return call(
            functools.partial(attend_kernel, groups, side, causal, planes, following),
            kept_like + more,
            (meta, resid, *slots, route_rows[j], *kv_blocks, moa_out[j], *extra),
            flops=5 * MICRO,
            name="attend",
        )

    middle, *saved_zero = attention(0, 0, False, source, slots_zero, kv_zero, False)
    weight_scratch = [pltpu.VMEM((planes, width, hidden), LOW)] * 2
    memory, memory_low, kv_memory = call(
        functools.partial(feed_forward_kernel, ways),
        [rows_like, low_like, kv_like],
        (meta, middle, norm_gain, norm_shift, ffn_out_bias, bias_zero, moa_keyval[2])
        + (ffn_in[0], second_weights[0], *pieces_zero),
        weight_scratch,
        flops=8 * MICRO,
        name="encoder_feed",
    )
    kv_two = gather_planes(kv_memory)
    first_state, *saved_one, next_slots, next_gates = attention(
        1, 1, True, target, slots_one, kv_one, True
    )
    slots_two = (next_slots, next_gates)
    second_state, *saved_two = attention(2, 0, False, first_state, slots_two, kv_two, False)

    back_scratch = weight_scratch + [pltpu.VMEM((width, hidden), FULL), pltpu.VMEM((tokens, width), FULL)]
    feed_like = [like((ways // 2, planes, 2 * width // ways, hidden), LOW)] * 2
    feed_like += [like((planes, 1, hidden), FULL), like((8, width), FULL)]
    decoded, second_grad, kept, sent, bias_grad_one, sums_four = call(
        functools.partial(decoder_feed_kernel, ways, groups),
        [rows_like, rows_like] + feed_like,
        (meta, second_state, cotangent, norm_gain, norm_shift, ffn_out_bias, bias_one)
        + (ffn_in[1], second_weights[1], *pieces_one),
        back_scratch,
        flops=15 * MICRO,
        name="decoder_feed",
    )
    feed_one = reduce_feed(kept, sent)

    moa_like = [like((ways // 2, 2 * width // ways, width), LOW)] * 2
    moa_like += [like((experts, width), FULL), like((8, width), FULL)] + [kv_like] * planes

    def attention_back(j, side, causal, norm_row, finish, upstream, state, slots, saved, kv_blocks):
        return call(
            functools.partial(
                attend_back_kernel, groups, side, causal, planes, ways, norm_row, finish
            ),
            [rows_like] + moa_like,
            (meta, upstream, state, norm_gain, norm_shift, *slots, route_rows[j], *saved)
            + (*kv_blocks, moa_query[j], moa_out[j], moa_router[j]),
            [pltpu.VMEM((width, width), FULL)],
            flops=8 * MICRO,
            name="attend_back",
        )

    def home(blocks):
        return [blocks[0]] + [swap(blocks[k], "ffn", k) for k in range(1, planes)]

    first_grad, kept_two, sent_two, router_two, sums_three, *d_kv_two = attention_back(
        2, 0, False, 3, True, second_grad, first_state, slots_two, saved_two, kv_two
    )
    d_kv_two = home(d_kv_two)
    self_grad, kept_one, sent_one, router_one, unused, *d_kv_one = attention_back(
        1, 1, True, 2, False, first_grad, target, slots_one, saved_one, kv_one
    )
    d_kv_one = home(d_kv_one)
    memory_grad, middle_grad, keyval_two, kept, sent, bias_grad_zero, sums_one = call(
        functools.partial(encoder_feed_kernel, ways, planes),
        [rows_like, rows_like, like((both, width), FULL)] + feed_like,
        (meta, middle, memory_low, norm_gain, norm_shift, bias_zero, moa_keyval[2], *d_kv_two)
        + (ffn_in[0], second_weights[0], *pieces_zero),
        back_scratch,
        flops=15 * MICRO,
        name="encoder_feed_back",
    )
    feed_zero = reduce_feed(kept, sent)
    moa_later = reduce_attention(
        jnp.concatenate([kept_two, kept_one], 1), jnp.concatenate([sent_two, sent_one], 1)
    )
    encoder_grad, kept_zero, sent_zero, router_zero, unused, *d_kv_zero = attention_back(
        0, 0, False, 0, False, middle_grad, source, slots_zero, saved_zero, kv_zero
    )
    d_kv_zero = home(d_kv_zero)
    moa_first = reduce_attention(kept_zero, sent_zero)

    def finish(j, norm_row, partial, upstream, state, blocks):
        return call(
            functools.partial(finish_kernel, planes, norm_row),
            [rows_like, like((both, width), FULL), like((8, width), FULL)],
            (meta, partial, upstream, state, norm_gain, norm_shift, moa_keyval[j], *blocks),
            flops=4 * MICRO,
            name="finish",
        )

    target_grad, keyval_one, sums_two = finish(1, 2, self_grad, first_grad, target, d_kv_one)
    source_grad, keyval_zero, sums_zero = finish(
        0, 0, encoder_grad, middle_grad, source, d_kv_zero
    )

    position = plane_index * row_count + jnp.arange(row_count, dtype=jnp.int32)
    source_rows = position[None, :] < source_lengths[:, None]
    target_rows = position[None, :] < target_lengths[:, None]
    valid = jnp.stack([source_rows, target_rows, target_rows])
    hits = (routes[..., None] == jnp.arange(experts, dtype=jnp.int32)) & valid[..., None, None]
    counted = jnp.sum(jnp.where(hits, 1.0, 0.0), (1, 2, 3)).reshape(-1)
    small = jnp.concatenate(
        [
            sums_one[:3],
            sums_two[:2],
            sums_three[:2],
            sums_four[:3],
            router_zero,
            router_one,
            router_two,
            bias_grad_zero[:, 0],
            bias_grad_one[:, 0],
            jnp.zeros((1, width), FULL).at[0, : counted.shape[0]].set(counted),
        ]
    )
    small = add_small(small)
    tail = jnp.concatenate([keyval_zero, keyval_one, keyval_two, sums_zero, sums_zero])
    tail = add_tail(tail.astype(LOW)).astype(FULL)

    moa_parts = []
    for pair in (
        moa_first,
        [part[:, 2 * width // ways :] for part in moa_later],
        [part[:, : 2 * width // ways] for part in moa_later],
    ):
        moa_parts += list(pair)
    first_grads, second_grads, query_grads, out_grads = call(
        functools.partial(place_kernel, 2, 3),
        [like((2, width, hidden), FULL), like((2, hidden, width), FULL)]
        + [like((3, width, experts * head), FULL), like((3, experts * head, width), FULL)],
        (meta, *feed_zero, *feed_one, *moa_parts),
        [pltpu.VMEM((width, width), FULL)],
        flops=4 * MICRO,
        name="place",
    )
    keyval_grads = jnp.swapaxes(tail[: 3 * both].reshape(3, both, width), 1, 2)
    gain_zero, shift_zero = tail[3 * both], tail[3 * both + 1]
    gain_one, shift_one, out_zero, gain_two, shift_two = (small[i] for i in range(5))
    gain_three, shift_three, gain_four, shift_four, out_one = (small[i] for i in range(5, 10))
    routers = jnp.swapaxes(small[10 : 10 + 3 * experts].reshape(3, experts, width), 1, 2)
    rest = small[10 + 3 * experts :]
    bias_grads = lax.dynamic_index_in_dim(
        rest[: 2 * planes].reshape(2, planes, hidden), plane_index, 1, keepdims=False
    )
    counts = rest[-1, : 3 * experts].reshape(3, experts).astype(jnp.int32)
    whole = lambda values: values.reshape(groups, row_count, width)
    return (
        whole(memory),
        whole(decoded),
        whole(source_grad),
        whole(target_grad),
        whole(memory_grad),
        jnp.stack([gain_zero, gain_one, gain_two, gain_three]),
        jnp.stack([shift_zero, shift_one, shift_two, shift_three]),
        jnp.stack([gain_four, shift_four]),
        routers,
        query_grads,
        keyval_grads,
        out_grads,
        first_grads,
        bias_grads,
        second_grads,
        jnp.stack([out_zero, out_one]),
        counts,
    )


def solution(mesh):
    in_specs = (
        P("rows", "ffn", None),
        P("rows", "ffn", None),
        P("rows", "ffn", None),
        P("rows"),
        P("rows"),
        P(None, "rows", "ffn", None),
        P(),
        P(),
        P(),
        P(),
        P(),
        P(),
        P(None, None, "ffn"),
        P(None, "ffn"),
        P(None, "ffn", None),
        P(),
    )
    out_specs = (
        P("rows", "ffn", None),
        P("rows", "ffn", None),
        P("rows", "ffn", None),
        P("rows", "ffn", None),
        P("rows", "ffn", None),
        P(),
        P(),
        P(),
        P(),
        P(),
        P(),
        P(),
        P(None, None, "ffn"),
        P(None, "ffn"),
        P(None, "ffn", None),
        P(),
        P(),
    )
    return jax.shard_map(body, mesh=mesh, in_specs=in_specs, out_specs=out_specs, check_vma=False)
```

time: 1120 us -> 411 us (0.37)
  waiting for transfers between devices: 753 us -> 96.4 us
  starting transfers between devices: 1.58 us -> 149 us
  matrix products: 129 us -> 0 us
  Pallas kernels: 0 us -> 103 us
  blocking collectives: 64 us -> 0 us
  other arithmetic: 67.2 us -> 21.6 us
  local copies, waits for them, and re-layouts: 80.2 us -> 35.9 us
  between operations: 16.5 us -> 2.19 us
    psum x3 -> x0, waiting for transfers between devices: 344 us -> none  [the longest x2 263 us: body(): lax.psum((jnp.stack([gain_zero, gain_one, gain_two, gain_three, gain_four...]
    reduce_scatter x7 -> x0, waiting for transfers between devices: 237 us -> none  [the longest x2 113 us: feed_backward(): lax.psum_scatter(flat_grad.reshape(groups, -1, model_width), 'ffn', scatt...]
    all_gather x4 -> x0, waiting for transfers between devices: 171 us -> none  [the longest x2 94.8 us: feed_forward(): gathered = lax.all_gather(normed, 'ffn', axis=1, tiled=True)]
    ppermute x0 -> x90, starting transfers between devices: none -> 149 us  [swap(): return lax.ppermute(values, axis_name, [(i, i ^ bits) for i in range(size)])]
    dot_general x66 -> x0, matrix products: 129 us -> none  [the longest x2 15 us: feed_backward(): jnp.einsum('nd,fd->nf', rows_grad, used_out, preferred_element_type=jnp.f...]
    pallas_call x0 -> x15, Pallas kernels: none -> 103 us  [call(): pl.pallas_call(body, out_shape=out_shape, in_specs=specs, out_specs=jax.t...]
    ppermute x0 -> x90, waiting for transfers between devices: none -> 96.4 us  [swap(): return lax.ppermute(values, axis_name, [(i, i ^ bits) for i in range(size)])]
    all_gather x3 -> x0, blocking collectives: 49.8 us -> none  [attend_forward(): gathered = lax.all_gather(key_value, 'ffn', axis=1, tiled=True)]
  transfers between devices with their start and end apart: 14 -> 90, of which waited for: 12 -> 24; matrix products, arithmetic and copies ran while one was open for 15% -> 12% of each run, Pallas kernels for 0% -> 9%
where the time goes in v2:
time: 411 us; the launch traced here: 408 us
  starting transfers between devices  149 us (36%)
  Pallas kernels  103 us (25%)
  waiting for transfers between devices  96.4 us (23%)
  local copies, waits for them, and re-layouts  35.9 us (9%)
  other arithmetic  21.6 us (5%)
    ppermute x90, starting transfers between devices, swap(): return lax.ppermute(values, axis_name, [(i, i ^ bits) for i in range(size)])  149 us
    pallas_call x15, Pallas kernels, call(): pl.pallas_call(body, out_shape=out_shape, in_specs=specs, out_specs=jax.t...  103 us
    ppermute x90, waiting for transfers between devices, swap(): return lax.ppermute(values, axis_name, [(i, i ^ bits) for i in range(size)])  96.4 us
    unnamed x142, local copies, waits for them, and re-layouts  9.54 us
  transfers between devices with their start and end apart: 90, of which 24 were waited for; matrix products, arithmetic and copies ran while one was open for 12% of the time, Pallas kernels for 9%

profile of v2, /device:TPU:1, one launch (start us, length us, event | category | flops | bytes accessed | tf_op | source)
XLA Modules:
  0.0 407.6 jit_solution(12849433370681118510)
XLA Ops:
  1.9 3.3 prepare.1
  5.2 2.1 collective-permute-start.13
  7.3 2.3 collective-permute-start.14
  9.8 3.4 collective-permute-start.2
  21.2 3.1 slice_bitcast_fusion.8
  24.3 2.4 queries.3
  26.7 2.4 queries.2
  33.2 3.2 collective-permute-start.5
  36.5 5.0 %attend.3 = (f32[512,512]{1,0:T(8,128)}, f32[1,1024]{1,0:T(1,128)}, f32[64,1024]{1,0:T(8,128)}, bf16[512,512]{1,0:T(8,128)(2,1)}) custom-call(s32[6]{0:T(128)} %pad_add_fusion.1.meta, bf16[512,512]{1,0:T(8,128)(2,1)} %bitcast.233, bf16[64,1024]{1,0:T(8,128)(2,1)} %get-tuple-element.103.slots, f32[1,1024]{1,0:T(1,128)} %get-tuple-element.104.gates, ...), custom_call_target="tpu_custom_call" | custom-call | flops 5368709120 | bytes 4194304 | tf_op jit(solution)/shard_map/attend/pallas_call | solution.py:57
  41.9 3.2 collective-permute-start.21
  45.7 5.6 %attend.4 = (f32[512,512]{1,0:T(8,128)}, f32[1,1024]{1,0:T(1,128)}, f32[64,1024]{1,0:T(8,128)}, bf16[512,512]{1,0:T(8,128)(2,1)}, bf16[64,1024]{1,0:T(8,128)(2,1)}, /*index=5*/f32[1,1024]{1,0:T(1,128)}) custom-call(s32[6]{0:T(128)} %pad_add_fusion.1.meta, bf16[512,512]{1,0:T(8,128)(2,1)} %bitcast.229, bf16[64,1024]{1,0:T(8,128)(2,1)} %get-tuple-element.109.slots, ...), custom_call_target="tpu_custom_call" | custom-call | flops 5368709120 | bytes 4194304 | tf_op jit(solution)/shard_map/attend/pallas_call | solution.py:57
  51.4 3.5 collective-permute-done.4
  57.8 5.1 %collective-permute-done.20 = bf16[144,512]{1,0:T(8,128)(2,1)S(1)} collective-permute-done((bf16[144,512]{1,0:T(8,128)(2,1)S(1)}, bf16[144,512]{1,0:T(8,128)(2,1)S(1)}, u32[]{:S(2)}, u32[]{:S(2)}) %collective-permute-start.20) | collective-permute-done | bytes 147488 | tf_op jit(solution)/shard_map/ppermute | solution.py:387
  62.9 3.4 collective-permute-start.6
  68.3 6.2 %collective-permute-start.10 = (bf16[3,128,512]{2,1,0:T(8,128)(2,1)S(1)}, bf16[3,128,512]{2,1,0:T(8,128)(2,1)S(1)}, u32[]{:S(2)}, u32[]{:S(2)}) collective-permute-start(bf16[3,128,512]{2,1,0:T(8,128)(2,1)S(1)} %collective-permute-done.9.rest_4_.rest_10_), channel_id=1, source_target_pairs={{0,4},{4,0},{8,12},{12,8},{16,20},{20,16},{24,28},{28,24},{1,5},{5... | collective-permute-start | bytes 1179656 | tf_op jit(solution)/shard_map/ppermute | solution.py:387
  75.6 5.0 %collective-permute-start.8 = (bf16[3,128,512]{2,1,0:T(8,128)(2,1)S(1)}, bf16[3,128,512]{2,1,0:T(8,128)(2,1)S(1)}, u32[]{:S(2)}, u32[]{:S(2)}) collective-permute-start(bf16[3,128,512]{2,1,0:T(8,128)(2,1)S(1)} %collective-permute-done.7.rest_2_.rest_8_), channel_id=1, source_target_pairs={{0,4},{4,0},{8,12},{12,8},{16,20},{20,16},{24,28},{28,24},{1,5},{5... | collective-permute-start | bytes 1179656 | tf_op jit(solution)/shard_map/ppermute | solution.py:387
  84.0 8.5 %encoder_feed.1 = (f32[512,512]{1,0:T(8,128)}, bf16[512,512]{1,0:T(8,128)(2,1)}, bf16[512,128]{1,0:T(8,128)(2,1)}) custom-call(s32[6]{0:T(128)} %pad_add_fusion.1.meta, f32[512,512]{1,0:T(8,128)} %get-tuple-element.106.state.state_in, f32[5,512]{1,0:T(8,128)} %gain.17, f32[5,512]{1,0:T(8,128)} %shift.17, bf16[2,512]{1,0:T(2,128)(2,1)} %out_bias.3, ...), custom_call_target="tpu_custom_call" | custom-call | flops 8589934592 | bytes 4194304 | tf_op jit(solution)/shard_map/encoder_feed/pallas_call | solution.py:57
  92.5 3.2 collective-permute-start.17
  96.6 3.2 collective-permute-done.25.rest_4_
  101.2 5.9 %collective-permute-start.28 = (bf16[3,128,512]{2,1,0:T(8,128)(2,1)S(1)}, bf16[3,128,512]{2,1,0:T(8,128)(2,1)S(1)}, u32[]{:S(2)}, u32[]{:S(2)}) collective-permute-start(bf16[3,128,512]{2,1,0:T(8,128)(2,1)S(1)} %collective-permute-done.27.rest_6_), channel_id=1, source_target_pairs={{0,4},{4,0},{8,12},{12,8},{16,20},{20,16},{24,28},{28,24},{1,5},{5... | collective-permute-start | bytes 1179656 | tf_op jit(solution)/shard_map/ppermute | solution.py:387
  107.7 5.1 %attend.5 = (f32[512,512]{1,0:T(8,128)}, f32[1,1024]{1,0:T(1,128)}, f32[64,1024]{1,0:T(8,128)}, bf16[512,512]{1,0:T(8,128)(2,1)}) custom-call(s32[6]{0:T(128)} %pad_add_fusion.1.meta, f32[512,512]{1,0:T(8,128)} %get-tuple-element.112.resid.state, bf16[64,1024]{1,0:T(8,128)(2,1)} %get-tuple-element.113.slots, f32[1,1024]{1,0:T(1,128)} %get-tuple-element.114.gates, ...), custom_call_target="tpu_custom_call" | custom-call | flops 5368709120 | bytes 4194304 | tf_op jit(solution)/shard_map/attend/pallas_call | solution.py:57
  114.0 14.9 %decoder_feed.1 = (f32[512,512]{1,0:T(8,128)}, f32[512,512]{1,0:T(8,128)}, bf16[4,4,128,512]{3,2,1,0:T(8,128)(2,1)}, bf16[4,4,128,512]{3,2,1,0:T(8,128)(2,1)}, f32[4,1,512]{2,1,0:T(1,128)}, /*index=5*/f32[8,512]{1,0:T(8,128)}) custom-call(s32[6]{0:T(128)} %pad_add_fusion.1.meta, f32[512,512]{1,0:T(8,128)} %get-tuple-element.116.state_in, ...), custom_call_target="tpu_custom_call" | custom-call | flops 16106127360 | bytes 4194304 | tf_op jit(solution)/shard_map/decoder_feed/pallas_call | solution.py:57
  128.9 8.6 %attend_back.3 = (f32[512,512]{1,0:T(8,128)}, bf16[4,128,512]{2,1,0:T(8,128)(2,1)}, bf16[4,128,512]{2,1,0:T(8,128)(2,1)}, f32[8,512]{1,0:T(8,128)}, f32[8,512]{1...) custom-call(s32[6]{0:T(128)} %pad_add_fusion.1.meta, ...), custom_call_target="tpu_custom_call" | custom-call | flops 8589934592 | bytes 4194304 | tf_op jit(solution)/shard_map/attend_back/pallas_call | solution.py:57
  137.5 8.4 %attend_back.5 = (f32[512,512]{1,0:T(8,128)}, bf16[4,128,512]{2,1,0:T(8,128)(2,1)}, bf16[4,128,512]{2,1,0:T(8,128)(2,1)}, f32[8,512]{1,0:T(8,128)}, f32[8,512]{1...) custom-call(s32[6]{0:T(128)} %pad_add_fusion.1.meta, ...), custom_call_target="tpu_custom_call" | custom-call | flops 8589934592 | bytes 4194304 | tf_op jit(solution)/shard_map/attend_back/pallas_call | solution.py:57
  150.4 2.4 collective-permute-start.30
  157.1 4.0 finish.3
  161.8 6.7 %collective-permute-done.30.rest_2_ = bf16[512,128]{1,0:T(8,128)(2,1)S(1)} collective-permute-done((bf16[512,128]{1,0:T(8,128)(2,1)S(1)}, bf16[512,128]{1,0:T(8,128)(2,1)S(1)}, u32[]{:S(2)}, u32[]{:S(2)}) %collective-permute-start.30) | collective-permute-done | bytes 131104 | tf_op jit(solution)/shard_map/ppermute | solution.py:387
  169.2 14.5 %encoder_feed_back.1 = (f32[512,512]{1,0:T(8,128)}, f32[512,512]{1,0:T(8,128)}, f32[128,512]{1,0:T(8,128)}, bf16[4,4,128,512]{3,2,1,0:T(8,128)(2,1)}, bf16[4,4,1...) custom-call(s32[6]{0:T(128)} %pad_add_fusion.1.meta, ...), custom_call_target="tpu_custom_call" | custom-call | flops 16106127360 | bytes 4194304 | tf_op jit(solution)/shard_map/encoder_feed_back/pallas_call | solution.py:57
  185.1 8.3 %attend_back.4 = (f32[512,512]{1,0:T(8,128)}, bf16[4,128,512]{2,1,0:T(8,128)(2,1)}, bf16[4,128,512]{2,1,0:T(8,128)(2,1)}, f32[8,512]{1,0:T(8,128)}, f32[8,512]{1...) custom-call(s32[6]{0:T(128)} %pad_add_fusion.1.meta, ...), custom_call_target="tpu_custom_call" | custom-call | flops 8589934592 | bytes 4194304 | tf_op jit(solution)/shard_map/attend_back/pallas_call | solution.py:57
  194.9 3.6 collective-permute-start.43
  198.5 2.9 collective-permute-start.32
  205.3 2.1 collective-permute-done.32.rest_1_
  208.5 4.3 %collective-permute-done.34.rest_3_ = bf16[512,128]{1,0:T(8,128)(2,1)S(1)} collective-permute-done((bf16[512,128]{1,0:T(8,128)(2,1)}, bf16[512,128]{1,0:T(8,128)(2,1)S(1)}, u32[]{:S(2)}, u32[]{:S(2)}) %collective-permute-start.34) | collective-permute-done | bytes 131104 | tf_op jit(solution)/shard_map/ppermute | solution.py:387
  213.5 4.0 finish.2
  219.9 2.2 collective-permute-done.45
  222.2 3.2 collective-permute-start.46
  227.4 2.3 collective-permute-start.47
  229.7 2.1 collective-permute-done.47
  239.9 5.7 %collective-permute-start.38 = (bf16[400,512]{1,0:T(8,128)(2,1)S(1)}, bf16[400,512]{1,0:T(8,128)(2,1)S(1)}, u32[]{:S(2)}, u32[]{:S(2)}) collective-permute-start(bf16[400,512]{1,0:T(8,128)(2,1)S(1)} %constant_dynamic-update-slice_fusion), channel_id=1, source_target_pairs={{0,4},{4,0},{8,12},{12,8},{16,20},{20,16},{24,28},{28,24},{1,5},{5... | collective-permute-start | bytes 1228808 | tf_op jit(solution)/shard_map/ppermute | solution.py:387
  253.1 3.0 collective-permute-done.81
  256.2 4.2 %collective-permute-start.48 = (bf16[4,4,128,512]{3,2,1,0:T(8,128)(2,1)}, bf16[4,4,128,512]{3,2,1,0:T(8,128)(2,1)}, u32[]{:S(2)}, u32[]{:S(2)}) collective-permute-start(bf16[4,4,128,512]{3,2,1,0:T(8,128)(2,1)} %get-tuple-element.162), channel_id=1, source_target_pairs={{0,4},{4,0},{8,12},{12,8},{16,20},{20,16},{24,28},{28,24},{1,5},{5... | collective-permute-start | bytes 6291464 | tf_op jit(solution)/shard_map/ppermute | solution.py:387
  260.3 2.4 collective-permute-start.75
  264.0 6.6 %collective-permute-done.39 = bf16[400,512]{1,0:T(8,128)(2,1)S(1)} collective-permute-done((bf16[400,512]{1,0:T(8,128)(2,1)S(1)}, bf16[400,512]{1,0:T(8,128)(2,1)S(1)}, u32[]{:S(2)}, u32[]{:S(2)}) %collective-permute-start.39) | collective-permute-done | bytes 409632 | tf_op jit(solution)/shard_map/ppermute | solution.py:387
  270.7 2.3 collective-permute-start.40
  273.2 2.9 collective-permute-start.85
  276.1 4.8 %collective-permute-done.40 = bf16[400,512]{1,0:T(8,128)(2,1)S(1)} collective-permute-done((bf16[400,512]{1,0:T(8,128)(2,1)S(1)}, bf16[400,512]{1,0:T(8,128)(2,1)S(1)}, u32[]{:S(2)}, u32[]{:S(2)}) %collective-permute-start.40) | collective-permute-done | bytes 409632 | tf_op jit(solution)/shard_map/ppermute | solution.py:387
  289.9 2.5 collective-permute-start.86
  292.4 2.2 collective-permute-start.87
  296.1 1.9 collective-permute-start.88
  299.3 6.1 %collective-permute-done.88 = bf16[256,512]{1,0:T(8,128)(2,1)S(1)} collective-permute-done((bf16[256,512]{1,0:T(8,128)(2,1)S(1)}, bf16[256,512]{1,0:T(8,128)(2,1)S(1)}, u32[]{:S(2)}, u32[]{:S(2)}) %collective-permute-start.88) | collective-permute-done | bytes 262176 | tf_op jit(solution)/shard_map/ppermute | solution.py:387
  305.5 2.9 collective-permute-start.89
  313.1 2.3 add_convert_fusion.1
  315.5 7.7 %collective-permute-done.60 = bf16[4,128,512]{2,1,0:T(8,128)(2,1)S(1)} collective-permute-done((bf16[4,128,512]{2,1,0:T(8,128)(2,1)S(1)}, bf16[4,128,512]{2,1,0:T(8,128)(2,1)S(1)}, u32[]{:S(2)}, u32[]{:S(2)}) %collective-permute-start.60) | collective-permute-done | bytes 524320 | tf_op jit(solution)/shard_map/ppermute | solution.py:387
  325.9 9.4 %collective-permute-done.62 = bf16[4,128,512]{2,1,0:T(8,128)(2,1)S(1)} collective-permute-done((bf16[4,128,512]{2,1,0:T(8,128)(2,1)S(1)}, bf16[4,128,512]{2,1,0:T(8,128)(2,1)S(1)}, u32[]{:S(2)}, u32[]{:S(2)}) %collective-permute-start.62) | collective-permute-done | bytes 524320 | tf_op jit(solution)/shard_map/ppermute | solution.py:387
  337.1 8.6 %collective-permute-done.49 = bf16[4,128,512]{2,1,0:T(8,128)(2,1)S(1)} collective-permute-done((bf16[4,128,512]{2,1,0:T(8,128)(2,1)S(1)}, bf16[4,128,512]{2,1,0:T(8,128)(2,1)S(1)}, u32[]{:S(2)}, u32[]{:S(2)}) %collective-permute-start.49) | collective-permute-done | bytes 524320 | tf_op jit(solution)/shard_map/ppermute | solution.py:387
  346.2 3.3 collective-permute-start.64
  349.5 8.3 %collective-permute-done.51 = bf16[4,128,512]{2,1,0:T(8,128)(2,1)S(1)} collective-permute-done((bf16[4,128,512]{2,1,0:T(8,128)(2,1)S(1)}, bf16[4,128,512]{2,1,0:T(8,128)(2,1)S(1)}, u32[]{:S(2)}, u32[]{:S(2)}) %collective-permute-start.51) | collective-permute-done | bytes 524320 | tf_op jit(solution)/shard_map/ppermute | solution.py:387
  357.9 2.3 collective-permute-start.65
  363.5 2.9 collective-permute-start.54
  368.3 4.1 %collective-permute-done.53 = bf16[128,512]{1,0:T(8,128)(2,1)S(1)} collective-permute-done((bf16[128,512]{1,0:T(8,128)(2,1)S(1)}, bf16[128,512]{1,0:T(8,128)(2,1)S(1)}, u32[]{:S(2)}, u32[]{:S(2)}) %collective-permute-start.53) | collective-permute-done | bytes 131104 | tf_op jit(solution)/shard_map/ppermute | solution.py:387
  378.7 9.0 %collective-permute-start.79 = (bf16[4,128,512]{2,1,0:T(8,128)(2,1)}, bf16[4,128,512]{2,1,0:T(8,128)(2,1)}, u32[]{:S(2)}, u32[]{:S(2)}) collective-permute-start(bf16[4,128,512]{2,1,0:T(8,128)(2,1)} %pad_maximum_fusion.4.refs_4_), channel_id=1, source_target_pairs={{0,4},{4,0},{8,12},{12,8},{16,20},{20,16},{24,28},{28,24},{1,5},{5... | collective-permute-start | bytes 1572872 | tf_op jit(solution)/shard_map/ppermute | solution.py:387
  389.9 4.4 %collective-permute-start.58 = (bf16[4,128,512]{2,1,0:T(8,128)(2,1)}, bf16[4,128,512]{2,1,0:T(8,128)(2,1)}, u32[]{:S(2)}, u32[]{:S(2)}) collective-permute-start(bf16[4,128,512]{2,1,0:T(8,128)(2,1)} %pad_maximum_fusion.2.refs_0_), channel_id=1, source_target_pairs={{0,4},{4,0},{8,12},{12,8},{16,20},{20,16},{24,28},{28,24},{1,5},{5... | collective-permute-start | bytes 1572872 | tf_op jit(solution)/shard_map/ppermute | solution.py:387
  396.8 2.3 fusion.25
  399.1 8.1 %place.1 = (f32[2,512,512]{2,1,0:T(8,128)}, f32[2,512,512]{2,1,0:T(8,128)}, f32[3,512,512]{2,1,0:T(8,128)}, f32[3,512,512]{2,1,0:T(8,128)}) custom-call(s32[6]{0:T(128)} %pad_add_fusion.1.meta, bf16[4,128,512]{2,1,0:T(8,128)(2,1)} %pad_maximum_fusion.2.refs_0_, bf16[4,128,512]{2,1,0:T(8,128)(2,1)} %collective-permute-done.58.refs_1_, ...), custom_call_target="tpu_custom_call" | custom-call | flops 4294967296 | bytes 4194304 | tf_op jit(solution)/shard_map/place/pallas_call | solution.py:57
  (378 shorter events, 105.7 us)
Async XLA Ops:
  5.2 36.2 %collective-permute-start.13 = (bf16[512,128]{1,0:T(8,128)(2,1)}, bf16[512,128]{1,0:T(8,128)(2,1)}, u32[]{:S(2)}, u32[]{:S(2)}) collective-permute-start(bf16[512,128]{1,0:T(8,128)(2,1)} %get-tuple-element.111.rest_0_), channel_id=1, source_target_pairs={{0,1},{1,0},{2,3},{3,2},{4,5},{5,4},{6,7},{7,6},{8,9},{9,8},{10,11... | collective-permute-start | bytes 393224 | tf_op jit(solution)/shard_map/ppermute | solution.py:387
  7.3 34.6 %collective-permute-start.14 = (bf16[512,128]{1,0:T(8,128)(2,1)}, bf16[512,128]{1,0:T(8,128)(2,1)}, u32[]{:S(2)}, u32[]{:S(2)}) collective-permute-start(bf16[512,128]{1,0:T(8,128)(2,1)} %get-tuple-element.111.rest_0_), channel_id=1, source_target_pairs={{0,2},{1,3},{2,0},{3,1},{4,6},{5,7},{6,4},{7,5},{8,10},{9,11},{10,... | collective-permute-start | bytes 393224 | tf_op jit(solution)/shard_map/ppermute | solution.py:387
  9.6 23.5 %collective-permute-start = (bf16[512,128]{1,0:T(8,128)(2,1)}, bf16[512,128]{1,0:T(8,128)(2,1)S(1)}, u32[]{:S(2)}, u32[]{:S(2)}) collective-permute-start(bf16[512,128]{1,0:T(8,128)(2,1)} %get-tuple-element.105.rest_0_), channel_id=1, source_target_pairs={{0,1},{1,0},{2,3},{3,2},{4,5},{5,4},{6,7},{7,6},{8,9},{9,8},{10,11... | collective-permute-start | bytes 393224 | tf_op jit(solution)/shard_map/ppermute | solution.py:387
  9.8 23.4 %collective-permute-start.1 = (bf16[512,128]{1,0:T(8,128)(2,1)}, bf16[512,128]{1,0:T(8,128)(2,1)}, u32[]{:S(2)}, u32[]{:S(2)}) collective-permute-start(bf16[512,128]{1,0:T(8,128)(2,1)} %get-tuple-element.105.rest_0_), channel_id=1, source_target_pairs={{0,2},{1,3},{2,0},{3,1},{4,6},{5,7},{6,4},{7,5},{8,10},{9,11},{10,... | collective-permute-start | bytes 393224 | tf_op jit(solution)/shard_map/ppermute | solution.py:387
  9.8 26.6 %collective-permute-start.2 = (bf16[512,128]{1,0:T(8,128)(2,1)}, bf16[512,128]{1,0:T(8,128)(2,1)}, u32[]{:S(2)}, u32[]{:S(2)}) collective-permute-start(bf16[512,128]{1,0:T(8,128)(2,1)} %get-tuple-element.105.rest_0_), channel_id=1, source_target_pairs={{0,3},{1,2},{2,1},{3,0},{4,7},{5,6},{6,5},{7,4},{8,11},{9,10},{10,... | collective-permute-start | bytes 393224 | tf_op jit(solution)/shard_map/ppermute | solution.py:387
  33.1 11.9 %collective-permute-start.15 = (bf16[512,128]{1,0:T(8,128)(2,1)S(1)}, bf16[512,128]{1,0:T(8,128)(2,1)S(1)}, u32[]{:S(2)}, u32[]{:S(2)}) collective-permute-start(bf16[512,128]{1,0:T(8,128)(2,1)S(1)} %copy-done.50), channel_id=1, source_target_pairs={{0,3},{1,2},{2,1},{3,0},{4,7},{5,6},{6,5},{7,4},{8,11},{9,10},{10,... | collective-permute-start | bytes 393224 | tf_op jit(solution)/shard_map/ppermute | solution.py:387
  33.2 18.1 %collective-permute-start.5 = (bf16[144,512]{1,0:T(8,128)(2,1)S(1)}, bf16[144,512]{1,0:T(8,128)(2,1)S(1)}, u32[]{:S(2)}, u32[]{:S(2)}) collective-permute-start(bf16[144,512]{1,0:T(8,128)(2,1)S(1)} %pad_maximum_fusion.7), channel_id=1, source_target_pairs={{0,3},{1,2},{2,1},{3,0},{4,7},{5,6},{6,5},{7,4},{8,11},{9,10},{10,... | collective-permute-start | bytes 442376 | tf_op jit(solution)/shard_map/ppermute | solution.py:387
  36.5 18.5 %collective-permute-start.4 = (bf16[144,512]{1,0:T(8,128)(2,1)S(1)}, bf16[144,512]{1,0:T(8,128)(2,1)S(1)}, u32[]{:S(2)}, u32[]{:S(2)}) collective-permute-start(bf16[144,512]{1,0:T(8,128)(2,1)S(1)} %pad_maximum_fusion.7), channel_id=1, source_target_pairs={{0,2},{1,3},{2,0},{3,1},{4,6},{5,7},{6,4},{7,5},{8,10},{9,11},{10,... | collective-permute-start | bytes 442376 | tf_op jit(solution)/shard_map/ppermute | solution.py:387
  41.4 13.5 %collective-permute-start.3 = (bf16[144,512]{1,0:T(8,128)(2,1)S(1)}, bf16[144,512]{1,0:T(8,128)(2,1)S(1)}, u32[]{:S(2)}, u32[]{:S(2)}) collective-permute-start(bf16[144,512]{1,0:T(8,128)(2,1)S(1)} %pad_maximum_fusion.7), channel_id=1, source_target_pairs={{0,1},{1,0},{2,3},{3,2},{4,5},{5,4},{6,7},{7,6},{8,9},{9,8},{10,11... | collective-permute-start | bytes 442376 | tf_op jit(solution)/shard_map/ppermute | solution.py:387
  41.9 15.7 %collective-permute-start.21 = (bf16[144,512]{1,0:T(8,128)(2,1)S(1)}, bf16[144,512]{1,0:T(8,128)(2,1)S(1)}, u32[]{:S(2)}, u32[]{:S(2)}) collective-permute-start(bf16[144,512]{1,0:T(8,128)(2,1)S(1)} %pad_maximum_fusion.8), channel_id=1, source_target_pairs={{0,3},{1,2},{2,1},{3,0},{4,7},{5,6},{6,5},{7,4},{8,11},{9,10},{10,... | collective-permute-start | bytes 442376 | tf_op jit(solution)/shard_map/ppermute | solution.py:387
  45.1 17.8 %collective-permute-start.20 = (bf16[144,512]{1,0:T(8,128)(2,1)S(1)}, bf16[144,512]{1,0:T(8,128)(2,1)S(1)}, u32[]{:S(2)}, u32[]{:S(2)}) collective-permute-start(bf16[144,512]{1,0:T(8,128)(2,1)S(1)} %pad_maximum_fusion.8), channel_id=1, source_target_pairs={{0,2},{1,3},{2,0},{3,1},{4,6},{5,7},{6,4},{7,5},{8,10},{9,11},{10,... | collective-permute-start | bytes 442376 | tf_op jit(solution)/shard_map/ppermute | solution.py:387
  51.3 15.0 %collective-permute-start.19 = (bf16[144,512]{1,0:T(8,128)(2,1)S(1)}, bf16[144,512]{1,0:T(8,128)(2,1)S(1)}, u32[]{:S(2)}, u32[]{:S(2)}) collective-permute-start(bf16[144,512]{1,0:T(8,128)(2,1)S(1)} %pad_maximum_fusion.8), channel_id=1, source_target_pairs={{0,1},{1,0},{2,3},{3,2},{4,5},{5,4},{6,7},{7,6},{8,9},{9,8},{10,11... | collective-permute-start | bytes 442376 | tf_op jit(solution)/shard_map/ppermute | solution.py:387
  55.1 13.2 %collective-permute-start.9 = (bf16[3,128,512]{2,1,0:T(8,128)(2,1)S(1)}, bf16[3,128,512]{2,1,0:T(8,128)(2,1)S(1)}, u32[]{:S(2)}, u32[]{:S(2)}) collective-permute-start(bf16[3,128,512]{2,1,0:T(8,128)(2,1)S(1)} %pad_maximum_fusion.5.rest_0_.rest_6_), channel_id=1, source_target_pairs={{0,16},{4,20},{8,24},{12,28},{16,0},{20,4},{24,8},{28,12},{1,17},{... | collective-permute-start | bytes 1179656 | tf_op jit(solution)/shard_map/ppermute | solution.py:387
  56.4 18.2 %collective-permute-start.11 = (bf16[3,128,512]{2,1,0:T(8,128)(2,1)S(1)}, bf16[3,128,512]{2,1,0:T(8,128)(2,1)S(1)}, u32[]{:S(2)}, u32[]{:S(2)}) collective-permute-start(bf16[3,128,512]{2,1,0:T(8,128)(2,1)S(1)} %pad_maximum_fusion.5.rest_0_.rest_6_), channel_id=1, source_target_pairs={{0,24},{4,28},{8,16},{12,20},{16,8},{20,12},{24,0},{28,4},{1,25},{... | collective-permute-start | bytes 1179656 | tf_op jit(solution)/shard_map/ppermute | solution.py:387
  57.5 18.1 %collective-permute-start.7 = (bf16[3,128,512]{2,1,0:T(8,128)(2,1)S(1)}, bf16[3,128,512]{2,1,0:T(8,128)(2,1)S(1)}, u32[]{:S(2)}, u32[]{:S(2)}) collective-permute-start(bf16[3,128,512]{2,1,0:T(8,128)(2,1)S(1)} %pad_maximum_fusion.5.rest_0_.rest_6_), channel_id=1, source_target_pairs={{0,8},{4,12},{8,0},{12,4},{16,24},{20,28},{24,16},{28,20},{1,9},{5... | collective-permute-start | bytes 1179656 | tf_op jit(solution)/shard_map/ppermute | solution.py:387
  62.9 17.7 %collective-permute-start.6 = (bf16[3,128,512]{2,1,0:T(8,128)(2,1)S(1)}, bf16[3,128,512]{2,1,0:T(8,128)(2,1)S(1)}, u32[]{:S(2)}, u32[]{:S(2)}) collective-permute-start(bf16[3,128,512]{2,1,0:T(8,128)(2,1)S(1)} %pad_maximum_fusion.5.rest_0_.rest_6_), channel_id=1, source_target_pairs={{0,4},{4,0},{8,12},{12,8},{16,20},{20,16},{24,28},{28,24},{1,5},{5... | collective-permute-start | bytes 1179656 | tf_op jit(solution)/shard_map/ppermute | solution.py:387
  66.4 29.3 %collective-permute-start.23 = (bf16[3,128,512]{2,1,0:T(8,128)(2,1)S(1)}, bf16[3,128,512]{2,1,0:T(8,128)(2,1)S(1)}, u32[]{:S(2)}, u32[]{:S(2)}) collective-permute-start(bf16[3,128,512]{2,1,0:T(8,128)(2,1)S(1)} %pad_maximum_fusion.6.rest_0_), channel_id=1, source_target_pairs={{0,8},{4,12},{8,0},{12,4},{16,24},{20,28},{24,16},{28,20},{1,9},{5... | collective-permute-start | bytes 1179656 | tf_op jit(solution)/shard_map/ppermute | solution.py:387
  68.3 13.6 %collective-permute-start.10 = (bf16[3,128,512]{2,1,0:T(8,128)(2,1)S(1)}, bf16[3,128,512]{2,1,0:T(8,128)(2,1)S(1)}, u32[]{:S(2)}, u32[]{:S(2)}) collective-permute-start(bf16[3,128,512]{2,1,0:T(8,128)(2,1)S(1)} %collective-permute-done.9.rest_4_.rest_10_), channel_id=1, source_target_pairs={{0,4},{4,0},{8,12},{12,8},{16,20},{20,16},{24,28},{28,24},{1,5},{5... | collective-permute-start | bytes 1179656 | tf_op jit(solution)/shard_map/ppermute | solution.py:387
  80.6 19.2 %collective-permute-start.25 = (bf16[3,128,512]{2,1,0:T(8,128)(2,1)S(1)}, bf16[3,128,512]{2,1,0:T(8,128)(2,1)S(1)}, u32[]{:S(2)}, u32[]{:S(2)}) collective-permute-start(bf16[3,128,512]{2,1,0:T(8,128)(2,1)S(1)} %pad_maximum_fusion.6.rest_0_), channel_id=1, source_target_pairs={{0,16},{4,20},{8,24},{12,28},{16,0},{20,4},{24,8},{28,12},{1,17},{... | collective-permute-start | bytes 1179656 | tf_op jit(solution)/shard_map/ppermute | solution.py:387
  81.9 18.7 %collective-permute-start.27 = (bf16[3,128,512]{2,1,0:T(8,128)(2,1)S(1)}, bf16[3,128,512]{2,1,0:T(8,128)(2,1)S(1)}, u32[]{:S(2)}, u32[]{:S(2)}) collective-permute-start(bf16[3,128,512]{2,1,0:T(8,128)(2,1)S(1)} %pad_maximum_fusion.6.rest_0_), channel_id=1, source_target_pairs={{0,24},{4,28},{8,16},{12,20},{16,8},{20,12},{24,0},{28,4},{1,25},{... | collective-permute-start | bytes 1179656 | tf_op jit(solution)/shard_map/ppermute | solution.py:387
  95.7 11.4 %collective-permute-start.18 = (bf16[512,128]{1,0:T(8,128)(2,1)}, bf16[512,128]{1,0:T(8,128)(2,1)S(1)}, u32[]{:S(2)}, u32[]{:S(2)}) collective-permute-start(bf16[512,128]{1,0:T(8,128)(2,1)} %get-tuple-element.115.rest_0_), channel_id=1, source_target_pairs={{0,3},{1,2},{2,1},{3,0},{4,7},{5,6},{6,5},{7,4},{8,11},{9,10},{10,... | collective-permute-start | bytes 393224 | tf_op jit(solution)/shard_map/ppermute | solution.py:387
  99.9 13.0 %collective-permute-start.22 = (bf16[3,128,512]{2,1,0:T(8,128)(2,1)S(1)}, bf16[3,128,512]{2,1,0:T(8,128)(2,1)S(1)}, u32[]{:S(2)}, u32[]{:S(2)}) collective-permute-start(bf16[3,128,512]{2,1,0:T(8,128)(2,1)S(1)} %pad_maximum_fusion.6.rest_0_), channel_id=1, source_target_pairs={{0,4},{4,0},{8,12},{12,8},{16,20},{20,16},{24,28},{28,24},{1,5},{5... | collective-permute-start | bytes 1179656 | tf_op jit(solution)/shard_map/ppermute | solution.py:387
  100.7 12.2 %collective-permute-start.24 = (bf16[3,128,512]{2,1,0:T(8,128)(2,1)S(1)}, bf16[3,128,512]{2,1,0:T(8,128)(2,1)S(1)}, u32[]{:S(2)}, u32[]{:S(2)}) collective-permute-start(bf16[3,128,512]{2,1,0:T(8,128)(2,1)S(1)} %collective-permute-done.23.rest_2_), channel_id=1, source_target_pairs={{0,4},{4,0},{8,12},{12,8},{16,20},{20,16},{24,28},{28,24},{1,5},{5... | collective-permute-start | bytes 1179656 | tf_op jit(solution)/shard_map/ppermute | solution.py:387
  100.7 12.2 %collective-permute-start.26 = (bf16[3,128,512]{2,1,0:T(8,128)(2,1)S(1)}, bf16[3,128,512]{2,1,0:T(8,128)(2,1)S(1)}, u32[]{:S(2)}, u32[]{:S(2)}) collective-permute-start(bf16[3,128,512]{2,1,0:T(8,128)(2,1)S(1)} %collective-permute-done.25.rest_4_), channel_id=1, source_target_pairs={{0,4},{4,0},{8,12},{12,8},{16,20},{20,16},{24,28},{28,24},{1,5},{5... | collective-permute-start | bytes 1179656 | tf_op jit(solution)/shard_map/ppermute | solution.py:387
  101.2 11.8 %collective-permute-start.28 = (bf16[3,128,512]{2,1,0:T(8,128)(2,1)S(1)}, bf16[3,128,512]{2,1,0:T(8,128)(2,1)S(1)}, u32[]{:S(2)}, u32[]{:S(2)}) collective-permute-start(bf16[3,128,512]{2,1,0:T(8,128)(2,1)S(1)} %collective-permute-done.27.rest_6_), channel_id=1, source_target_pairs={{0,4},{4,0},{8,12},{12,8},{16,20},{20,16},{24,28},{28,24},{1,5},{5... | collective-permute-start | bytes 1179656 | tf_op jit(solution)/shard_map/ppermute | solution.py:387
  150.3 11.5 %collective-permute-start.29 = (bf16[512,128]{1,0:T(8,128)(2,1)S(1)}, bf16[512,128]{1,0:T(8,128)(2,1)S(1)}, u32[]{:S(2)}, u32[]{:S(2)}) collective-permute-start(bf16[512,128]{1,0:T(8,128)(2,1)S(1)} %copy-done.54), channel_id=1, source_target_pairs={{0,1},{1,0},{2,3},{3,2},{4,5},{5,4},{6,7},{7,6},{8,9},{9,8},{10,11... | collective-permute-start | bytes 393224 | tf_op jit(solution)/shard_map/ppermute | solution.py:387
  150.4 18.1 %collective-permute-start.30 = (bf16[512,128]{1,0:T(8,128)(2,1)S(1)}, bf16[512,128]{1,0:T(8,128)(2,1)S(1)}, u32[]{:S(2)}, u32[]{:S(2)}) collective-permute-start(bf16[512,128]{1,0:T(8,128)(2,1)S(1)} %copy-done.53), channel_id=1, source_target_pairs={{0,2},{1,3},{2,0},{3,1},{4,6},{5,7},{6,4},{7,5},{8,10},{9,11},{10,... | collective-permute-start | bytes 393224 | tf_op jit(solution)/shard_map/ppermute | solution.py:387
  153.6 14.9 %collective-permute-start.31 = (bf16[512,128]{1,0:T(8,128)(2,1)S(1)}, bf16[512,128]{1,0:T(8,128)(2,1)S(1)}, u32[]{:S(2)}, u32[]{:S(2)}) collective-permute-start(bf16[512,128]{1,0:T(8,128)(2,1)S(1)} %copy-done.52), channel_id=1, source_target_pairs={{0,3},{1,2},{2,1},{3,0},{4,7},{5,6},{6,5},{7,4},{8,11},{9,10},{10,... | collective-permute-start | bytes 393224 | tf_op jit(solution)/shard_map/ppermute | solution.py:387
  194.9 10.3 %collective-permute-start.43 = (f32[43,512]{1,0:T(8,128)S(1)}, f32[43,512]{1,0:T(8,128)S(1)}, u32[]{:S(2)}, u32[]{:S(2)}) collective-permute-start(f32[43,512]{1,0:T(8,128)S(1)} %concatenate.42), channel_id=1, source_target_pairs={{0,4},{4,0},{8,12},{12,8},{16,20},{20,16},{24,28},{28,24},{1,5},{5... | collective-permute-start | bytes 264200 | tf_op jit(solution)/shard_map/ppermute | solution.py:387
  202.2 10.7 %collective-permute-start.34 = (bf16[512,128]{1,0:T(8,128)(2,1)}, bf16[512,128]{1,0:T(8,128)(2,1)S(1)}, u32[]{:S(2)}, u32[]{:S(2)}) collective-permute-start(bf16[512,128]{1,0:T(8,128)(2,1)} %get-tuple-element.135), channel_id=1, source_target_pairs={{0,3},{1,2},{2,1},{3,0},{4,7},{5,6},{6,5},{7,4},{8,11},{9,10},{10,... | collective-permute-start | bytes 393224 | tf_op jit(solution)/shard_map/ppermute | solution.py:387
  204.5 43.4 %collective-permute-start.80 = (bf16[4,256,512]{2,1,0:T(8,128)(2,1)}, bf16[4,256,512]{2,1,0:T(8,128)(2,1)}, u32[]{:S(2)}, u32[]{:S(2)}) collective-permute-start(bf16[4,256,512]{2,1,0:T(8,128)(2,1)} %pad_maximum_fusion), channel_id=1, source_target_pairs={{0,4},{4,0},{8,12},{12,8},{16,20},{20,16},{24,28},{28,24},{1,5},{5... | collective-permute-start | bytes 3145736 | tf_op jit(solution)/shard_map/ppermute | solution.py:387
  205.3 104.2 %collective-permute-start.59 = (bf16[4,4,128,512]{3,2,1,0:T(8,128)(2,1)}, bf16[4,4,128,512]{3,2,1,0:T(8,128)(2,1)S(1)}, u32[]{:S(2)}, u32[]{:S(2)}) collective-permute-start(bf16[4,4,128,512]{3,2,1,0:T(8,128)(2,1)} %get-tuple-element.164), channel_id=1, source_target_pairs={{0,4},{4,0},{8,12},{12,8},{16,20},{20,16},{24,28},{28,24},{1,5},{5... | collective-permute-start | bytes 6291464 | tf_op jit(solution)/shard_map/ppermute | solution.py:387
  207.4 25.1 %collective-permute-start.70 = (bf16[4,128,512]{2,1,0:T(8,128)(2,1)}, bf16[4,128,512]{2,1,0:T(8,128)(2,1)S(1)}, u32[]{:S(2)}, u32[]{:S(2)}) collective-permute-start(bf16[4,128,512]{2,1,0:T(8,128)(2,1)} %get-tuple-element.166), channel_id=1, source_target_pairs={{0,4},{4,0},{8,12},{12,8},{16,20},{20,16},{24,28},{28,24},{1,5},{5... | collective-permute-start | bytes 1572872 | tf_op jit(solution)/shard_map/ppermute | solution.py:387
  208.2 10.4 %collective-permute-start.44 = (f32[43,512]{1,0:T(8,128)S(1)}, f32[43,512]{1,0:T(8,128)S(1)}, u32[]{:S(2)}, u32[]{:S(2)}) collective-permute-start(f32[43,512]{1,0:T(8,128)S(1)} %add.147), channel_id=1, source_target_pairs={{0,8},{4,12},{8,0},{12,4},{16,24},{20,28},{24,16},{28,20},{1,9},{5... | collective-permute-start | bytes 264200 | tf_op jit(solution)/shard_map/ppermute | solution.py:387
  233.8 11.8 %collective-permute-start.72 = (bf16[128,512]{1,0:T(8,128)(2,1)}, bf16[128,512]{1,0:T(8,128)(2,1)}, u32[]{:S(2)}, u32[]{:S(2)}) collective-permute-start(bf16[128,512]{1,0:T(8,128)(2,1)} %get-tuple-element.210), channel_id=1, source_target_pairs={{0,16},{4,20},{8,24},{12,28},{16,0},{20,4},{24,8},{28,12},{1,17},{... | collective-permute-start | bytes 393224 | tf_op jit(solution)/shard_map/ppermute | solution.py:387
  235.0 10.6 %collective-permute-start.73 = (bf16[128,512]{1,0:T(8,128)(2,1)}, bf16[128,512]{1,0:T(8,128)(2,1)}, u32[]{:S(2)}, u32[]{:S(2)}) collective-permute-start(bf16[128,512]{1,0:T(8,128)(2,1)} %get-tuple-element.209), channel_id=1, source_target_pairs={{0,24},{4,28},{8,16},{12,20},{16,8},{20,12},{24,0},{28,4},{1,25},{... | collective-permute-start | bytes 393224 | tf_op jit(solution)/shard_map/ppermute | solution.py:387
  239.9 11.6 %collective-permute-start.38 = (bf16[400,512]{1,0:T(8,128)(2,1)S(1)}, bf16[400,512]{1,0:T(8,128)(2,1)S(1)}, u32[]{:S(2)}, u32[]{:S(2)}) collective-permute-start(bf16[400,512]{1,0:T(8,128)(2,1)S(1)} %constant_dynamic-update-slice_fusion), channel_id=1, source_target_pairs={{0,4},{4,0},{8,12},{12,8},{16,20},{20,16},{24,28},{28,24},{1,5},{5... | collective-permute-start | bytes 1228808 | tf_op jit(solution)/shard_map/ppermute | solution.py:387
  250.2 10.1 %collective-permute-start.82 = (bf16[256,512]{1,0:T(8,128)(2,1)S(1)}, bf16[256,512]{1,0:T(8,128)(2,1)S(1)}, u32[]{:S(2)}, u32[]{:S(2)}) collective-permute-start(bf16[256,512]{1,0:T(8,128)(2,1)S(1)} %get-tuple-element.199), channel_id=1, source_target_pairs={{0,16},{4,20},{8,24},{12,28},{16,0},{20,4},{24,8},{28,12},{1,17},{... | collective-permute-start | bytes 786440 | tf_op jit(solution)/shard_map/ppermute | solution.py:387
  251.5 12.2 %collective-permute-start.83 = (bf16[256,512]{1,0:T(8,128)(2,1)S(1)}, bf16[256,512]{1,0:T(8,128)(2,1)S(1)}, u32[]{:S(2)}, u32[]{:S(2)}) collective-permute-start(bf16[256,512]{1,0:T(8,128)(2,1)S(1)} %get-tuple-element.198), channel_id=1, source_target_pairs={{0,24},{4,28},{8,16},{12,20},{16,8},{20,12},{24,0},{28,4},{1,25},{... | collective-permute-start | bytes 786440 | tf_op jit(solution)/shard_map/ppermute | solution.py:387
  252.5 18.1 %collective-permute-start.39 = (bf16[400,512]{1,0:T(8,128)(2,1)S(1)}, bf16[400,512]{1,0:T(8,128)(2,1)S(1)}, u32[]{:S(2)}, u32[]{:S(2)}) collective-permute-start(bf16[400,512]{1,0:T(8,128)(2,1)S(1)} %add_convert_fusion.8), channel_id=1, source_target_pairs={{0,8},{4,12},{8,0},{12,4},{16,24},{20,28},{24,16},{28,20},{1,9},{5... | collective-permute-start | bytes 1228808 | tf_op jit(solution)/shard_map/ppermute | solution.py:387
  256.2 56.5 %collective-permute-start.48 = (bf16[4,4,128,512]{3,2,1,0:T(8,128)(2,1)}, bf16[4,4,128,512]{3,2,1,0:T(8,128)(2,1)}, u32[]{:S(2)}, u32[]{:S(2)}) collective-permute-start(bf16[4,4,128,512]{3,2,1,0:T(8,128)(2,1)} %get-tuple-element.162), channel_id=1, source_target_pairs={{0,4},{4,0},{8,12},{12,8},{16,20},{20,16},{24,28},{28,24},{1,5},{5... | collective-permute-start | bytes 6291464 | tf_op jit(solution)/shard_map/ppermute | solution.py:387
  260.3 12.6 %collective-permute-start.75 = (bf16[128,512]{1,0:T(8,128)(2,1)S(1)}, bf16[128,512]{1,0:T(8,128)(2,1)S(1)}, u32[]{:S(2)}, u32[]{:S(2)}) collective-permute-start(bf16[128,512]{1,0:T(8,128)(2,1)S(1)} %add_convert_fusion.12), channel_id=1, source_target_pairs={{0,2},{1,3},{2,0},{3,1},{4,6},{5,7},{6,4},{7,5},{8,10},{9,11},{10,... | collective-permute-start | bytes 393224 | tf_op jit(solution)/shard_map/ppermute | solution.py:387
  270.7 10.2 %collective-permute-start.40 = (bf16[400,512]{1,0:T(8,128)(2,1)S(1)}, bf16[400,512]{1,0:T(8,128)(2,1)S(1)}, u32[]{:S(2)}, u32[]{:S(2)}) collective-permute-start(bf16[400,512]{1,0:T(8,128)(2,1)S(1)} %add_convert_fusion.7), channel_id=1, source_target_pairs={{0,16},{4,20},{8,24},{12,28},{16,0},{20,4},{24,8},{28,12},{1,17},{... | collective-permute-start | bytes 1228808 | tf_op jit(solution)/shard_map/ppermute | solution.py:387
  273.0 12.1 %collective-permute-start.76 = (bf16[128,512]{1,0:T(8,128)(2,1)S(1)}, bf16[128,512]{1,0:T(8,128)(2,1)S(1)}, u32[]{:S(2)}, u32[]{:S(2)}) collective-permute-start(bf16[128,512]{1,0:T(8,128)(2,1)S(1)} %add_convert_fusion.11), channel_id=1, source_target_pairs={{0,8},{4,12},{8,0},{12,4},{16,24},{20,28},{24,16},{28,20},{1,9},{5... | collective-permute-start | bytes 393224 | tf_op jit(solution)/shard_map/ppermute | solution.py:387
  273.2 14.1 %collective-permute-start.85 = (bf16[256,512]{1,0:T(8,128)(2,1)S(1)}, bf16[256,512]{1,0:T(8,128)(2,1)}, u32[]{:S(2)}, u32[]{:S(2)}) collective-permute-start(bf16[256,512]{1,0:T(8,128)(2,1)S(1)} %add_convert_fusion.10), channel_id=1, source_target_pairs={{0,2},{1,3},{2,0},{3,1},{4,6},{5,7},{6,4},{7,5},{8,10},{9,11},{10,... | collective-permute-start | bytes 786440 | tf_op jit(solution)/shard_map/ppermute | solution.py:387
  281.0 15.0 %collective-permute-start.41 = (bf16[400,512]{1,0:T(8,128)(2,1)S(1)}, bf16[400,512]{1,0:T(8,128)(2,1)S(1)}, u32[]{:S(2)}, u32[]{:S(2)}) collective-permute-start(bf16[400,512]{1,0:T(8,128)(2,1)S(1)} %add_convert_fusion.6), channel_id=1, source_target_pairs={{0,1},{1,0},{2,3},{3,2},{4,5},{5,4},{6,7},{7,6},{8,9},{9,8},{10,11... | collective-permute-start | bytes 1228808 | tf_op jit(solution)/shard_map/ppermute | solution.py:387
  296.1 9.3 %collective-permute-start.88 = (bf16[256,512]{1,0:T(8,128)(2,1)S(1)}, bf16[256,512]{1,0:T(8,128)(2,1)S(1)}, u32[]{:S(2)}, u32[]{:S(2)}) collective-permute-start(bf16[256,512]{1,0:T(8,128)(2,1)S(1)} %add_convert_fusion.9), channel_id=1, source_target_pairs={{0,24},{4,28},{8,16},{12,20},{16,8},{20,12},{24,0},{28,4},{1,25},{... | collective-permute-start | bytes 786440 | tf_op jit(solution)/shard_map/ppermute | solution.py:387
  298.9 75.6 %collective-permute-start.42 = (bf16[400,512]{1,0:T(8,128)(2,1)S(1)}, bf16[400,512]{1,0:T(8,128)(2,1)S(1)}, u32[]{:S(2)}, u32[]{:S(2)}) collective-permute-start(bf16[400,512]{1,0:T(8,128)(2,1)S(1)} %add_convert_fusion.5), channel_id=1, source_target_pairs={{0,2},{1,3},{2,0},{3,1},{4,6},{5,7},{6,4},{7,5},{8,10},{9,11},{10,... | collective-permute-start | bytes 1228808 | tf_op jit(solution)/shard_map/ppermute | solution.py:387
  305.5 91.2 %collective-permute-start.89 = (bf16[4,256,512]{2,1,0:T(8,128)(2,1)S(1)}, bf16[4,256,512]{2,1,0:T(8,128)(2,1)}, u32[]{:S(2)}, u32[]{:S(2)}) collective-permute-start(bf16[4,256,512]{2,1,0:T(8,128)(2,1)S(1)} %pad_maximum_fusion.1), channel_id=1, source_target_pairs={{0,4},{4,0},{8,12},{12,8},{16,20},{20,16},{24,28},{28,24},{1,5},{5... | collective-permute-start | bytes 3145736 | tf_op jit(solution)/shard_map/ppermute | solution.py:387
  310.3 12.9 %collective-permute-start.60 = (bf16[4,128,512]{2,1,0:T(8,128)(2,1)S(1)}, bf16[4,128,512]{2,1,0:T(8,128)(2,1)S(1)}, u32[]{:S(2)}, u32[]{:S(2)}) collective-permute-start(bf16[4,128,512]{2,1,0:T(8,128)(2,1)S(1)} %get-tuple-element.181), channel_id=1, source_target_pairs={{0,8},{4,12},{8,0},{12,4},{16,24},{20,28},{24,16},{28,20},{1,9},{5... | collective-permute-start | bytes 1572872 | tf_op jit(solution)/shard_map/ppermute | solution.py:387
  311.8 12.8 %collective-permute-start.61 = (bf16[4,128,512]{2,1,0:T(8,128)(2,1)S(1)}, bf16[4,128,512]{2,1,0:T(8,128)(2,1)S(1)}, u32[]{:S(2)}, u32[]{:S(2)}) collective-permute-start(bf16[4,128,512]{2,1,0:T(8,128)(2,1)S(1)} %get-tuple-element.183), channel_id=1, source_target_pairs={{0,16},{4,20},{8,24},{12,28},{16,0},{20,4},{24,8},{28,12},{1,17},{... | collective-permute-start | bytes 1572872 | tf_op jit(solution)/shard_map/ppermute | solution.py:387
  312.7 22.7 %collective-permute-start.62 = (bf16[4,128,512]{2,1,0:T(8,128)(2,1)S(1)}, bf16[4,128,512]{2,1,0:T(8,128)(2,1)S(1)}, u32[]{:S(2)}, u32[]{:S(2)}) collective-permute-start(bf16[4,128,512]{2,1,0:T(8,128)(2,1)S(1)} %get-tuple-element.182), channel_id=1, source_target_pairs={{0,24},{4,28},{8,16},{12,20},{16,8},{20,12},{24,0},{28,4},{1,25},{... | collective-permute-start | bytes 1572872 | tf_op jit(solution)/shard_map/ppermute | solution.py:387
  323.2 22.5 %collective-permute-start.49 = (bf16[4,128,512]{2,1,0:T(8,128)(2,1)S(1)}, bf16[4,128,512]{2,1,0:T(8,128)(2,1)S(1)}, u32[]{:S(2)}, u32[]{:S(2)}) collective-permute-start(bf16[4,128,512]{2,1,0:T(8,128)(2,1)S(1)} %get-tuple-element.184), channel_id=1, source_target_pairs={{0,8},{4,12},{8,0},{12,4},{16,24},{20,28},{24,16},{28,20},{1,9},{5... | collective-permute-start | bytes 1572872 | tf_op jit(solution)/shard_map/ppermute | solution.py:387
  324.6 21.6 %collective-permute-start.50 = (bf16[4,128,512]{2,1,0:T(8,128)(2,1)S(1)}, bf16[4,128,512]{2,1,0:T(8,128)(2,1)S(1)}, u32[]{:S(2)}, u32[]{:S(2)}) collective-permute-start(bf16[4,128,512]{2,1,0:T(8,128)(2,1)S(1)} %get-tuple-element.186), channel_id=1, source_target_pairs={{0,16},{4,20},{8,24},{12,28},{16,0},{20,4},{24,8},{28,12},{1,17},{... | collective-permute-start | bytes 1572872 | tf_op jit(solution)/shard_map/ppermute | solution.py:387
  335.3 22.5 %collective-permute-start.51 = (bf16[4,128,512]{2,1,0:T(8,128)(2,1)S(1)}, bf16[4,128,512]{2,1,0:T(8,128)(2,1)S(1)}, u32[]{:S(2)}, u32[]{:S(2)}) collective-permute-start(bf16[4,128,512]{2,1,0:T(8,128)(2,1)S(1)} %get-tuple-element.185), channel_id=1, source_target_pairs={{0,24},{4,28},{8,16},{12,20},{16,8},{20,12},{24,0},{28,4},{1,25},{... | collective-permute-start | bytes 1572872 | tf_op jit(solution)/shard_map/ppermute | solution.py:387
  345.7 14.8 %collective-permute-start.63 = (bf16[128,512]{1,0:T(8,128)(2,1)S(1)}, bf16[128,512]{1,0:T(8,128)(2,1)S(1)}, u32[]{:S(2)}, u32[]{:S(2)}) collective-permute-start(bf16[128,512]{1,0:T(8,128)(2,1)S(1)} %get-tuple-element.211), channel_id=1, source_target_pairs={{0,1},{1,0},{2,3},{3,2},{4,5},{5,4},{6,7},{7,6},{8,9},{9,8},{10,11... | collective-permute-start | bytes 393224 | tf_op jit(solution)/shard_map/ppermute | solution.py:387
  346.2 14.4 %collective-permute-start.64 = (bf16[128,512]{1,0:T(8,128)(2,1)S(1)}, bf16[128,512]{1,0:T(8,128)(2,1)S(1)}, u32[]{:S(2)}, u32[]{:S(2)}) collective-permute-start(bf16[128,512]{1,0:T(8,128)(2,1)S(1)} %get-tuple-element.213), channel_id=1, source_target_pairs={{0,2},{1,3},{2,0},{3,1},{4,6},{5,7},{6,4},{7,5},{8,10},{9,11},{10,... | collective-permute-start | bytes 393224 | tf_op jit(solution)/shard_map/ppermute | solution.py:387
  360.6 11.8 %collective-permute-start.53 = (bf16[128,512]{1,0:T(8,128)(2,1)S(1)}, bf16[128,512]{1,0:T(8,128)(2,1)S(1)}, u32[]{:S(2)}, u32[]{:S(2)}) collective-permute-start(bf16[128,512]{1,0:T(8,128)(2,1)S(1)} %get-tuple-element.216), channel_id=1, source_target_pairs={{0,2},{1,3},{2,0},{3,1},{4,6},{5,7},{6,4},{7,5},{8,10},{9,11},{10,... | collective-permute-start | bytes 393224 | tf_op jit(solution)/shard_map/ppermute | solution.py:387
  363.5 10.2 %collective-permute-start.54 = (bf16[128,512]{1,0:T(8,128)(2,1)S(1)}, bf16[128,512]{1,0:T(8,128)(2,1)S(1)}, u32[]{:S(2)}, u32[]{:S(2)}) collective-permute-start(bf16[128,512]{1,0:T(8,128)(2,1)S(1)} %get-tuple-element.215), channel_id=1, source_target_pairs={{0,3},{1,2},{2,1},{3,0},{4,7},{5,6},{6,5},{7,4},{8,11},{9,10},{10,... | collective-permute-start | bytes 393224 | tf_op jit(solution)/shard_map/ppermute | solution.py:387
  374.5 14.1 %collective-permute-start.55 = (bf16[128,512]{1,0:T(8,128)(2,1)S(1)}, bf16[128,512]{1,0:T(8,128)(2,1)S(1)}, u32[]{:S(2)}, u32[]{:S(2)}) collective-permute-start(bf16[128,512]{1,0:T(8,128)(2,1)S(1)} %fusion.15), channel_id=1, source_target_pairs={{0,8},{4,12},{8,0},{12,4},{16,24},{20,28},{24,16},{28,20},{1,9},{5... | collective-permute-start | bytes 393224 | tf_op jit(solution)/shard_map/ppermute | solution.py:387
  375.2 13.8 %collective-permute-start.56 = (bf16[128,512]{1,0:T(8,128)(2,1)S(1)}, bf16[128,512]{1,0:T(8,128)(2,1)S(1)}, u32[]{:S(2)}, u32[]{:S(2)}) collective-permute-start(bf16[128,512]{1,0:T(8,128)(2,1)S(1)} %fusion.15), channel_id=1, source_target_pairs={{0,16},{4,20},{8,24},{12,28},{16,0},{20,4},{24,8},{28,12},{1,17},{... | collective-permute-start | bytes 393224 | tf_op jit(solution)/shard_map/ppermute | solution.py:387
  376.5 12.5 %collective-permute-start.57 = (bf16[128,512]{1,0:T(8,128)(2,1)S(1)}, bf16[128,512]{1,0:T(8,128)(2,1)S(1)}, u32[]{:S(2)}, u32[]{:S(2)}) collective-permute-start(bf16[128,512]{1,0:T(8,128)(2,1)S(1)} %fusion.15), channel_id=1, source_target_pairs={{0,24},{4,28},{8,16},{12,20},{16,8},{20,12},{24,0},{28,4},{1,25},{... | collective-permute-start | bytes 393224 | tf_op jit(solution)/shard_map/ppermute | solution.py:387
  378.7 20.4 %collective-permute-start.79 = (bf16[4,128,512]{2,1,0:T(8,128)(2,1)}, bf16[4,128,512]{2,1,0:T(8,128)(2,1)}, u32[]{:S(2)}, u32[]{:S(2)}) collective-permute-start(bf16[4,128,512]{2,1,0:T(8,128)(2,1)} %pad_maximum_fusion.4.refs_4_), channel_id=1, source_target_pairs={{0,4},{4,0},{8,12},{12,8},{16,20},{20,16},{24,28},{28,24},{1,5},{5... | collective-permute-start | bytes 1572872 | tf_op jit(solution)/shard_map/ppermute | solution.py:387
  388.6 10.5 %collective-permute-start.69 = (bf16[4,128,512]{2,1,0:T(8,128)(2,1)}, bf16[4,128,512]{2,1,0:T(8,128)(2,1)}, u32[]{:S(2)}, u32[]{:S(2)}) collective-permute-start(bf16[4,128,512]{2,1,0:T(8,128)(2,1)} %pad_maximum_fusion.3.refs_2_), channel_id=1, source_target_pairs={{0,4},{4,0},{8,12},{12,8},{16,20},{20,16},{24,28},{28,24},{1,5},{5... | collective-permute-start | bytes 1572872 | tf_op jit(solution)/shard_map/ppermute | solution.py:387
  (93 other events, 756.1 us)
